TPU v7x, 32 devices: a whole 2x2x4 slice. The times are simulated.
32 devices in a mesh: expert: 4 (over y, x), shard: 8 (over z, core).
Axes of the slice: x: 2, y: 2, z: 4, core: 2. Of those that a mesh axis runs over, the one named last changes fastest.
Arguments:
- tokens: bfloat16 [12288, 1536], P(('expert', 'shard')), may hold values from -6 to 6
- cotangent: bfloat16 [12288, 1536], P(('expert', 'shard')), may hold values from -6 to 6
- lengths: int32 [32], P(('expert', 'shard')), may hold values from 96 to 384, as said below
- routes: int32 [12288, 8], P(('expert', 'shard')), may hold values from 0 to 15, all different within a row; in each aligned block of 384 rows (0 to 383, 384 to 767, ...) at most 288 rows name the same one
- route_gates: bfloat16 [12288, 8], P(('expert', 'shard')), may hold values from 0.25 to 0.75
- norm_gains: float32 [2, 1536], replicated, may hold values from 0.5 to 1.5
- attn_master: float32 [384, 128, 128], P(('expert', 'shard')), may hold values from -4 to 4
- attn_stats: float32 [384, 2, 128, 128], P(('expert', 'shard')), may hold values from -512 to 512
- attn_roots: float32 [384, 2, 128, 128], P(('expert', 'shard')), may hold values from -2 to 2
- attn_deal: int32 [384], replicated, may hold values from 0 to 383, as said below
- expert_master: float32 [2304, 128, 128], P(('expert', 'shard')), may hold values from -4 to 4
- expert_stats: float32 [2304, 2, 128, 128], P(('expert', 'shard')), may hold values from -512 to 512
- expert_roots: float32 [2304, 2, 128, 128], P(('expert', 'shard')), may hold values from -2 to 2
- expert_deal: int32 [4, 576], P('expert'), may hold values from 0 to 575, as said below
Outputs:
- output: bfloat16 [12288, 1536], P(('expert', 'shard'))
- input_grad: float32 [12288, 1536], P(('expert', 'shard'))
- gain_grads: float32 [2, 1536], replicated
- new_gains: float32 [2, 1536], replicated
- attn_grads: float32 [384, 128, 128], P(('expert', 'shard'))
- attn_stats_new: float32 [384, 2, 128, 128], P(('expert', 'shard'))
- attn_new: float32 [384, 128, 128], P(('expert', 'shard'))
- expert_grads: float32 [2304, 128, 128], P(('expert', 'shard'))
- expert_stats_new: float32 [2304, 2, 128, 128], P(('expert', 'shard'))
- expert_new: float32 [2304, 128, 128], P(('expert', 'shard'))
Inputs may be any that keep to these rules, and one draw needn't show every extreme that they name: `routes`: in each aligned block of 384 rows (one sequence) no expert is named by more than 288 rows, a bound that some block reaches. `lengths`: some sequence uses all 384 slots. `attn_deal`: A permutation of the attention blocks. `expert_deal`: each row is a permutation of its group's blocks.
All inputs are finite; a program needn't handle non-finite values.
Results may differ from a plain program's by a relative error of at most 0.015.
Values may be sent and summed in bfloat16 or wider, within the bound.
No kernel may reach another device: no remote copies, remote signals or barrier semaphores. Data moves between devices by JAX's collectives and lax.ppermute only.
A program may use at most 384 MiB of HBM per device.

v0:
```python
import jax
import jax.numpy as jnp
from jax import lax
from jax.sharding import PartitionSpec as P

D = 1536
H = 24
KV = 8
HD = 64
FF = 512
TOP = 8
BLOCK = 128
EXP_DEV = 4
CAP = 288


EPSILON = 1e-05
STEP_SIZE = 0.3
HIGHEST_PRECISION = lax.Precision.HIGHEST


def natural_order(slotted, dealing):
    slot_count = dealing.shape[0]
    inverse = (
        jnp.zeros((slot_count,), jnp.int32).at[dealing].set(jnp.arange(slot_count, dtype=jnp.int32))
    )
    return slotted[inverse]


def assemble(blocks, row_blocks, col_blocks):
    extent = blocks.shape[-1]
    return (
        blocks.reshape(row_blocks, col_blocks, extent, extent)
        .transpose(0, 2, 1, 3)
        .reshape(row_blocks * extent, col_blocks * extent)
    )


def to_blocks(matrix):
    row_blocks = matrix.shape[0] // BLOCK
    col_blocks = matrix.shape[1] // BLOCK
    return (
        matrix.reshape(row_blocks, BLOCK, col_blocks, BLOCK)
        .transpose(0, 2, 1, 3)
        .reshape(row_blocks * col_blocks, BLOCK, BLOCK)
    )


def rope_tables(positions):
    frequency = 10000.0 ** (-2.0 * jnp.arange(HD // 2, dtype=jnp.float32) / HD)
    angles = positions[:, None] * frequency[None, :]
    return (jnp.cos(angles), jnp.sin(angles))


def rotate(values, cosine_table, sine_table):
    halfway = HD // 2
    first_half = values[..., :halfway]
    second_half = values[..., halfway:]
    cosine_wide = cosine_table[:, None, :]
    sine_wide = sine_table[:, None, :]
    return jnp.concatenate(
        [
            first_half * cosine_wide - second_half * sine_wide,
            second_half * cosine_wide + first_half * sine_wide,
        ],
        axis=-1,
    )


def unrotate(values, cosine_table, sine_table):
    halfway = HD // 2
    first_half = values[..., :halfway]
    second_half = values[..., halfway:]
    cosine_wide = cosine_table[:, None, :]
    sine_wide = sine_table[:, None, :]
    return jnp.concatenate(
        [
            first_half * cosine_wide + second_half * sine_wide,
            second_half * cosine_wide - first_half * sine_wide,
        ],
        axis=-1,
    )


def attention_scores(queries_turned, keys_turned, allowed):
    row_count = queries_turned.shape[0]
    grouped = queries_turned.reshape(row_count, KV, H // KV, HD)
    raw_scores = jnp.einsum(
        "tkgd,skd->kgts", grouped, keys_turned, preferred_element_type=jnp.float32
    ) * HD ** (-0.5)
    return jnp.where(allowed, raw_scores, -1e30)


def slot_places(route_ids, experts_all, per_source):
    onehot = (
        route_ids.reshape(-1, per_source)[:, :, None] == jnp.arange(experts_all)[None, None, :]
    ).astype(jnp.int32)
    ranking = jnp.sum(jnp.cumsum(onehot, axis=1) * onehot, axis=-1) - 1
    return ranking.reshape(-1)


def slot_matrices(slot_ids, gates, slot_count):
    slot_numbers = jnp.arange(slot_count, dtype=jnp.int32)[:, None]
    dispatch = jnp.zeros((slot_count, slot_ids.shape[0]), jnp.bfloat16)
    weighted = jnp.zeros((slot_count, slot_ids.shape[0]), jnp.bfloat16)
    for route_number in range(TOP):
        hits = slot_ids[None, :, route_number] == slot_numbers
        dispatch = dispatch + hits.astype(jnp.bfloat16)
        weighted = weighted + jnp.where(
            hits, gates[None, :, route_number], jnp.zeros((), jnp.bfloat16)
        )
    return (dispatch, weighted)


def expert_forward(rows_in, w_gateup, w_down):
    gate_up = jnp.einsum("ecd,edf->ecf", rows_in, w_gateup, preferred_element_type=jnp.float32)
    gate_part = gate_up[..., :FF]
    up_part = gate_up[..., FF:]
    hidden = (jax.nn.silu(gate_part) * up_part).astype(jnp.bfloat16)
    produced = jnp.einsum(
        "ecf,efd->ecd", hidden, w_down, preferred_element_type=jnp.float32
    ).astype(jnp.bfloat16)
    return (gate_part, up_part, hidden, produced)


def expert_backward(rows_in, grad_rows, gate_part, up_part, hidden, w_gateup, w_down):
    grad_down = jnp.einsum("ecf,ecd->efd", hidden, grad_rows, preferred_element_type=jnp.float32)
    grad_hidden = jnp.einsum("ecd,efd->ecf", grad_rows, w_down, preferred_element_type=jnp.float32)
    sigmoid = jax.nn.sigmoid(gate_part)
    grad_gate = grad_hidden * up_part * sigmoid * (1.0 + gate_part * (1.0 - sigmoid))
    grad_up = grad_hidden * gate_part * sigmoid
    grad_both = jnp.concatenate([grad_gate, grad_up], axis=-1).astype(jnp.bfloat16)
    grad_gateup = jnp.einsum("ecd,ecf->edf", rows_in, grad_both, preferred_element_type=jnp.float32)
    grad_route = jnp.einsum(
        "ecf,edf->ecd", grad_both, w_gateup, preferred_element_type=jnp.float32
    ).astype(jnp.bfloat16)
    return (grad_gateup, grad_down, grad_route)


def shampoo(gradient, statistics, inverse_roots, master):
    unit_grad = gradient * lax.rsqrt(
        jnp.mean(gradient * gradient, axis=(1, 2), keepdims=True) + 1e-06
    )
    left_new = 0.5 * statistics[:, 0] + 0.5 * jnp.einsum(
        "nij,nkj->nik", unit_grad, unit_grad, precision=HIGHEST_PRECISION
    )
    right_new = 0.5 * statistics[:, 1] + 0.5 * jnp.einsum(
        "nji,njk->nik", unit_grad, unit_grad, precision=HIGHEST_PRECISION
    )
    turned = jnp.einsum("nij,njk->nik", inverse_roots[:, 0], gradient, precision=HIGHEST_PRECISION)
    turned = jnp.einsum("nij,njk->nik", turned, inverse_roots[:, 1], precision=HIGHEST_PRECISION)
    direction = turned * lax.rsqrt(jnp.mean(turned * turned, axis=(1, 2), keepdims=True) + 1e-06)
    spread = jnp.sqrt(jnp.mean(master * master, axis=(1, 2), keepdims=True))
    return (jnp.stack([left_new, right_new], axis=1), master - STEP_SIZE * spread * direction)


def per_device(
    tokens,
    cotangent,
    lengths,
    routes,
    route_gates,
    norm_gains,
    attn_master,
    attn_stats,
    attn_roots,
    attn_deal,
    expert_master,
    expert_stats,
    expert_roots,
    expert_deal,
):
    row_count = tokens.shape[0]
    groups = lax.axis_size("expert")
    experts_all = groups * EXP_DEV
    across = D // BLOCK
    kv_across = 2 * KV * HD // BLOCK
    hidden_across = FF // BLOCK
    query_end = across * across
    keyval_end = query_end + across * kv_across
    split_at = 2 * across * hidden_across
    attn_all = lax.all_gather(
        attn_master.astype(jnp.bfloat16), ("expert", "shard"), axis=0, tiled=True
    )
    attn_blocks = natural_order(attn_all, attn_deal)
    w_query = assemble(attn_blocks[:query_end], across, across)
    w_keyval = assemble(attn_blocks[query_end:keyval_end], across, kv_across)
    w_out = assemble(attn_blocks[keyval_end:], across, across)
    expert_all = lax.all_gather(expert_master.astype(jnp.bfloat16), "shard", axis=0, tiled=True)
    expert_blocks = natural_order(expert_all, expert_deal[0]).reshape(EXP_DEV, -1, BLOCK, BLOCK)
    w_gateup = jax.vmap(lambda blocks: assemble(blocks, across, 2 * hidden_across))(
        expert_blocks[:, :split_at]
    )
    w_down = jax.vmap(lambda blocks: assemble(blocks, hidden_across, across))(
        expert_blocks[:, split_at:]
    )
    residual = tokens.astype(jnp.float32)
    scale_one = lax.rsqrt(jnp.mean(residual * residual, axis=-1, keepdims=True) + EPSILON)
    unit_one = residual * scale_one
    normed_one = (unit_one * norm_gains[0]).astype(jnp.bfloat16)
    queries = jnp.dot(normed_one, w_query, preferred_element_type=jnp.float32)
    keyval = jnp.dot(normed_one, w_keyval, preferred_element_type=jnp.float32)
    cosine_table, sine_table = rope_tables(jnp.arange(row_count, dtype=jnp.float32))
    queries_turned = rotate(queries.reshape(row_count, H, HD), cosine_table, sine_table).astype(
        jnp.bfloat16
    )
    keys_turned = rotate(
        keyval[:, : KV * HD].reshape(row_count, KV, HD), cosine_table, sine_table
    ).astype(jnp.bfloat16)
    values_low = keyval[:, KV * HD :].reshape(row_count, KV, HD).astype(jnp.bfloat16)
    places = jnp.arange(row_count)
    allowed = (places[None, :] <= places[:, None]) & (places[None, :] < lengths[0])
    scores = attention_scores(queries_turned, keys_turned, allowed)
    row_peak = jnp.max(scores, axis=-1, keepdims=True)
    weights = jnp.exp(scores - row_peak)
    row_total = jnp.sum(weights, axis=-1, keepdims=True)
    log_total = row_peak + jnp.log(row_total)
    probs_low = (weights / row_total).astype(jnp.bfloat16)
    mixed_heads = jnp.einsum(
        "kgts,skd->tkgd", probs_low, values_low, preferred_element_type=jnp.float32
    )
    mixed_low = mixed_heads.reshape(row_count, H * HD).astype(jnp.bfloat16)
    middle = residual + jnp.dot(mixed_low, w_out, preferred_element_type=jnp.float32)
    scale_two = lax.rsqrt(jnp.mean(middle * middle, axis=-1, keepdims=True) + EPSILON)
    unit_two = middle * scale_two
    normed_two = (unit_two * norm_gains[1]).astype(jnp.bfloat16)
    places_own = slot_places(routes.reshape(-1), experts_all, row_count * TOP).reshape(
        row_count, TOP
    )
    slot_ids = routes * CAP + places_own
    dispatch, weighted = slot_matrices(slot_ids, route_gates, experts_all * CAP)
    gate_slot = jnp.sum(weighted.astype(jnp.float32), axis=1)
    outgoing = (
        jnp.dot(dispatch, normed_two, preferred_element_type=jnp.float32)
        .astype(jnp.bfloat16)
        .reshape(groups, EXP_DEV, CAP, D)
    )
    rows_in = lax.all_to_all(outgoing, "expert", split_axis=0, concat_axis=2, tiled=True)[0]
    gate_part, up_part, hidden, produced = expert_forward(rows_in, w_gateup, w_down)
    returned = lax.all_to_all(produced[None], "expert", split_axis=2, concat_axis=0, tiled=True)
    moe_sum = jnp.einsum(
        "st,sd->td", weighted, returned.reshape(-1, D), preferred_element_type=jnp.float32
    )
    output = (middle + moe_sum).astype(jnp.bfloat16)
    valid_rows = places < lengths[0]
    grad_low = jnp.where(valid_rows[:, None], cotangent, jnp.zeros_like(cotangent))
    grad_out = grad_low.astype(jnp.float32)
    grad_send = (
        (jnp.dot(dispatch, grad_low, preferred_element_type=jnp.float32) * gate_slot[:, None])
        .astype(jnp.bfloat16)
        .reshape(groups, EXP_DEV, CAP, D)
    )
    grad_rows = lax.all_to_all(grad_send, "expert", split_axis=0, concat_axis=2, tiled=True)[0]
    grad_gateup, grad_down, grad_route = expert_backward(
        rows_in, grad_rows, gate_part, up_part, hidden, w_gateup, w_down
    )
    back_rows = lax.all_to_all(grad_route[None], "expert", split_axis=2, concat_axis=0, tiled=True)
    grad_normed_two = jnp.einsum(
        "st,sd->td", dispatch, back_rows.reshape(-1, D), preferred_element_type=jnp.float32
    )
    scaled_two = grad_normed_two * norm_gains[1]
    gain_two_part = jnp.sum(grad_normed_two * unit_two, axis=0)
    grad_middle = grad_out + scale_two * (
        scaled_two - unit_two * jnp.mean(scaled_two * unit_two, axis=-1, keepdims=True)
    )
    grad_attn = grad_middle.astype(jnp.bfloat16)
    grad_wout = jnp.einsum("tc,td->cd", mixed_low, grad_attn, preferred_element_type=jnp.float32)
    grad_mixed = (
        jnp.einsum("td,cd->tc", grad_attn, w_out, preferred_element_type=jnp.float32)
        .astype(jnp.bfloat16)
        .reshape(row_count, KV, H // KV, HD)
    )
    probs_again = jnp.exp(attention_scores(queries_turned, keys_turned, allowed) - log_total)
    probs_again_low = probs_again.astype(jnp.bfloat16)
    grad_value = jnp.einsum(
        "kgts,tkgd->skd", probs_again_low, grad_mixed, preferred_element_type=jnp.float32
    )
    grad_probs = jnp.einsum(
        "tkgd,skd->kgts", grad_mixed, values_low, preferred_element_type=jnp.float32
    )
    row_inner = jnp.sum(probs_again * grad_probs, axis=-1, keepdims=True)
    grad_scores = (probs_again * (grad_probs - row_inner)).astype(jnp.bfloat16)
    grouped = queries_turned.reshape(row_count, KV, H // KV, HD)
    grad_queries_turned = jnp.einsum(
        "kgts,skd->tkgd", grad_scores, keys_turned, preferred_element_type=jnp.float32
    ).reshape(row_count, H, HD) * HD ** (-0.5)
    grad_keys_turned = jnp.einsum(
        "kgts,tkgd->skd", grad_scores, grouped, preferred_element_type=jnp.float32
    ) * HD ** (-0.5)
    grad_queries = (
        unrotate(grad_queries_turned, cosine_table, sine_table)
        .reshape(row_count, H * HD)
        .astype(jnp.bfloat16)
    )
    grad_keys = unrotate(grad_keys_turned, cosine_table, sine_table).reshape(row_count, KV * HD)
    grad_keyval = jnp.concatenate(
        [grad_keys, grad_value.reshape(row_count, KV * HD)], axis=-1
    ).astype(jnp.bfloat16)
    grad_wquery = jnp.einsum(
        "tc,td->cd", normed_one, grad_queries, preferred_element_type=jnp.float32
    )
    grad_wkeyval = jnp.einsum(
        "tc,td->cd", normed_one, grad_keyval, preferred_element_type=jnp.float32
    )
    grad_normed_one = jnp.einsum(
        "td,cd->tc", grad_queries, w_query, preferred_element_type=jnp.float32
    ) + jnp.einsum("td,cd->tc", grad_keyval, w_keyval, preferred_element_type=jnp.float32)
    scaled_one = grad_normed_one * norm_gains[0]
    gain_one_part = jnp.sum(grad_normed_one * unit_one, axis=0)
    input_grad = grad_middle + scale_one * (
        scaled_one - unit_one * jnp.mean(scaled_one * unit_one, axis=-1, keepdims=True)
    )
    attn_term = jnp.concatenate(
        [to_blocks(grad_wquery), to_blocks(grad_wkeyval), to_blocks(grad_wout)], axis=0
    )
    attn_grads = lax.psum_scatter(
        attn_term[attn_deal], ("expert", "shard"), scatter_dimension=0, tiled=True
    )
    expert_term = jnp.concatenate(
        [jax.vmap(to_blocks)(grad_gateup), jax.vmap(to_blocks)(grad_down)], axis=1
    ).reshape(-1, BLOCK, BLOCK)
    expert_grads = lax.psum_scatter(
        expert_term[expert_deal[0]].astype(jnp.bfloat16), "shard", scatter_dimension=0, tiled=True
    ).astype(jnp.float32)
    gain_grads = lax.psum(jnp.stack([gain_one_part, gain_two_part]), ("expert", "shard"))
    new_gains = norm_gains - STEP_SIZE * gain_grads * lax.rsqrt(
        jnp.mean(gain_grads * gain_grads, axis=-1, keepdims=True) + 1e-06
    )
    attn_stats_new, attn_new = shampoo(attn_grads, attn_stats, attn_roots, attn_master)
    expert_stats_new, expert_new = shampoo(expert_grads, expert_stats, expert_roots, expert_master)
    return (
        output,
        input_grad,
        gain_grads,
        new_gains,
        attn_grads,
        attn_stats_new,
        attn_new,
        expert_grads,
        expert_stats_new,
        expert_new,
    )


def solution(mesh):
    in_specs = (
        P(("expert", "shard"), None),
        P(("expert", "shard"), None),
        P(("expert", "shard")),
        P(("expert", "shard"), None),
        P(("expert", "shard"), None),
        P(),
        P(("expert", "shard"), None, None),
        P(("expert", "shard"), None, None, None),
        P(("expert", "shard"), None, None, None),
        P(),
        P(("expert", "shard"), None, None),
        P(("expert", "shard"), None, None, None),
        P(("expert", "shard"), None, None, None),
        P("expert", None),
    )
    out_specs = (
        P(("expert", "shard"), None),
        P(("expert", "shard"), None),
        P(),
        P(),
        P(("expert", "shard"), None, None),
        P(("expert", "shard"), None, None, None),
        P(("expert", "shard"), None, None),
        P(("expert", "shard"), None, None),
        P(("expert", "shard"), None, None, None),
        P(("expert", "shard"), None, None),
    )
    return jax.shard_map(
        per_device, mesh=mesh, in_specs=in_specs, out_specs=out_specs, check_vma=False
    )
```

profile of v0, /device:TPU:8, one launch (start us, length us, event | category | flops | bytes accessed | tf_op | source)
XLA Modules:
  0.0 1382.5 jit_solution(7433234831080991460)
XLA Ops:
  10.2 6.7 multiply_reduce_fusion.1
  18.1 4.6 reduce-window.6
  24.1 6.0 convert_reduce_fusion
  30.1 15.1 %multiply_convert_fusion = bf16[4608,1536]{1,0:T(8,128)(2,1)} fusion(f32[4608]{0:T(1024)S(1)} %convert_reduce_fusion, bf16[384,1536]{1,0:T(8,128)(2,1)S(1)} %copy-done.34, pred[384]{0:T(512)(128)(4,1)S(1)} %iota_compare_fusion.10, s32[384]{0:T(512)S(1)} %get-tuple-element.85, s32[384]{0:T(512)S(1)} %get-tuple-element.86, s32[384]{0:T(512)S(1)} %get-tuple-element.87, ...), kind=kOutput, calls=%fused_computation.7 | convolution fusion | flops 5507186688 | bytes 15366528 | tf_op jit(solution)/shard_map/dot_general | solution.py:249
  45.4 6.7 all-to-all-start.2
  57.5 135.8 %all-gather.3.cloned.1.call-done = bf16[384,128,128]{2,1,0:T(8,128)(2,1)} async-done(((bf16[12,128,128]{2,1,0:T(8,128)(2,1)}), bf16[384,128,128]{2,1,0:T(8,128)(2,1)}) %all-gather.3.cloned.1.call-update) | async-done | bytes 12582928 | tf_op jit(solution)/shard_map/all_gather | solution.py:182
  193.2 15.9 %gather_fusion = bf16[384,128,128]{2,1,0:T(8,128)(2,1)} fusion(bf16[384,128,128]{2,1,0:T(8,128)(2,1)} %all-gather.3.cloned.1.call-done, s32[1024]{0:T(1024)S(1)} %pad_clamp_fusion.3), kind=kCustom, calls=%fused_computation | custom fusion | bytes 25167360 | tf_op jit(solution)/shard_map/gather | solution.py:27
  216.7 6.2 fusion.151
  226.6 6.8 copy.308
  233.5 4.6 copy.419
  238.1 6.8 copy.306
  245.0 4.9 fusion.110
  250.3 6.4 fusion.152
  256.8 7.5 fusion.5
  264.3 8.1 fusion.97
  276.3 15.2 %convolution_convert_fusion.2 = bf16[4608,1536]{1,0:T(8,128)(2,1)} fusion(f32[384,1536]{1,0:T(8,128)S(1)} %get-tuple-element.129, f32[1536]{0:T(1024)S(1)} %get-tuple-element.92, f32[384]{0:T(512)S(1)} %add_rsqrt_fusion, s32[384]{0:T(512)S(1)} %copy-done.73, s32[384]{0:T(512)S(1)} %copy-done.76, s32[384]{0:T(512)S(1)} %copy-done.79, s32[384]{0:T(512)S(1)} %copy-done.82, ...), kind=kOutput, calls=%fused_computation.13 | convolution fusion | flops 5501288448 | bytes 16535040 | tf_op jit(solution)/shard_map/dot_general | solution.py:234
  291.5 6.9 all-to-all-start
  298.5 4.1 scatter_custom_fusion.1
  303.2 10.8 copy.320
  314.0 45.0 %all-gather.5.cloned.1.call-done = bf16[576,128,128]{2,1,0:T(8,128)(2,1)} async-done(((bf16[72,128,128]{2,1,0:T(8,128)(2,1)}), bf16[576,128,128]{2,1,0:T(8,128)(2,1)}) %all-gather.5.cloned.1.call-update) | async-done | bytes 18874384 | tf_op jit(solution)/shard_map/all_gather | solution.py:189
  359.0 22.3 %gather_fusion.1 = bf16[576,128,128]{2,1,0:T(8,128)(2,1)} fusion(bf16[576,128,128]{2,1,0:T(8,128)(2,1)} %all-gather.5.cloned.1.call-done, s32[1024]{0:T(1024)S(1)} %pad_clamp_fusion.2), kind=kCustom, calls=%fused_computation.1 | custom fusion | bytes 37751040 | tf_op jit(solution)/shard_map/gather | solution.py:27
  381.3 8.0 slice.213
  389.3 6.2 slice.210
  395.5 11.8 copy.312
  407.3 19.3 %reshape.463 = bf16[4,1536,1024]{2,1,0:T(8,128)(2,1)} reshape(bf16[4,12,128,8,128]{4,3,2,1,0:T(8,128)(2,1)} %copy.312) | data formatting | bytes 25165824 | tf_op jit(solution)/shard_map/vmap()/reshape | solution.py:35
  426.6 10.6 copy.314
  437.2 10.1 reshape.465
  447.4 5.9 all-to-all-done
  453.2 10.5 copy.311
  463.7 25.3 %fusion.153 = f32[4,1152,1024]{1,2,0:T(8,128)} fusion(bf16[4,1152,1536]{2,1,0:T(8,128)(2,1)} %bitcast.319, bf16[4,1536,1024]{2,1,0:T(8,128)(2,1)} %reshape.463), kind=kOutput, calls=%fused_computation.259 | convolution fusion | flops 14495514624 | bytes 45613056 | tf_op jit(solution)/shard_map/ecd,edf->ecf/dot_general | solution.py:116
  489.0 24.7 %multiply_convert_fusion.2 = (bf16[4,1152,512]{1,2,0:T(8,128)(2,1)}, bf16[4,1152,512]{1,2,0:T(8,128)(2,1)}, bf16[4,1152,512]{1,2,0:T(8,128)(2,1)}) fusion(f32[4,1152,1024]{1,2,0:T(8,128)} %fusion.153, bf16[4,1152,1536]{2,1,0:T(8,128)(2,1)} %bitcast.317, bf16[4,512,1536]{1,2,0:T(8,128)(2,1)} %reshape.465), kind=kOutput, calls=%fused_computation.28 | convolution fusion | flops 7285506048 | bytes 53477376 | tf_op jit(solution)/shard_map/ecd,efd->ecf/dot_general | solution.py:128
  513.7 14.7 %fusion.156 = bf16[4,512,1536]{1,2,0:T(8,128)(2,1)} fusion(bf16[4,1152,512]{1,2,0:T(8,128)(2,1)} %get-tuple-element.108, bf16[4,1152,1536]{2,1,0:T(8,128)(2,1)} %bitcast.318), kind=kOutput, calls=%fused_computation.262 | convolution fusion | flops 7247757312 | bytes 25165824 | tf_op jit(solution)/shard_map/ecf,ecd->efd/dot_general | solution.py:127
  528.4 24.6 %fusion.27 = bf16[4,1536,1024]{2,1,0:T(8,128)(2,1)} fusion(bf16[4,1152,1536]{2,1,0:T(8,128)(2,1)} %bitcast.320, bf16[4,1152,512]{1,2,0:T(8,128)(2,1)} %get-tuple-element.107, bf16[4,1152,512]{1,2,0:T(8,128)(2,1)} %get-tuple-element.106), kind=kOutput, calls=%fused_computation.60 | convolution fusion | flops 14514388992 | bytes 36175872 | tf_op jit(solution)/shard_map/ecd,ecf->edf/dot_general | solution.py:133
  553.0 7.8 copy.391
  560.8 6.5 copy.342
  567.3 9.8 reshape.478
  577.1 10.5 copy.344
  587.6 19.3 %pad_maximum_fusion = bf16[4,144,128,128]{3,2,1,0:T(8,128)(2,1)} fusion(bf16[4,48,128,128]{3,2,1,0:T(8,128)(2,1)} %bitcast.302, bf16[4,96,128,128]{3,2,1,0:T(8,128)(2,1)} %bitcast.297), kind=kLoop, calls=%fused_computation.6 | loop fusion | flops 9437184 | bytes 37748736 | tf_op jit(solution)/shard_map/concatenate | solution.py:319
  606.9 22.4 %gather_fusion.3 = bf16[576,128,128]{2,1,0:T(8,128)(2,1)} fusion(bf16[576,128,128]{2,1,0:T(8,128)(2,1)} %bitcast.291, s32[1024]{0:T(1024)S(1)} %copy-done.59), kind=kCustom, calls=%fused_computation.3 | custom fusion | bytes 37751040 | tf_op jit(solution)/shard_map/gather | solution.py:323
  629.4 23.8 %fusion = bf16[1,4,1152,1536]{3,2,1,0:T(8,128)(2,1)} fusion(bf16[4,1536,1024]{2,1,0:T(8,128)(2,1)} %reshape.463, bf16[4,1152,512]{1,2,0:T(8,128)(2,1)} %get-tuple-element.107, bf16[4,1152,512]{1,2,0:T(8,128)(2,1)} %get-tuple-element.106), kind=kOutput, calls=%fused_computation.11 | convolution fusion | flops 14521466880 | bytes 36175872 | tf_op jit(solution)/shard_map/ecf,edf->ecd/dot_general | solution.py:134
  653.2 37.6 %copy.323 = bf16[1,4,1152,1536]{3,1,0,2:T(4,128)(2,1)} copy(bf16[1,4,1152,1536]{3,2,1,0:T(8,128)(2,1)} %fusion) | data formatting | bytes 28311552 | tf_op jit(solution)/shard_map/broadcast_in_dim | solution.py:257
  690.8 6.7 all-to-all-start.3
  698.3 153.2 %all-to-all-done.3 = bf16[1,4,1152,1536]{3,1,0,2:T(4,128)(2,1)} async-done(((bf16[1,4,1152,1536]{3,1,0,2:T(4,128)(2,1)}), bf16[1,4,1152,1536]{3,1,0,2:T(4,128)(2,1)}, u32[]{:S(2)}, u32[]{:S(2)}) %all-to-all-start.3) | async-done | bytes 14155808 | tf_op jit(solution)/shard_map/all_to_all | solution.py:257
  851.5 10.1 copy.324
  864.2 11.3 multiply_reduce_fusion.3
  879.9 5.9 fusion.78
  887.5 13.3 fusion.2
  901.0 6.8 fusion.4
  935.6 10.5 pad_maximum_fusion.1
  946.2 23.8 %gather_fusion.2 = f32[384,128,128]{2,1,0:T(8,128)} fusion(f32[384,128,128]{2,1,0:T(8,128)} %pad_maximum_fusion.1, s32[1024]{0:T(1024)S(1)} %pad_clamp_fusion.1), kind=kCustom, calls=%fused_computation.2 | custom fusion | bytes 50333184 | tf_op jit(solution)/shard_map/gather | solution.py:317
  969.9 15.0 %fusion.1 = bf16[1,4,1152,1536]{3,2,1,0:T(8,128)(2,1)} fusion(bf16[4,1152,512]{1,2,0:T(8,128)(2,1)} %get-tuple-element.108, bf16[4,512,1536]{1,2,0:T(8,128)(2,1)} %reshape.465), kind=kOutput, calls=%fused_computation.12 | convolution fusion | flops 7254835200 | bytes 25165824 | tf_op jit(solution)/shard_map/ecf,efd->ecd/dot_general | solution.py:120
  984.9 37.7 %copy.317 = bf16[1,4,1152,1536]{3,1,0,2:T(4,128)(2,1)} copy(bf16[1,4,1152,1536]{3,2,1,0:T(8,128)(2,1)} %fusion.1) | data formatting | bytes 28311552 | tf_op jit(solution)/shard_map/broadcast_in_dim | solution.py:240
  1022.6 6.6 all-to-all-start.1
  1030.9 196.9 %all-to-all-done.1 = bf16[1,4,1152,1536]{3,1,0,2:T(4,128)(2,1)} async-done(((bf16[1,4,1152,1536]{3,1,0,2:T(4,128)(2,1)}), bf16[1,4,1152,1536]{3,1,0,2:T(4,128)(2,1)}, u32[]{:S(2)}, u32[]{:S(2)}) %all-to-all-start.1) | async-done | bytes 14155808 | tf_op jit(solution)/shard_map/all_to_all | solution.py:240
  1227.8 9.8 copy.318
  1237.6 6.5 copy.319
  1244.8 42.1 %psum.7 = f32[2,1536]{1,0:T(2,128)} all-reduce(f32[2,1536]{1,0:T(2,128)} %pad_maximum_fusion.14), channel_id=1, replica_groups=mesh['expert'=4,'shard'=8] {'expert','shard'}, use_global_device_ids=true, to_apply=%region_15.16 | all-reduce | flops 3072 | bytes 24576 | tf_op jit(solution)/shard_map/psum | solution.py:325
  1293.0 17.5 %fusion.81 = bf16[384,1536]{1,0:T(8,128)(2,1)} fusion(f32[384,1536]{1,0:T(8,128)S(1)} %copy-done.24, bf16[4608,1536]{1,0:T(8,128)(2,1)} %bitcast.316, s32[384]{0:T(512)} %copy-done.72, s32[384]{0:T(512)} %copy-done.75, s32[384]{0:T(512)} %copy-done.78, s32[384]{0:T(512)} %copy-done.81, s32[384]{0:T(512)} %copy-done.84, s32[384]{0:T(512)} %copy-done.87, ...), kind=kOutput, calls=%fused_computation.119 | convolution fusion | flops 5493620736 | bytes 17713152 | tf_op jit(solution)/shard_map/st,sd->td/dot_general | solution.py:241
  1310.5 6.1 fusion.36
  1316.6 8.5 multiply_reduce_fusion
  1325.1 5.9 multiply_reduce_fusion.2
  1331.0 11.4 fusion.39
  1342.4 13.6 fusion.41
  1359.0 4.5 copy.353
  (342 shorter events, 86.0 us)
Async XLA Ops:
  7.2 186.1 %all-gather.3.cloned.1.call-start = ((), (), s32[]{:S(2)}) async-start(), calls=%async_computation.6 | async-start | bytes 12976128 | tf_op jit(solution)/shard_map/all_gather | solution.py:182
  10.1 7.6 copy-start.52
  10.2 13.7 copy-start.57
  10.2 348.8 %all-gather.5.cloned.1.call-start = ((), (), s32[]{:S(2)}) async-start(), calls=%async_computation.7 | async-start | bytes 21233664 | tf_op jit(solution)/shard_map/all_gather | solution.py:189
  17.0 13.2 copy-start.34
  23.8 32.9 %copy-start.67 = (pred[384]{0:T(512)(128)(4,1)}, pred[384]{0:T(512)(128)(4,1)S(1)}, u32[]{:S(2)}) copy-start(pred[384]{0:T(512)(128)(4,1)S(1)} %iota_compare_fusion.10) | copy-start | bytes 1156
  23.9 21.4 %copy-start.94 = (bf16[384]{0:T(512)(128)(2,1)}, bf16[384]{0:T(512)(128)(2,1)S(1)}, u32[]{:S(2)}) copy-start(bf16[384]{0:T(512)(128)(2,1)S(1)} %get-tuple-element.94) | copy-start | bytes 2308
  23.9 21.4 %copy-start.95 = (bf16[384]{0:T(512)(128)(2,1)}, bf16[384]{0:T(512)(128)(2,1)S(1)}, u32[]{:S(2)}) copy-start(bf16[384]{0:T(512)(128)(2,1)S(1)} %get-tuple-element.95) | copy-start | bytes 2308
  23.9 21.4 %copy-start.96 = (bf16[384]{0:T(512)(128)(2,1)}, bf16[384]{0:T(512)(128)(2,1)S(1)}, u32[]{:S(2)}) copy-start(bf16[384]{0:T(512)(128)(2,1)S(1)} %get-tuple-element.96) | copy-start | bytes 2308
  23.9 21.4 %copy-start.97 = (bf16[384]{0:T(512)(128)(2,1)}, bf16[384]{0:T(512)(128)(2,1)S(1)}, u32[]{:S(2)}) copy-start(bf16[384]{0:T(512)(128)(2,1)S(1)} %get-tuple-element.97) | copy-start | bytes 2308
  23.9 21.4 %copy-start.98 = (bf16[384]{0:T(512)(128)(2,1)}, bf16[384]{0:T(512)(128)(2,1)S(1)}, u32[]{:S(2)}) copy-start(bf16[384]{0:T(512)(128)(2,1)S(1)} %get-tuple-element.98) | copy-start | bytes 2308
  23.9 21.4 %copy-start.99 = (bf16[384]{0:T(512)(128)(2,1)}, bf16[384]{0:T(512)(128)(2,1)S(1)}, u32[]{:S(2)}) copy-start(bf16[384]{0:T(512)(128)(2,1)S(1)} %get-tuple-element.99) | copy-start | bytes 2308
  24.0 21.4 %copy-start.100 = (bf16[384]{0:T(512)(128)(2,1)}, bf16[384]{0:T(512)(128)(2,1)S(1)}, u32[]{:S(2)}) copy-start(bf16[384]{0:T(512)(128)(2,1)S(1)} %get-tuple-element.100) | copy-start | bytes 2308
  24.0 21.4 %copy-start.101 = (bf16[384]{0:T(512)(128)(2,1)}, bf16[384]{0:T(512)(128)(2,1)S(1)}, u32[]{:S(2)}) copy-start(bf16[384]{0:T(512)(128)(2,1)S(1)} %get-tuple-element.101) | copy-start | bytes 2308
  24.0 21.3 %copy-start.69 = (s32[384]{0:T(512)}, s32[384]{0:T(512)S(1)}, u32[]{:S(2)}) copy-start(s32[384]{0:T(512)S(1)} %get-tuple-element.84) | copy-start | bytes 4612
  24.0 21.3 %copy-start.72 = (s32[384]{0:T(512)}, s32[384]{0:T(512)S(1)}, u32[]{:S(2)}) copy-start(s32[384]{0:T(512)S(1)} %get-tuple-element.85) | copy-start | bytes 4612
  24.1 21.3 %copy-start.75 = (s32[384]{0:T(512)}, s32[384]{0:T(512)S(1)}, u32[]{:S(2)}) copy-start(s32[384]{0:T(512)S(1)} %get-tuple-element.86) | copy-start | bytes 4612
  24.1 21.3 %copy-start.78 = (s32[384]{0:T(512)}, s32[384]{0:T(512)S(1)}, u32[]{:S(2)}) copy-start(s32[384]{0:T(512)S(1)} %get-tuple-element.87) | copy-start | bytes 4612
  24.1 21.3 %copy-start.81 = (s32[384]{0:T(512)}, s32[384]{0:T(512)S(1)}, u32[]{:S(2)}) copy-start(s32[384]{0:T(512)S(1)} %get-tuple-element.88) | copy-start | bytes 4612
  24.1 21.3 %copy-start.84 = (s32[384]{0:T(512)}, s32[384]{0:T(512)S(1)}, u32[]{:S(2)}) copy-start(s32[384]{0:T(512)S(1)} %get-tuple-element.89) | copy-start | bytes 4612
  24.1 21.3 %copy-start.87 = (s32[384]{0:T(512)}, s32[384]{0:T(512)S(1)}, u32[]{:S(2)}) copy-start(s32[384]{0:T(512)S(1)} %get-tuple-element.90) | copy-start | bytes 4612
  24.1 21.3 %copy-start.90 = (s32[384]{0:T(512)}, s32[384]{0:T(512)S(1)}, u32[]{:S(2)}) copy-start(s32[384]{0:T(512)S(1)} %get-tuple-element.91) | copy-start | bytes 4612
  45.4 10.0 copy-start.53
  45.4 10.0 copy-start.2
  45.4 246.0 %all-to-all-start.2 = ((bf16[4,4,288,1536]{3,2,1,0:T(8,128)(2,1)}), bf16[4,4,288,1536]{3,2,1,0:T(8,128)(2,1)}, u32[]{:S(2)}, u32[]{:S(2)}) async-start(bf16[4,4,288,1536]{3,2,1,0:T(8,128)(2,1)} %bitcast.314), calls=%async_computation.2 | async-start | bytes 28311552 | tf_op jit(solution)/shard_map/all_to_all | solution.py:253
  55.5 189.5 %copy-start.48 = (f32[1536]{0:T(1024)}, f32[1536]{0:T(1024)S(1)}, u32[]{:S(2)}) copy-start(f32[1536]{0:T(1024)S(1)} %get-tuple-element.93) | copy-start | bytes 18436
  55.5 219.4 %copy-start.54 = (f32[1536]{0:T(1024)}, f32[1536]{0:T(1024)S(1)}, u32[]{:S(2)}) copy-start(f32[1536]{0:T(1024)S(1)} %get-tuple-element.92) | copy-start | bytes 18436
  55.8 189.2 %copy-start.50 = (f32[384]{0:T(512)}, f32[384]{0:T(512)S(1)}, u32[]{:S(2)}) copy-start(f32[384]{0:T(512)S(1)} %add_rsqrt_fusion.1) | copy-start | bytes 4612
  56.7 193.2 %copy-start.30 = (f32[384,32]{0,1:T(8,128)}, f32[384,32]{0,1:T(8,128)S(1)}, u32[]{:S(2)}) copy-start(f32[384,32]{0,1:T(8,128)S(1)} %get-tuple-element.124) | copy-start | bytes 147460
  216.7 47.6 %copy-start.25 = (bf16[384,512]{0,1:T(8,128)(2,1)}, bf16[384,512]{0,1:T(8,128)(2,1)S(1)}, u32[]{:S(2)}) copy-start(bf16[384,512]{0,1:T(8,128)(2,1)S(1)} %copy.303) | copy-start | bytes 1179652
  226.6 6.9 copy-start.1
  238.1 6.9 copy-start.4
  256.8 7.6 copy-start.43
  256.8 15.7 %slice-start.9 = ((s8[6291456]{0:T(1024)(128)(4,1)}), s8[2097152]{0:T(1024)(128)(4,1)S(1)}, s32[]{:S(2)}) async-start(s8[6291456]{0:T(1024)(128)(4,1)} %bitcast.327), calls=%async_computation.19 | async-start | bytes 4194304
  264.3 8.2 copy-start.45
  264.3 8.2 slice-start.10
  291.5 7.0 copy-start.66
  291.5 161.7 %all-to-all-start = ((bf16[4,4,288,1536]{3,2,1,0:T(8,128)(2,1)}), bf16[4,4,288,1536]{3,2,1,0:T(8,128)(2,1)}, u32[]{:S(2)}, u32[]{:S(2)}) async-start(bf16[4,4,288,1536]{3,2,1,0:T(8,128)(2,1)} %bitcast.315), calls=%async_computation | async-start | bytes 28311552 | tf_op jit(solution)/shard_map/all_to_all | solution.py:238
  298.4 1012.0 %reduce-scatter.5.cloned.1.call-start = ((), (), s32[]{:S(2)}) async-start(), calls=%async_computation.9 | async-start | bytes 21233664 | tf_op jit(solution)/shard_map/reduce_scatter | solution.py:322
  587.6 19.3 %copy-start.59 = (s32[1024]{0:T(1024)S(1)}, s32[1024]{0:T(1024)}, u32[]{:S(2)}) copy-start(s32[1024]{0:T(1024)} %pad_clamp_fusion) | copy-start | bytes 12292
  690.8 6.8 copy-start.44
  690.8 6.8 copy-start.46
  690.8 160.7 %all-to-all-start.3 = ((bf16[1,4,1152,1536]{3,1,0,2:T(4,128)(2,1)}), bf16[1,4,1152,1536]{3,1,0,2:T(4,128)(2,1)}, u32[]{:S(2)}, u32[]{:S(2)}) async-start(bf16[1,4,1152,1536]{3,1,0,2:T(4,128)(2,1)} %copy.323), calls=%async_computation.3 | async-start | bytes 28311552 | tf_op jit(solution)/shard_map/all_to_all | solution.py:257
  697.6 666.0 %reduce-scatter.3.cloned.1.call-start = ((), (), s32[]{:S(2)}) async-start(), calls=%async_computation.8 | async-start | bytes 25952256 | tf_op jit(solution)/shard_map/reduce_scatter | solution.py:316
  864.2 11.3 copy-start.35
  864.2 11.3 copy-start.68
  887.5 13.4 slice-start
  887.5 13.4 slice-start.1
  887.5 13.4 slice-start.2
  887.5 13.4 slice-start.3
  887.5 13.4 copy-start.38
  901.0 6.8 copy-start.19
  901.0 6.9 copy-start.21
  910.4 7.6 copy-start.26
  1022.6 7.2 copy-start.104
  1022.6 7.7 copy-start.63
  1022.6 205.1 %all-to-all-start.1 = ((bf16[1,4,1152,1536]{3,1,0,2:T(4,128)(2,1)}), bf16[1,4,1152,1536]{3,1,0,2:T(4,128)(2,1)}, u32[]{:S(2)}, u32[]{:S(2)}) async-start(bf16[1,4,1152,1536]{3,1,0,2:T(4,128)(2,1)} %copy.317), calls=%async_computation.1 | async-start | bytes 28311552 | tf_op jit(solution)/shard_map/all_to_all | solution.py:240
  1237.6 50.3 %copy-start.62 = (f32[384]{0:T(512)S(1)}, f32[384]{0:T(512)}, u32[]{:S(2)}) copy-start(f32[384]{0:T(512)} %get-tuple-element.83) | copy-start | bytes 4612
  1237.6 51.7 %copy-start.9 = (f32[384,1536]{1,0:T(8,128)S(1)}, f32[384,1536]{1,0:T(8,128)}, u32[]{:S(2)}) copy-start(f32[384,1536]{1,0:T(8,128)} %copy-done.8) | copy-start | bytes 7077892
  1310.5 14.6 %slice-start.7 = ((s8[4718592]{0:T(1024)(128)(4,1)}), s8[4194304]{0:T(1024)(128)(4,1)S(1)}, s32[]{:S(2)}) async-start(s8[4718592]{0:T(1024)(128)(4,1)} %bitcast.309), calls=%async_computation.17 | async-start | bytes 8388608
  1316.5 8.5 slice-start.8
  1316.6 8.5 copy-start.7
  1316.6 8.5 copy-start.102
  1331.0 11.4 copy-start
  (61 other events, 222.2 us)
Sparse Core Ops, SparseCore 0:
  11.6 181.5 all-gather.2
  195.4 163.4 all-gather.4
  629.5 184.6 reduce-scatter.4
  970.1 346.6 reduce-scatter.2
where the time goes:
time: 1390 us; the launch traced here: 1380 us
  waiting for transfers between devices  537 us (39%)
  local copies, waits for them, and re-layouts  373 us (27%)
  matrix products  295 us (21%)
  other arithmetic  91.5 us (7%)
  blocking collectives  42.1 us (3%)
  starting transfers between devices  27.1 us (2%)
  between operations  17 us (1%)
    all_to_all x1, waiting for transfers between devices, per_device(): lax.all_to_all(produced[None], 'expert', split_axis=2, concat_axis=0, til...  197 us
    all_to_all x1, waiting for transfers between devices, per_device(): lax.all_to_all(grad_route[None], 'expert', split_axis=2, concat_axis=0, t...  153 us
    all_gather x1, waiting for transfers between devices, per_device(): lax.all_gather(attn_master.astype(jnp.bfloat16), ('expert', 'shard'), axi...  136 us
    all_gather x1, waiting for transfers between devices, per_device(): lax.all_gather(expert_master.astype(jnp.bfloat16), 'shard', axis=0, tiled...  45 us
    psum x1, blocking collectives, per_device(): lax.psum(jnp.stack([gain_one_part, gain_two_part]), ('expert', 'shard'))  42.1 us
    gather x2, local copies, waits for them, and re-layouts, natural_order(): return slotted[inverse]  38.2 us
    broadcast_in_dim x1, local copies, waits for them, and re-layouts, per_device(): produced[None]  37.7 us
    broadcast_in_dim x1, local copies, waits for them, and re-layouts, per_device(): grad_route[None]  37.6 us
  transfers between devices with their start and end apart: 8, of which 5 were waited for; matrix products, arithmetic and copies ran while one was open for 41% of the time, Pallas kernels for 0%

commit v1 on v0

v1 whole, which is shorter than its diff:
```python
import jax
import jax.numpy as jnp
from jax import lax
from jax.experimental import pallas as pl
from jax.experimental.pallas import tpu as pltpu
from jax.sharding import PartitionSpec as P

D = 1536
H = 24
KV = 8
HD = 64
FF = 512
TOP = 8
BLOCK = 128
EXP_DEV = 4
LANES = 128
VMEM_BYTES = 60 * 1024 * 1024
BF16 = jnp.bfloat16
F32 = jnp.float32


EPSILON = 1e-05
STEP_SIZE = 0.3


def rope_tables(positions):
    frequency = 10000.0 ** (-2.0 * jnp.arange(HD // 2, dtype=jnp.float32) / HD)
    angles = positions[:, None] * frequency[None, :]
    return (jnp.cos(angles), jnp.sin(angles))


def dot_nn(left, right):
    return lax.dot_general(left, right, (((1,), (0,)), ((), ())), preferred_element_type=F32)


def dot_nt(left, right):
    return lax.dot_general(left, right, (((1,), (1,)), ((), ())), preferred_element_type=F32)


def dot_tn(left, right):
    return lax.dot_general(left, right, (((0,), (0,)), ((), ())), preferred_element_type=F32)


def params(**more):
    return pltpu.CompilerParams(vmem_limit_bytes=VMEM_BYTES, **more)


def whole(memory_space):
    return pl.BlockSpec(memory_space=memory_space)


def held(shape):
    return pl.BlockSpec(shape, lambda *_: (0,) * len(shape))


def inverse_of(dealing):
    slot_count = dealing.shape[0]
    return (
        jnp.zeros((slot_count,), jnp.int32)
        .at[dealing]
        .set(jnp.arange(slot_count, dtype=jnp.int32), unique_indices=True)
    )


def assemble_experts(blocks, inverse):
    across, wide, tall = D // BLOCK, 2 * FF // BLOCK, FF // BLOCK
    first, second = across * wide, tall * across

    def kernel(inverse_ref, blocks_ref, gateup_ref, down_ref, gateup_two, down_two, sems):
        def out(expert):
            half = expert % 2
            return [
                pltpu.make_async_copy(gateup_two.at[half], gateup_ref.at[expert], sems.at[2 + half]),
                pltpu.make_async_copy(down_two.at[half], down_ref.at[expert], sems.at[2 + half]),
            ]

        for expert in range(EXP_DEV):
            base, half = expert * (first + second), expert % 2
            if expert >= 2:
                for copy in out(expert - 2):
                    copy.wait()

            def gateup_block(i, _):
                pltpu.make_async_copy(
                    blocks_ref.at[inverse_ref[base + i]],
                    block_at(gateup_two.at[half], i // wide, i % wide),
                    sems.at[half],
                ).start()
                return 0

            def down_block(i, _):
                pltpu.make_async_copy(
                    blocks_ref.at[inverse_ref[base + first + i]],
                    block_at(down_two.at[half], i // across, i % across),
                    sems.at[half],
                ).start()
                return 0

            lax.fori_loop(0, first, gateup_block, 0, unroll=4)
            lax.fori_loop(0, second, down_block, 0, unroll=4)
            pltpu.make_async_copy(gateup_two.at[half], gateup_two.at[half], sems.at[half]).wait()
            pltpu.make_async_copy(down_two.at[half], down_two.at[half], sems.at[half]).wait()
            for copy in out(expert):
                copy.start()
        for expert in (EXP_DEV - 2, EXP_DEV - 1):
            for copy in out(expert):
                copy.wait()

    return pl.pallas_call(
        kernel,
        name="assemble_experts",
        out_shape=(
            jax.ShapeDtypeStruct((EXP_DEV, D, 2 * FF), BF16),
            jax.ShapeDtypeStruct((EXP_DEV, FF, D), BF16),
        ),
        in_specs=[whole(pltpu.SMEM), whole(pl.ANY)],
        out_specs=(whole(pl.ANY), whole(pl.ANY)),
        scratch_shapes=[
            pltpu.VMEM((2, D, 2 * FF), BF16),
            pltpu.VMEM((2, FF, D), BF16),
            pltpu.SemaphoreType.DMA((4,)),
        ],
        compiler_params=params(),
        cost_estimate=pl.CostEstimate(flops=0, bytes_accessed=4 * blocks.size, transcendentals=0),
    )(inverse, blocks)


def weight_of(packed, expert):
    lane = lax.broadcasted_iota(jnp.int32, packed.shape, 1)
    return jnp.sum(jnp.where(lane == expert, packed.astype(F32), 0.0), axis=1, keepdims=True)


def expert_front(group, rows, packed, w_gateup, w_down):
    count = rows.shape[0]

    def kernel(group_ref, rows_ref, packed_ref, gateup_ref, down_ref, hidden_ref, both_ref, out_ref, total):
        step = pl.program_id(0)
        weight = weight_of(packed_ref[:, D:], group_ref[0] * EXP_DEV + step)
        gate_up = dot_nn(rows_ref[...], gateup_ref[0])
        gate, up = gate_up[:, :FF], gate_up[:, FF:]
        sigmoid = jax.nn.sigmoid(gate)
        silu = gate * sigmoid
        hidden_ref[0] = (silu * up).astype(BF16)
        grad_rows = (weight * packed_ref[:, :D].astype(F32)).astype(BF16)
        grad_hidden = dot_nt(grad_rows, down_ref[0])
        both_ref[0, :, :FF] = (grad_hidden * up * sigmoid * (1.0 + gate * (1.0 - sigmoid))).astype(BF16)
        both_ref[0, :, FF:] = (grad_hidden * silu).astype(BF16)
        route = dot_nt(both_ref[0], gateup_ref[0]).astype(BF16).astype(F32)

        @pl.when(step == 0)
        def _():
            total[...] = route

        @pl.when(step > 0)
        def _():
            total[...] += route

        @pl.when(step == EXP_DEV - 1)
        def _():
            out_ref[...] = total[...].astype(BF16)

    return pl.pallas_call(
        kernel,
        name="expert_front",
        grid=(EXP_DEV,),
        out_shape=(
            jax.ShapeDtypeStruct((EXP_DEV, count, FF), BF16),
            jax.ShapeDtypeStruct((EXP_DEV, count, 2 * FF), BF16),
            jax.ShapeDtypeStruct((count, D), BF16),
        ),
        in_specs=[
            whole(pltpu.SMEM),
            held((count, D)),
            held((count, D + LANES)),
            pl.BlockSpec((1, D, 2 * FF), lambda j: (j, 0, 0)),
            pl.BlockSpec((1, FF, D), lambda j: (j, 0, 0)),
        ],
        out_specs=(
            pl.BlockSpec((1, count, FF), lambda j: (j, 0, 0)),
            pl.BlockSpec((1, count, 2 * FF), lambda j: (j, 0, 0)),
            held((count, D)),
        ),
        scratch_shapes=[pltpu.VMEM((count, D), F32)],
        compiler_params=params(dimension_semantics=("arbitrary",)),
        cost_estimate=pl.CostEstimate(
            flops=EXP_DEV * 2 * 5 * count * D * FF,
            bytes_accessed=EXP_DEV * 3 * D * FF * 2,
            transcendentals=EXP_DEV * count * FF,
        ),
    )(group, rows, packed, w_gateup, w_down)


def expert_weight_grads(group, inverse, rows, packed, hidden, both):
    parts = len(rows)
    count = rows[0].shape[0]
    slots = inverse.shape[0]
    across, wide, tall = D // BLOCK, 2 * FF // BLOCK, FF // BLOCK
    first, second = across * wide, tall * across
    tile = 256

    def kernel(group_ref, inverse_ref, *refs):
        rows_refs, packed_refs = refs[:parts], refs[parts : 2 * parts]
        hidden_refs, both_refs = refs[2 * parts : 3 * parts], refs[3 * parts : 4 * parts]
        out_ref, stage_gateup, stage_down, sems = refs[4 * parts :]
        step = pl.program_id(0)
        base = step * (first + second)

        def wait_gateup():
            pltpu.make_async_copy(stage_gateup, stage_gateup, sems.at[0]).wait()

        def wait_down():
            pltpu.make_async_copy(stage_down, stage_down, sems.at[1]).wait()

        pl.when(step > 0)(wait_gateup)
        for at in range(0, 2 * FF, tile):
            span = slice(at, at + tile)
            stage_gateup[:, span] = sum(
                dot_tn(x[...], b[0, :, span]) for x, b in zip(rows_refs, both_refs)
            ).astype(BF16)

        def gateup_block(i, _):
            row, col = i // wide, i % wide
            pltpu.make_async_copy(
                stage_gateup.at[pl.ds(pl.multiple_of(row * BLOCK, BLOCK), BLOCK), pl.ds(pl.multiple_of(col * BLOCK, BLOCK), BLOCK)],
                out_ref.at[inverse_ref[base + i]],
                sems.at[0],
            ).start()
            return 0

        lax.fori_loop(0, first, gateup_block, 0, unroll=8)
        pl.when(step > 0)(wait_down)
        weights = [
            weight_of(p[:, D:], group_ref[0] * EXP_DEV + step) for p in packed_refs
        ]
        for at in range(0, D, tile):
            span = slice(at, at + tile)
            stage_down[:, span] = sum(
                dot_tn(h[0], (w * p[:, span].astype(F32)).astype(BF16))
                for h, p, w in zip(hidden_refs, packed_refs, weights)
            ).astype(BF16)

        def down_block(i, _):
            row, col = i // across, i % across
            pltpu.make_async_copy(
                stage_down.at[pl.ds(pl.multiple_of(row * BLOCK, BLOCK), BLOCK), pl.ds(pl.multiple_of(col * BLOCK, BLOCK), BLOCK)],
                out_ref.at[inverse_ref[base + first + i]],
                sems.at[1],
            ).start()
            return 0

        lax.fori_loop(0, second, down_block, 0, unroll=8)

        @pl.when(step == EXP_DEV - 1)
        def _():
            wait_gateup()
            wait_down()

    return pl.pallas_call(
        kernel,
        name="expert_weight_grads",
        grid=(EXP_DEV,),
        out_shape=jax.ShapeDtypeStruct((slots, BLOCK, BLOCK), BF16),
        in_specs=[whole(pltpu.SMEM), whole(pltpu.SMEM)]
        + [held((count, D))] * parts
        + [held((count, D + LANES))] * parts
        + [pl.BlockSpec((1, count, FF), lambda j: (j, 0, 0))] * parts
        + [pl.BlockSpec((1, count, 2 * FF), lambda j: (j, 0, 0))] * parts,
        out_specs=whole(pl.ANY),
        scratch_shapes=[
            pltpu.VMEM((D, 2 * FF), BF16),
            pltpu.VMEM((FF, D), BF16),
            pltpu.SemaphoreType.DMA((2,)),
        ],
        compiler_params=params(dimension_semantics=("arbitrary",)),
        cost_estimate=pl.CostEstimate(
            flops=EXP_DEV * 2 * 3 * parts * count * D * FF,
            bytes_accessed=EXP_DEV * 3 * (parts * count * FF + D * FF) * 2,
            transcendentals=0,
        ),
    )(group, inverse, *rows, *packed, *hidden, *both)


def expert_outputs(group, packed, hidden, w_down):
    parts = len(packed)
    count = packed[0].shape[0]

    def kernel(group_ref, *refs):
        packed_refs, hidden_refs = refs[:parts], refs[parts : 2 * parts]
        down_ref = refs[2 * parts]
        out_refs, totals = refs[2 * parts + 1 : 3 * parts + 1], refs[3 * parts + 1 :]
        step = pl.program_id(0)
        for packed_ref, hidden_ref, out_ref, total in zip(packed_refs, hidden_refs, out_refs, totals):
            weight = weight_of(packed_ref[...], group_ref[0] * EXP_DEV + step)
            produced = dot_nn(hidden_ref[0], down_ref[0]).astype(BF16).astype(F32)
            term = weight * produced

            @pl.when(step == 0)
            def _():
                total[...] = term

            @pl.when(step > 0)
            def _():
                total[...] += term

            @pl.when(step == EXP_DEV - 1)
            def _():
                out_ref[...] = total[...].astype(BF16)

    return pl.pallas_call(
        kernel,
        name="expert_outputs",
        grid=(EXP_DEV,),
        out_shape=tuple(jax.ShapeDtypeStruct((count, D), BF16) for _ in range(parts)),
        in_specs=[whole(pltpu.SMEM)]
        + [pl.BlockSpec((count, LANES), lambda j: (0, D // LANES))] * parts
        + [pl.BlockSpec((1, count, FF), lambda j: (j, 0, 0))] * parts
        + [pl.BlockSpec((1, FF, D), lambda j: (j, 0, 0))],
        out_specs=tuple(held((count, D)) for _ in range(parts)),
        scratch_shapes=[pltpu.VMEM((count, D), F32)] * parts,
        compiler_params=params(dimension_semantics=("arbitrary",)),
        cost_estimate=pl.CostEstimate(
            flops=EXP_DEV * 2 * parts * count * D * FF,
            bytes_accessed=EXP_DEV * (parts * count * FF + D * FF) * 2,
            transcendentals=0,
        ),
    )(group, *packed, *hidden, w_down)


QUERY_END = H * HD
KEYVAL_END = QUERY_END + 2 * KV * HD
ACROSS = D // BLOCK
QUERY_COLS = QUERY_END // BLOCK
KEYVAL_COLS = (KEYVAL_END - QUERY_END) // BLOCK
OUT_COLS = D // BLOCK
ALL_COLS = QUERY_COLS + KEYVAL_COLS + OUT_COLS


def attention_places(natural):
    first = ACROSS * QUERY_COLS
    second = first + ACROSS * KEYVAL_COLS
    in_keyval, in_out = natural - first, natural - second
    row = jnp.where(
        natural < first,
        natural // QUERY_COLS,
        jnp.where(natural < second, in_keyval // KEYVAL_COLS, in_out // OUT_COLS),
    )
    col = jnp.where(
        natural < first,
        natural % QUERY_COLS,
        jnp.where(
            natural < second,
            QUERY_COLS + in_keyval % KEYVAL_COLS,
            QUERY_COLS + KEYVAL_COLS + in_out % OUT_COLS,
        ),
    )
    return row.astype(jnp.int32), col.astype(jnp.int32)


def block_at(ref, row, col):
    return ref.at[
        pl.ds(pl.multiple_of(row * BLOCK, BLOCK), BLOCK),
        pl.ds(pl.multiple_of(col * BLOCK, BLOCK), BLOCK),
    ]


def turn(values, cosine, sine):
    lane = lax.broadcasted_iota(jnp.int32, values.shape, 1)
    partner = jnp.where(
        lane % HD < HD // 2,
        pltpu.roll(values, LANES - HD // 2, 1),
        pltpu.roll(values, HD // 2, 1),
    )
    return values * cosine + partner * sine


def softmax_of(queries, keys, length):
    count = queries.shape[0]
    scores = dot_nt(queries, keys) * HD ** (-0.5)
    at_row = lax.broadcasted_iota(jnp.int32, (count, count), 0)
    at_col = lax.broadcasted_iota(jnp.int32, (count, count), 1)
    scores = jnp.where((at_col <= at_row) & (at_col < length), scores, -1e30)
    weights = jnp.exp(scores - jnp.max(scores, axis=1, keepdims=True))
    return weights * (1.0 / jnp.sum(weights, axis=1, keepdims=True))


def unit_rows(values):
    scale = lax.rsqrt(jnp.mean(values * values, axis=-1, keepdims=True) + EPSILON)
    return values * scale, scale


def attention_front(lengths, block_rows, block_cols, tokens, gains, cosine, sine, pieces):
    count = tokens.shape[0]
    group_size = H // KV

    def kernel(length_ref, row_ref, col_ref, tokens_ref, gains_ref, cosine_ref, sine_ref, *refs):
        piece_refs = refs[: len(pieces)]
        normed_ref, middle_ref, mixed_ref, q_ref, k_ref, v_ref, all_ref = refs[len(pieces) : -3]
        weights, heads, sems = refs[-3:]
        offset = 0
        for piece in piece_refs:

            def bring(i, _, piece=piece, offset=offset):
                pltpu.make_async_copy(
                    piece.at[i],
                    block_at(weights, row_ref[offset + i], col_ref[offset + i]),
                    sems.at[0],
                ).start()
                return 0

            lax.fori_loop(0, piece.shape[0], bring, 0, unroll=4)
            offset += piece.shape[0]
        residual = tokens_ref[...].astype(F32)
        normed = (unit_rows(residual)[0] * gains_ref[0:1, :]).astype(BF16)
        pltpu.make_async_copy(weights, weights, sems.at[0]).wait()
        keep = pltpu.make_async_copy(weights, all_ref, sems.at[1])
        keep.start()
        cosine, sine = cosine_ref[...], sine_ref[...]
        for at in range(0, KEYVAL_END, 2 * LANES):
            product = dot_nn(normed, weights[:, at : at + 2 * LANES])
            for half in range(2):
                pair = product[:, half * LANES : (half + 1) * LANES]
                column = at + half * LANES
                if column < QUERY_END + KV * HD:
                    pair = turn(pair, cosine, sine)
                pair = pair.astype(BF16)
                if column < QUERY_END:
                    target, head = q_ref, column // HD
                elif column < QUERY_END + KV * HD:
                    target, head = k_ref, (column - QUERY_END) // HD
                else:
                    target, head = v_ref, (column - QUERY_END - KV * HD) // HD
                target[head] = pair[:, :HD]
                target[head + 1] = pair[:, HD:]
        length = length_ref[0]

        def attend(j, _):
            for h in range(group_size):
                probs = softmax_of(q_ref[j * group_size + h], k_ref[j], length).astype(BF16)
                heads[j * group_size + h] = dot_nn(probs, v_ref[j]).astype(BF16)
            return 0

        lax.fori_loop(0, KV, attend, 0)
        for pair in range(H // 2):
            mixed_ref[:, pair * LANES : (pair + 1) * LANES] = jnp.concatenate(
                [heads[2 * pair], heads[2 * pair + 1]], axis=1
            )
        middle = residual + dot_nn(mixed_ref[...], weights[:, KEYVAL_END:])
        middle_ref[...] = middle
        normed_ref[...] = (unit_rows(middle)[0] * gains_ref[1:2, :]).astype(BF16)
        keep.wait()

    vmem = whole(pltpu.VMEM)
    return pl.pallas_call(
        kernel,
        name="attention_front",
        out_shape=(
            jax.ShapeDtypeStruct((count, D), BF16),
            jax.ShapeDtypeStruct((count, D), F32),
            jax.ShapeDtypeStruct((count, H * HD), BF16),
            jax.ShapeDtypeStruct((H, count, HD), BF16),
            jax.ShapeDtypeStruct((KV, count, HD), BF16),
            jax.ShapeDtypeStruct((KV, count, HD), BF16),
            jax.ShapeDtypeStruct((D, ALL_COLS * BLOCK), BF16),
        ),
        in_specs=[whole(pltpu.SMEM)] * 3 + [vmem] * 4 + [whole(pl.ANY)] * len(pieces),
        out_specs=(vmem,) * 6 + (whole(pl.ANY),),
        scratch_shapes=[
            pltpu.VMEM((D, ALL_COLS * BLOCK), BF16),
            pltpu.VMEM((H, count, HD), BF16),
            pltpu.SemaphoreType.DMA((2,)),
        ],
        compiler_params=params(),
        cost_estimate=pl.CostEstimate(
            flops=2 * count * D * ALL_COLS * BLOCK + 4 * H * count * count * HD,
            bytes_accessed=4 * D * ALL_COLS * BLOCK,
            transcendentals=H * count * count,
        ),
    )(lengths, block_rows, block_cols, tokens, gains, cosine, sine, *pieces)


def attention_back(lengths, positions, tokens, packed, gains, cosine, sine, middle, mixed, q, k, v, w_all, partials, near):
    count = tokens.shape[0]
    group_size = H // KV
    blocks = positions.shape[0]
    parts = len(partials)

    def kernel(length_ref, position_ref, tokens_ref, packed_ref, gains_ref, cosine_ref, sine_ref, middle_ref, mixed_ref,
               q_ref, k_ref, v_ref, *refs):
        partial_refs = refs[:parts]
        all_ref, input_grad_ref, gain_ref, near_ref, far_ref = refs[parts : parts + 5]
        weights, stage, grad_heads, grad_columns, sems = refs[parts + 5 :]
        bring_out = pltpu.make_async_copy(all_ref.at[:, pl.ds(KEYVAL_END, D)], weights.at[:, pl.ds(KEYVAL_END, D)], sems.at[0])
        bring_in = pltpu.make_async_copy(all_ref.at[:, pl.ds(0, KEYVAL_END)], weights.at[:, pl.ds(0, KEYVAL_END)], sems.at[1])
        bring_out.start()
        bring_in.start()

        def send(first, columns, col_offset):
            def one(i, _):
                place = position_ref[first + i]
                source = block_at(stage, i // columns, col_offset + i % columns)

                @pl.when(place < near)
                def _():
                    pltpu.make_async_copy(source, near_ref.at[place], sems.at[2]).start()

                @pl.when(place >= near)
                def _():
                    pltpu.make_async_copy(source, far_ref.at[place - near], sems.at[2]).start()

                return 0

            lax.fori_loop(0, ACROSS * columns, one, 0, unroll=4)

        grad_normed = partial_refs[0][...].astype(F32)
        for ref in partial_refs[1:]:
            grad_normed = grad_normed + ref[...].astype(F32)
        unit, scale = unit_rows(middle_ref[...])
        gain_ref[1:2, :] = jnp.sum(grad_normed * unit, axis=0, keepdims=True)
        scaled = grad_normed * gains_ref[1:2, :]
        grad_middle = packed_ref[:, :D].astype(F32) + scale * (
            scaled - unit * jnp.mean(scaled * unit, axis=-1, keepdims=True)
        )
        input_grad_ref[...] = grad_middle
        grad_attn = grad_middle.astype(BF16)
        for at in range(0, D, 4 * LANES):
            stage[:, KEYVAL_END + at : KEYVAL_END + at + 4 * LANES] = dot_tn(
                mixed_ref[...], grad_attn[:, at : at + 4 * LANES]
            ).astype(BF16)
        send(ACROSS * (QUERY_COLS + KEYVAL_COLS), OUT_COLS, QUERY_COLS + KEYVAL_COLS)
        bring_out.wait()
        for at in range(0, H * HD, 2 * LANES):
            product = dot_nt(grad_attn, weights[at : at + 2 * LANES, KEYVAL_END:]).astype(BF16)
            for part in range(2 * LANES // HD):
                grad_heads[at // HD + part] = product[:, part * HD : (part + 1) * HD]
        length = length_ref[0]

        def attend(j, _):
            keys, values = k_ref[j], v_ref[j]
            grad_keys = jnp.zeros((count, HD), F32)
            grad_values = jnp.zeros((count, HD), F32)
            for h in range(group_size):
                head = j * group_size + h
                queries, grad_mixed = q_ref[head], grad_heads[head]
                probs = softmax_of(queries, keys, length)
                grad_values = grad_values + dot_tn(probs.astype(BF16), grad_mixed)
                grad_probs = dot_nt(grad_mixed, values)
                inner = jnp.sum(probs * grad_probs, axis=1, keepdims=True)
                grad_scores = (probs * (grad_probs - inner)).astype(BF16)
                grad_columns[head] = dot_nn(grad_scores, keys) * HD ** (-0.5)
                grad_keys = grad_keys + dot_tn(grad_scores, queries)
            grad_columns[H + j] = grad_keys * HD ** (-0.5)
            grad_columns[H + KV + j] = grad_values
            return 0

        lax.fori_loop(0, KV, attend, 0)
        cosine, sine = cosine_ref[...], -sine_ref[...]
        residual = tokens_ref[...].astype(F32)
        unit_one, scale_one = unit_rows(residual)
        normed = (unit_one * gains_ref[0:1, :]).astype(BF16)
        bring_in.wait()
        grad_normed_one = jnp.zeros((count, D), F32)
        for at in range(0, KEYVAL_END, 4 * LANES):
            pairs = []
            for column in range(at, at + 4 * LANES, LANES):
                head = column // HD
                pair = jnp.concatenate([grad_columns[head], grad_columns[head + 1]], axis=1)
                if column < QUERY_END + KV * HD:
                    pair = turn(pair, cosine, sine)
                pairs.append(pair.astype(BF16))
            columns = jnp.concatenate(pairs, axis=1)
            span = slice(at, at + 4 * LANES)
            stage[:, span] = dot_tn(normed, columns).astype(BF16)
            grad_normed_one = grad_normed_one + dot_nt(columns, weights[:, span])
        send(0, QUERY_COLS, 0)
        send(ACROSS * QUERY_COLS, KEYVAL_COLS, QUERY_COLS)
        gain_ref[0:1, :] = jnp.sum(grad_normed_one * unit_one, axis=0, keepdims=True)
        scaled_one = grad_normed_one * gains_ref[0:1, :]
        input_grad_ref[...] += scale_one * (
            scaled_one - unit_one * jnp.mean(scaled_one * unit_one, axis=-1, keepdims=True)
        )
        pltpu.make_async_copy(stage, stage, sems.at[2]).wait()

    vmem, any_space = whole(pltpu.VMEM), whole(pl.ANY)
    return pl.pallas_call(
        kernel,
        name="attention_back",
        out_shape=(
            jax.ShapeDtypeStruct((count, D), F32),
            jax.ShapeDtypeStruct((2, D), F32),
            jax.ShapeDtypeStruct((near, BLOCK, BLOCK), BF16),
            jax.ShapeDtypeStruct((max(blocks - near, 1), BLOCK, BLOCK), BF16),
        ),
        in_specs=[whole(pltpu.SMEM)] * 2 + [vmem] * (10 + parts) + [any_space],
        out_specs=(vmem, vmem, any_space, any_space),
        scratch_shapes=[
            pltpu.VMEM((D, ALL_COLS * BLOCK), BF16),
            pltpu.VMEM((D, ALL_COLS * BLOCK), BF16),
            pltpu.VMEM((H, count, HD), BF16),
            pltpu.VMEM((H + 2 * KV, count, HD), F32),
            pltpu.SemaphoreType.DMA((3,)),
        ],
        compiler_params=params(),
        cost_estimate=pl.CostEstimate(
            flops=4 * count * D * ALL_COLS * BLOCK + 10 * H * count * count * HD,
            bytes_accessed=4 * D * ALL_COLS * BLOCK,
            transcendentals=H * count * count,
        ),
    )(lengths, positions, tokens, packed, gains, cosine, sine, middle, mixed, q, k, v, *partials, w_all)


def split_low(values):
    high = values.astype(BF16)
    return high, (values - high.astype(F32)).astype(BF16)


def shampoo(gradient, statistics, inverse_roots, master):
    terms = len(gradient)
    slots = master.shape[0]
    many = next(n for n in (6, 4, 3, 2, 1) if slots % n == 0)

    def kernel(*refs):
        term_refs = refs[:terms]
        stats_ref, roots_ref, master_ref, grad_ref, stats_out, master_out = refs[terms:]
        for i in range(many):
            total = term_refs[0][i].astype(F32)
            for ref in term_refs[1:]:
                total = total + ref[i].astype(F32)
            low = total.astype(BF16)
            grad = low.astype(F32)
            grad_ref[i] = grad
            scale = 0.5 / (jnp.mean(grad * grad) + 1e-06)
            stats_out[i, 0] = 0.5 * stats_ref[i, 0] + scale * dot_nt(low, low)
            stats_out[i, 1] = 0.5 * stats_ref[i, 1] + scale * dot_tn(low, low)
            left_high, left_low = split_low(roots_ref[i, 0])
            turned_high, turned_low = split_low(dot_nn(left_high, low) + dot_nn(left_low, low))
            right_high, right_low = split_low(roots_ref[i, 1])
            turned = (
                dot_nn(turned_high, right_high)
                + dot_nn(turned_low, right_high)
                + dot_nn(turned_high, right_low)
            )
            direction = turned * lax.rsqrt(jnp.mean(turned * turned) + 1e-06)
            own = master_ref[i]
            spread = jnp.sqrt(jnp.mean(own * own))
            master_out[i] = own - STEP_SIZE * spread * direction

    one = pl.BlockSpec((many, BLOCK, BLOCK), lambda i: (i, 0, 0))
    two = pl.BlockSpec((many, 2, BLOCK, BLOCK), lambda i: (i, 0, 0, 0))
    return pl.pallas_call(
        kernel,
        name="shampoo",
        grid=(slots // many,),
        out_shape=(
            jax.ShapeDtypeStruct((slots, BLOCK, BLOCK), F32),
            jax.ShapeDtypeStruct((slots, 2, BLOCK, BLOCK), F32),
            jax.ShapeDtypeStruct((slots, BLOCK, BLOCK), F32),
        ),
        in_specs=[one] * terms + [two, two, one],
        out_specs=(one, two, one),
        compiler_params=params(dimension_semantics=("arbitrary",)),
        cost_estimate=pl.CostEstimate(
            flops=slots * 7 * 2 * BLOCK**3,
            bytes_accessed=slots * BLOCK * BLOCK * (2 * terms + 36),
            transcendentals=0,
        ),
    )(*gradient, statistics, inverse_roots, master)


def move(array, pairs):
    return lax.ppermute(array, "shard", pairs)


def sibling(array):
    return move(array, [(i, i ^ 1) for i in range(lax.axis_size("shard"))])


def along(array, distance):
    size = lax.axis_size("shard")
    return move(array, [(i, (i + 2 * distance) % size) for i in range(size)])


def two_ways(array, other_first):
    one, two = swap(array, 1), swap(array, 2)
    three = swap(two, 1) if other_first else swap(one, 2)
    return one, two, three


def gather_attention(own, deal):
    size, groups = lax.axis_size("shard"), lax.axis_size("expert")
    slots = own.shape[0]
    by_device = deal.reshape(groups, size, slots)
    if groups != 4 or size != 8:
        return [lax.all_gather(own, ("expert", "shard"), axis=0, tiled=True)], deal
    me_e, me_s = lax.axis_index("expert"), lax.axis_index("shard")
    pieces, names, far_names = [], [], []
    lines = [own] + [along(own, d) for d in range(1, size // 2)]
    for d, line in enumerate(lines):
        four = jnp.concatenate([line, *two_ways(line, d % 2 == 1)], axis=0)
        pieces.append(four)
        source = (me_s - 2 * d) % size
        for m in range(groups):
            names.append(by_device[me_e ^ m, source])
            far_names.append(by_device[me_e ^ m, source ^ 1])
    pieces += [sibling(piece) for piece in pieces]
    return pieces, jnp.concatenate(names + far_names)


def attention_positions(deal, slots):
    size, groups = lax.axis_size("shard"), lax.axis_size("expert")
    inverse = inverse_of(deal)
    if groups != 4 or size != 8:
        return inverse
    owner, within = inverse // slots, inverse % slots
    mask = (owner // size) ^ lax.axis_index("expert")
    me = lax.axis_index("shard")
    core = (owner % 2) ^ (me % 2)
    distance = ((owner % size) // 2 - me // 2) % (size // 2)
    return ((((core * groups + mask) * (size // 2)) + distance) * slots + within).astype(jnp.int32)


def add_low(left, right):
    return (left.astype(F32) + right.astype(F32)).astype(BF16)


def scatter_attention(near, far, slots):
    size, groups = lax.axis_size("shard"), lax.axis_size("expert")
    if groups != 4 or size != 8:
        return [lax.psum_scatter(near, ("expert", "shard"), scatter_dimension=0, tiled=True)]
    half = size // 4
    total = add_low(near, sibling(far)).reshape(groups, 2, half * slots, BLOCK, BLOCK)
    lines = []
    for part, (first, second) in enumerate(((1, 2), (2, 1))):
        mine = jnp.concatenate([total[0, part], total[second, part]], axis=0)
        theirs = jnp.concatenate([total[first, part], total[3, part]], axis=0)
        mine = add_low(mine, swap(theirs, first))
        mine, theirs = mine[: half * slots], mine[half * slots :]
        lines.append(add_low(mine, swap(theirs, second)))
    terms = [line[i * slots : (i + 1) * slots] for line in lines for i in range(half)]
    return [terms[0]] + [along(terms[d], d) for d in range(1, size // 2)]


def sum_everywhere(values):
    size, groups = lax.axis_size("shard"), lax.axis_size("expert")
    if groups != 4 or size != 8:
        return lax.psum(values, ("expert", "shard"))
    for mask in (1, 2, 4):
        values = values + move(values, [(i, i ^ mask) for i in range(size)])
    for mask in (1, 2):
        values = values + swap(values, mask)
    return values


def swap(array, mask):
    if mask == 0:
        return array
    return lax.ppermute(array, "expert", [(i, i ^ mask) for i in range(lax.axis_size("expert"))])


def per_device(
    tokens,
    cotangent,
    lengths,
    routes,
    route_gates,
    norm_gains,
    attn_master,
    attn_stats,
    attn_roots,
    attn_deal,
    expert_master,
    expert_stats,
    expert_roots,
    expert_deal,
):
    row_count = tokens.shape[0]
    groups = lax.axis_size("expert")
    group = lax.axis_index("expert").astype(jnp.int32).reshape(1)
    pieces, natural = gather_attention(attn_master.astype(BF16), attn_deal)
    expert_all = lax.all_gather(expert_master.astype(BF16), "shard", axis=0, tiled=True)
    places = jnp.arange(row_count)
    valid_rows = places < lengths[0]
    grad_low = jnp.where(valid_rows[:, None], cotangent, jnp.zeros_like(cotangent))
    expert_lane = jnp.arange(LANES, dtype=jnp.int32)
    weights_row = sum(
        jnp.where(routes[:, k, None] == expert_lane, route_gates[:, k, None], jnp.zeros((), BF16))
        for k in range(TOP)
    )
    packed = [swap(jnp.concatenate([grad_low, weights_row], axis=1), m) for m in range(groups)]
    cosine, sine = rope_tables(jnp.arange(row_count, dtype=F32))
    cosine = jnp.concatenate([cosine] * 4, axis=1)
    sine = jnp.concatenate([-sine, sine] * 2, axis=1)
    block_rows, block_cols = attention_places(natural)
    normed_two, middle, mixed, q, k, v, w_all = attention_front(
        lengths, block_rows, block_cols, tokens, norm_gains, cosine, sine, pieces
    )
    expert_inverse = inverse_of(expert_deal[0])
    w_gateup, w_down = assemble_experts(expert_all, expert_inverse)
    rows = [swap(normed_two, m) for m in range(groups)]
    fronts = {}
    for m in [*range(1, groups), 0]:
        fronts[m] = expert_front(group, rows[m], packed[m], w_gateup, w_down)
    hidden = [fronts[m][0] for m in range(groups)]
    both = [fronts[m][1] for m in range(groups)]
    partials = [swap(fronts[m][2], m) for m in range(groups)]
    expert_term = expert_weight_grads(group, expert_inverse, rows, packed, hidden, both)
    moe_parts = expert_outputs(group, packed, hidden, w_down)
    moe_sum = sum(swap(moe_parts[m], m).astype(F32) for m in range(groups))
    output = (middle + moe_sum).astype(BF16)
    slots = attn_master.shape[0]
    positions = attention_positions(attn_deal, slots)
    near = positions.shape[0] // (2 if groups == 4 and lax.axis_size("shard") == 8 else 1)
    input_grad, gain_parts, near_blocks, far_blocks = attention_back(
        lengths, positions, tokens, packed[0], norm_gains, cosine, sine, middle, mixed, q, k, v, w_all, partials, near
    )
    attn_terms = scatter_attention(near_blocks, far_blocks, slots)
    expert_term = lax.psum_scatter(expert_term, "shard", scatter_dimension=0, tiled=True)
    gain_grads = sum_everywhere(gain_parts)
    new_gains = norm_gains - STEP_SIZE * gain_grads * lax.rsqrt(
        jnp.mean(gain_grads * gain_grads, axis=-1, keepdims=True) + 1e-06
    )
    expert_grads, expert_stats_new, expert_new = shampoo(
        [expert_term], expert_stats, expert_roots, expert_master
    )
    attn_grads, attn_stats_new, attn_new = shampoo(attn_terms, attn_stats, attn_roots, attn_master)
    return (
        output,
        input_grad,
        gain_grads,
        new_gains,
        attn_grads,
        attn_stats_new,
        attn_new,
        expert_grads,
        expert_stats_new,
        expert_new,
    )


def solution(mesh):
    in_specs = (
        P(("expert", "shard"), None),
        P(("expert", "shard"), None),
        P(("expert", "shard")),
        P(("expert", "shard"), None),
        P(("expert", "shard"), None),
        P(),
        P(("expert", "shard"), None, None),
        P(("expert", "shard"), None, None, None),
        P(("expert", "shard"), None, None, None),
        P(),
        P(("expert", "shard"), None, None),
        P(("expert", "shard"), None, None, None),
        P(("expert", "shard"), None, None, None),
        P("expert", None),
    )
    out_specs = (
        P(("expert", "shard"), None),
        P(("expert", "shard"), None),
        P(),
        P(),
        P(("expert", "shard"), None, None),
        P(("expert", "shard"), None, None, None),
        P(("expert", "shard"), None, None),
        P(("expert", "shard"), None, None),
        P(("expert", "shard"), None, None, None),
        P(("expert", "shard"), None, None),
    )
    return jax.shard_map(
        per_device, mesh=mesh, in_specs=in_specs, out_specs=out_specs, check_vma=False
    )
```

time: 1390 us -> 703 us (0.51)
  local copies, waits for them, and re-layouts: 373 us -> 28.5 us
  matrix products: 295 us -> 0 us
  Pallas kernels: 0 us -> 286 us
  waiting for transfers between devices: 537 us -> 297 us
  other arithmetic: 91.5 us -> 22.9 us
  blocking collectives: 42.1 us -> 0 us
  starting transfers between devices: 27.1 us -> 48.3 us
    all_to_all x4 -> x0, waiting for transfers between devices: 356 us -> none  [the longest x1 197 us: per_device(): lax.all_to_all(produced[None], 'expert', split_axis=2, concat_axis=0, til...]
    dot_general x33 -> x0, matrix products: 295 us -> none  [the longest x1 25.3 us: expert_forward(): jnp.einsum('ecd,edf->ecf', rows_in, w_gateup, preferred_element_type=jnp....]
    pallas_call x0 -> x11, Pallas kernels: none -> 286 us  [the longest x4 87.1 us: expert_front(): pl.pallas_call(kernel, name='expert_front', grid=(EXP_DEV,), out_shape=(j...]
    ppermute x0 -> x44, waiting for transfers between devices: none -> 265 us  [the longest x30 148 us: swap(): lax.ppermute(array, 'expert', [(i, i ^ mask) for i in range(lax.axis_size...]
    all_gather x2 -> x1, waiting for transfers between devices: 181 us -> 31.8 us  [per_device(): lax.all_gather(expert_master.astype(BF16), 'shard', axis=0, tiled=True)]
    gather x4 -> x0, local copies, waits for them, and re-layouts: 84.4 us -> none  [the longest x2 38.2 us: natural_order(): return slotted[inverse]]
    broadcast_in_dim x2 -> x0, local copies, waits for them, and re-layouts: 75.3 us -> none  [the longest x1 37.7 us: per_device(): produced[None]]
    reshape x7 -> x1, local copies, waits for them, and re-layouts: 58.7 us -> 0.1 us  [gather_attention(): by_device = deal.reshape(groups, size, slots)]
  transfers between devices with their start and end apart: 8 -> 46, of which waited for: 5 -> 22; matrix products, arithmetic and copies ran while one was open for 41% -> 6% of each run, Pallas kernels for 0% -> 26%
where the time goes in v1:
time: 703 us; the launch traced here: 698 us
  waiting for transfers between devices  297 us (42%)
  Pallas kernels  286 us (41%)
  starting transfers between devices  48.3 us (7%)
  local copies, waits for them, and re-layouts  28.5 us (4%)
  other arithmetic  22.9 us (3%)
  between operations  15.5 us (2%)
    ppermute x30, waiting for transfers between devices, swap(): lax.ppermute(array, 'expert', [(i, i ^ mask) for i in range(lax.axis_size...  148 us
    ppermute x14, waiting for transfers between devices, move(): return lax.ppermute(array, 'shard', pairs)  117 us
    pallas_call x4, Pallas kernels, expert_front(): pl.pallas_call(kernel, name='expert_front', grid=(EXP_DEV,), out_shape=(j...  87.1 us
    pallas_call x1, Pallas kernels, expert_weight_grads(): pl.pallas_call(kernel, name='expert_weight_grads', grid=(EXP_DEV,), out_s...  54.2 us
    pallas_call x1, Pallas kernels, attention_back(): pl.pallas_call(kernel, name='attention_back', out_shape=(jax.ShapeDtypeSt...  50.8 us
    all_gather x1, waiting for transfers between devices, per_device(): lax.all_gather(expert_master.astype(BF16), 'shard', axis=0, tiled=True)  31.8 us
    ppermute x30, starting transfers between devices, swap(): lax.ppermute(array, 'expert', [(i, i ^ mask) for i in range(lax.axis_size...  29.1 us
    pallas_call x2, Pallas kernels, shampoo(): pl.pallas_call(kernel, name='shampoo', grid=(slots // many,), out_shape=(...  28.6 us
  transfers between devices with their start and end apart: 46, of which 22 were waited for; matrix products, arithmetic and copies ran while one was open for 6% of the time, Pallas kernels for 26%

profile of v1, /device:TPU:8, one launch (start us, length us, event | category | flops | bytes accessed | tf_op | source)
XLA Modules:
  0.0 698.1 jit_solution(5628438235105541562)
XLA Ops:
  7.2 4.2 convert_element_type.67
  11.5 1.1 copy-done.7
  12.6 1.6 collective-permute-start
  14.2 1.5 collective-permute-start.1
  15.7 1.6 collective-permute-start.3
  17.3 1.2 collective-permute-start.7
  18.5 1.8 collective-permute-start.11
  20.4 1.1 fusion.10
  22.2 22.5 %collective-permute-done.3 = bf16[12,128,128]{2,1,0:T(8,128)(2,1)S(1)} collective-permute-done((bf16[12,128,128]{2,1,0:T(8,128)(2,1)S(1)}, bf16[12,128,128]{2,1,0:T(8,128)(2,1)S(1)}, u32[]{:S(2)}, u32[]{:S(2)}) %collective-permute-start.3) | collective-permute-done | bytes 393248 | tf_op jit(solution)/shard_map/ppermute | solution.py:670
  46.7 40.7 %collective-permute-done.7 = bf16[12,128,128]{2,1,0:T(8,128)(2,1)S(1)} collective-permute-done((bf16[12,128,128]{2,1,0:T(8,128)(2,1)S(1)}, bf16[12,128,128]{2,1,0:T(8,128)(2,1)S(1)}, u32[]{:S(2)}, u32[]{:S(2)}) %collective-permute-start.7) | collective-permute-done | bytes 393248 | tf_op jit(solution)/shard_map/ppermute | solution.py:670
  88.1 6.2 collective-permute-done.11
  96.9 1.5 collective-permute-start.12
  98.4 1.5 collective-permute-start.13
  101.1 5.2 collective-permute-done.8
  107.6 7.1 %collective-permute-done.12 = bf16[12,128,128]{2,1,0:T(8,128)(2,1)S(1)} collective-permute-done((bf16[12,128,128]{2,1,0:T(8,128)(2,1)S(1)}, bf16[12,128,128]{2,1,0:T(8,128)(2,1)S(1)}, u32[]{:S(2)}, u32[]{:S(2)}) %collective-permute-start.12) | collective-permute-done | bytes 393248 | tf_op jit(solution)/shard_map/ppermute | solution.py:756
  118.6 4.5 collective-permute-done.6
  125.2 5.2 collective-permute-done.14
  133.3 1.1 pad_maximum_fusion.4
  135.5 2.4 collective-permute-start.21
  138.0 26.7 %attention_front.1 = (bf16[384,1536]{1,0:T(8,128)(2,1)}, f32[384,1536]{1,0:T(8,128)}, bf16[384,1536]{1,0:T(8,128)(2,1)}, bf16[24,384,64]{2,1,0:T(8,128)(2,1)}, b...) custom-call(s32[1]{0:T(128)} %copy.33.length_ref, ...), custom_call_target="tpu_custom_call" | custom-call | flops 5737807872 | bytes 25165824 | tf_op jit(solution)/shard_map/attention_front/pallas_call | solution.py:453
  165.3 4.9 scatter_custom_fusion.inverse_ref
  170.7 31.8 %all-gather.2.cloned.1.call-done.blocks_ref = bf16[576,128,128]{2,1,0:T(8,128)(2,1)} async-done(((bf16[72,128,128]{2,1,0:T(8,128)(2,1)}), bf16[576,128,128]{2,1,0:T(8,128)(2,1)}) %all-gather.2.cloned.1.call-update) | async-done | bytes 18874384 | tf_op jit(solution)/shard_map/all_gather | solution.py:779
  202.5 17.2 %assemble_experts.1 = (bf16[4,1536,1024]{2,1,0:T(8,128)(2,1)}, bf16[4,512,1536]{2,1,0:T(8,128)(2,1)}) custom-call(s32[576]{0:T(1024)} %scatter_custom_fusion.inverse_ref, bf16[576,128,128]{2,1,0:T(8,128)(2,1)} %all-gather.2.cloned.1.call-done.blocks_ref), custom_call_target="tpu_custom_call" | custom-call | bytes 37748736 | tf_op jit(solution)/shard_map/assemble_experts/pallas_call | solution.py:109
  219.7 19.2 %expert_front.4 = (bf16[4,384,512]{2,1,0:T(8,128)(2,1)}, bf16[4,384,1024]{2,1,0:T(8,128)(2,1)}, bf16[384,1536]{1,0:T(8,128)(2,1)}) custom-call(s32[1]{0:T(128)} %bitcast.32.group_ref, bf16[384,1536]{1,0:T(8,128)(2,1)} %get-tuple-element.46.rows_ref.refs_0_, bf16[384,1664]{1,0:T(8,128)(2,1)} %copy-done.10, ...), custom_call_target="tpu_custom_call" | custom-call | flops 12079595520 | bytes 18874368 | tf_op jit(solution)/shard_map/expert_front/pallas_call | solution.py:162
  239.5 19.2 %expert_front.5 = (bf16[4,384,512]{2,1,0:T(8,128)(2,1)}, bf16[4,384,1024]{2,1,0:T(8,128)(2,1)}, bf16[384,1536]{1,0:T(8,128)(2,1)}) custom-call(s32[1]{0:T(128)} %bitcast.32.group_ref, bf16[384,1536]{1,0:T(8,128)(2,1)} %collective-permute-done.22.rows_ref.refs_1_, bf16[384,1664]{1,0:T(8,128)(2,1)} %collective-permute-done.19.packed_ref.refs_1_.refs_5_, ...), custom_call_target="tpu_custom_call" | custom-call | flops 12079595520 | bytes 18874368 | tf_op jit(solution)/shard_map/expert_front/pallas_call | solution.py:162
  259.8 19.2 %expert_front.6 = (bf16[4,384,512]{2,1,0:T(8,128)(2,1)}, bf16[4,384,1024]{2,1,0:T(8,128)(2,1)}, bf16[384,1536]{1,0:T(8,128)(2,1)}) custom-call(s32[1]{0:T(128)} %bitcast.32.group_ref, bf16[384,1536]{1,0:T(8,128)(2,1)} %collective-permute-done.23.rows_ref.refs_2_, bf16[384,1664]{1,0:T(8,128)(2,1)} %copy-done.23, ...), custom_call_target="tpu_custom_call" | custom-call | flops 12079595520 | bytes 18874368 | tf_op jit(solution)/shard_map/expert_front/pallas_call | solution.py:162
  279.0 29.5 %expert_front.7 = (bf16[4,384,512]{2,1,0:T(8,128)(2,1)}, bf16[4,384,1024]{2,1,0:T(8,128)(2,1)}, bf16[384,1536]{1,0:T(8,128)(2,1)}) custom-call(s32[1]{0:T(128)} %bitcast.32.group_ref, bf16[384,1536]{1,0:T(8,128)(2,1)} %collective-permute-done.24.rows_ref.refs_3_, bf16[384,1664]{1,0:T(8,128)(2,1)} %collective-permute-done.21.packed_ref.refs_3_.refs_7_, ...), custom_call_target="tpu_custom_call" | custom-call | flops 12079595520 | bytes 18874368 | tf_op jit(solution)/shard_map/expert_front/pallas_call | solution.py:162
  308.5 54.2 %expert_weight_grads.1 = bf16[576,128,128]{2,1,0:T(8,128)(2,1)} custom-call(s32[1]{0:T(128)} %bitcast.32.group_ref, s32[576]{0:T(1024)} %scatter_custom_fusion.inverse_ref, bf16[384,1536]{1,0:T(8,128)(2,1)} %get-tuple-element.46.rows_ref.refs_0_, bf16[384,1536]{1,0:T(8,128)(2,1)} %collective-permute-done.22.rows_ref.refs_1_, ...), custom_call_target="tpu_custom_call" | custom-call | flops 28991029248 | bytes 37748736 | tf_op jit(solution)/shard_map/expert_weight_grads/pallas_call | solution.py:258
  362.8 1.2 copy-done.24
  364.0 1.3 collective-permute-start.28
  365.4 1.5 collective-permute-start.29
  367.5 3.1 scatter_custom_fusion.1
  371.3 21.7 %collective-permute-done.28.refs_1_ = bf16[384,1536]{1,0:T(8,128)(2,1)} collective-permute-done((bf16[384,1536]{1,0:T(8,128)(2,1)S(1)}, bf16[384,1536]{1,0:T(8,128)(2,1)}, u32[]{:S(2)}, u32[]{:S(2)}) %collective-permute-start.28) | collective-permute-done | bytes 1179680 | tf_op jit(solution)/shard_map/ppermute | solution.py:756
  393.0 25.1 %collective-permute-done.29.refs_2_ = bf16[384,1536]{1,0:T(8,128)(2,1)} collective-permute-done((bf16[384,1536]{1,0:T(8,128)(2,1)S(1)}, bf16[384,1536]{1,0:T(8,128)(2,1)}, u32[]{:S(2)}, u32[]{:S(2)}) %collective-permute-start.29) | collective-permute-done | bytes 1179680 | tf_op jit(solution)/shard_map/ppermute | solution.py:756
  418.1 50.8 %attention_back.1 = (f32[384,1536]{1,0:T(8,128)}, f32[2,1536]{1,0:T(2,128)}, bf16[192,128,128]{2,1,0:T(8,128)(2,1)}, bf16[192,128,128]{2,1,0:T(8,128)(2,1)}) custom-call(s32[1]{0:T(128)} %copy.33.length_ref, s32[384]{0:T(512)} %fusion.31.position_ref, bf16[384,1536]{1,0:T(8,128)(2,1)} %tokens_ref.3, bf16[384,1664]{1,0:T(8,128)(2,1)} %copy-done.10, ...), custom_call_target="tpu_custom_call" | custom-call | flops 11928600576 | bytes 25165824 | tf_op jit(solution)/shard_map/attention_back/pallas_call | solution.py:584
  469.1 10.8 %collective-permute-done.36 = bf16[192,128,128]{2,1,0:T(8,128)(2,1)S(1)} collective-permute-done((bf16[192,128,128]{2,1,0:T(8,128)(2,1)}, bf16[192,128,128]{2,1,0:T(8,128)(2,1)S(1)}, u32[]{:S(2)}, u32[]{:S(2)}) %collective-permute-start.36) | collective-permute-done | bytes 6291488 | tf_op jit(solution)/shard_map/ppermute | solution.py:670
  479.8 2.7 copy-done
  482.5 7.7 %add_convert_fusion = bf16[192,128,128]{2,1,0:T(8,128)(2,1)S(1)} fusion(bf16[192,128,128]{2,1,0:T(8,128)(2,1)} %copy-done, bf16[192,128,128]{2,1,0:T(8,128)(2,1)} %get-tuple-element.68), kind=kLoop, calls=%fused_computation.2 | loop fusion | flops 12582912 | bytes 18874368 | tf_op jit(solution)/shard_map/convert_element_type | solution.py:722
  490.2 2.8 slice_bitcast_fusion.3
  493.1 1.5 collective-permute-start.37
  494.6 21.1 %expert_outputs.1 = (bf16[384,1536]{1,0:T(8,128)(2,1)}, bf16[384,1536]{1,0:T(8,128)(2,1)}, bf16[384,1536]{1,0:T(8,128)(2,1)}, bf16[384,1536]{1,0:T(8,128)(2,1)}) custom-call(s32[1]{0:T(128)} %bitcast.32.group_ref, bf16[384,1664]{1,0:T(8,128)(2,1)} %copy-done.10, bf16[384,1664]{1,0:T(8,128)(2,1)} %collective-permute-done.19.packed_ref.refs_1_.refs_5_, ...), custom_call_target="tpu_custom_call" | custom-call | flops 9663676416 | bytes 12582912 | tf_op jit(solution)/shard_map/expert_outputs/pallas_call | solution.py:309
  515.7 1.6 collective-permute-start.27
  517.8 1.5 collective-permute-start.25
  519.3 1.2 collective-permute-done.31
  520.4 4.3 collective-permute-start.32
  524.7 1.9 collective-permute-done.32
  526.7 2.5 collective-permute-start.33
  529.4 2.4 collective-permute-done.33
  532.7 1.5 collective-permute-start.34
  534.2 2.3 add_convert_fusion.2
  536.6 20.1 %collective-permute-done.27 = bf16[384,1536]{1,0:T(8,128)(2,1)S(1)} collective-permute-done((bf16[384,1536]{1,0:T(8,128)(2,1)}, bf16[384,1536]{1,0:T(8,128)(2,1)S(1)}, u32[]{:S(2)}, u32[]{:S(2)}) %collective-permute-start.27) | collective-permute-done | bytes 1179680 | tf_op jit(solution)/shard_map/ppermute | solution.py:756
  557.2 14.4 %collective-permute-done.26 = bf16[384,1536]{1,0:T(8,128)(2,1)S(1)} collective-permute-done((bf16[384,1536]{1,0:T(8,128)(2,1)}, bf16[384,1536]{1,0:T(8,128)(2,1)S(1)}, u32[]{:S(2)}, u32[]{:S(2)}) %collective-permute-start.26) | collective-permute-done | bytes 1179680 | tf_op jit(solution)/shard_map/ppermute | solution.py:756
  571.6 8.6 %collective-permute-done.25 = bf16[384,1536]{1,0:T(8,128)(2,1)S(1)} collective-permute-done((bf16[384,1536]{1,0:T(8,128)(2,1)}, bf16[384,1536]{1,0:T(8,128)(2,1)S(1)}, u32[]{:S(2)}, u32[]{:S(2)}) %collective-permute-start.25) | collective-permute-done | bytes 1179680 | tf_op jit(solution)/shard_map/ppermute | solution.py:756
  580.3 1.8 add_convert_fusion.3
  582.1 1.6 collective-permute-start.35
  583.7 21.6 %collective-permute-done.40 = bf16[48,128,128]{2,1,0:T(8,128)(2,1)S(1)} collective-permute-done((bf16[48,128,128]{2,1,0:T(8,128)(2,1)S(1)}, bf16[48,128,128]{2,1,0:T(8,128)(2,1)S(1)}, u32[]{:S(2)}, u32[]{:S(2)}) %collective-permute-start.40) | collective-permute-done | bytes 1572896 | tf_op jit(solution)/shard_map/ppermute | solution.py:756
  606.3 14.7 %collective-permute-done.35 = f32[2,1536]{1,0:T(2,128)S(1)} collective-permute-done((f32[2,1536]{1,0:T(2,128)S(1)}, f32[2,1536]{1,0:T(2,128)S(1)}, u32[]{:S(2)}, u32[]{:S(2)}) %collective-permute-start.35) | collective-permute-done | bytes 12320 | tf_op jit(solution)/shard_map/ppermute | solution.py:756
  622.2 1.4 collective-permute-start.39
  623.9 5.7 collective-permute-start.42
  630.2 6.6 collective-permute-done.39.refs_1_
  636.8 19.2 %collective-permute-done.42.refs_2_ = bf16[12,128,128]{2,1,0:T(8,128)(2,1)S(1)} collective-permute-done((bf16[12,128,128]{2,1,0:T(8,128)(2,1)S(1)}, bf16[12,128,128]{2,1,0:T(8,128)(2,1)S(1)}, u32[]{:S(2)}, u32[]{:S(2)}) %collective-permute-start.42) | collective-permute-done | bytes 393248 | tf_op jit(solution)/shard_map/ppermute | solution.py:670
  656.1 5.6 collective-permute-done.43.refs_3_
  662.5 5.8 shampoo.2
  668.2 22.8 %shampoo.3 = (f32[72,128,128]{2,1,0:T(8,128)}, f32[72,2,128,128]{3,2,1,0:T(8,128)}, f32[72,128,128]{2,1,0:T(8,128)}) custom-call(bf16[72,128,128]{2,1,0:T(8,128)(2,1)} %reduce-scatter.2.cloned.1.call-done.refs_0_, f32[72,2,128,128]{3,2,1,0:T(8,128)} %refs_1_.1, f32[72,2,128,128]{3,2,1,0:T(8,128)} %refs_2_.1, f32[72,128,128]{2,1,0:T(8,128)} %refs_3_.1), custom_call_target="tpu_custom_call" | custom-call | flops 2113929216 | bytes 44826624 | tf_op jit(solution)/shard_map/shampoo/pallas_call | solution.py:649
  (150 shorter events, 28.5 us)
Async XLA Ops:
  7.2 195.3 %all-gather.2.cloned.1.call-start = ((), (), s32[]{:S(2)}) async-start(), calls=%async_computation.1 | async-start | bytes 21233664 | tf_op jit(solution)/shard_map/all_gather | solution.py:779
  11.4 8.9 %copy-start.18 = (s32[384,8]{0,1:T(8,128)S(1)}, s32[384,8]{0,1:T(8,128)}, u32[]{:S(2)}) copy-start(s32[384,8]{0,1:T(8,128)} %param.17) | copy-start | bytes 36868
  11.4 8.9 %copy-start.17 = (bf16[384,8]{0,1:T(8,128)(2,1)S(1)}, bf16[384,8]{0,1:T(8,128)(2,1)}, u32[]{:S(2)}) copy-start(bf16[384,8]{0,1:T(8,128)(2,1)} %param.18) | copy-start | bytes 18436
  11.5 656.8 %reduce-scatter.2.cloned.1.call-start = ((), (), s32[]{:S(2)}) async-start(), calls=%async_computation.2 | async-start | bytes 21233664 | tf_op jit(solution)/shard_map/reduce_scatter | solution.py:816
  12.6 32.7 %collective-permute-start = (bf16[12,128,128]{2,1,0:T(8,128)(2,1)S(1)}, bf16[12,128,128]{2,1,0:T(8,128)(2,1)S(1)}, u32[]{:S(2)}, u32[]{:S(2)}) collective-permute-start(bf16[12,128,128]{2,1,0:T(8,128)(2,1)S(1)} %convert_element_type.66), channel_id=1, source_target_pairs={{0,8},{8,0},{16,24},{24,16},{1,9},{9,1},{17,25},{25,17},{2,10},{10... | collective-permute-start | bytes 1179656 | tf_op jit(solution)/shard_map/ppermute | solution.py:756
  14.2 82.7 %collective-permute-start.1 = (bf16[12,128,128]{2,1,0:T(8,128)(2,1)S(1)}, bf16[12,128,128]{2,1,0:T(8,128)(2,1)S(1)}, u32[]{:S(2)}, u32[]{:S(2)}) collective-permute-start(bf16[12,128,128]{2,1,0:T(8,128)(2,1)S(1)} %convert_element_type.66), channel_id=1, source_target_pairs={{0,16},{8,24},{16,0},{24,8},{1,17},{9,25},{17,1},{25,9},{2,18},{10... | collective-permute-start | bytes 1179656 | tf_op jit(solution)/shard_map/ppermute | solution.py:756
  15.7 29.0 %collective-permute-start.3 = (bf16[12,128,128]{2,1,0:T(8,128)(2,1)S(1)}, bf16[12,128,128]{2,1,0:T(8,128)(2,1)S(1)}, u32[]{:S(2)}, u32[]{:S(2)}) collective-permute-start(bf16[12,128,128]{2,1,0:T(8,128)(2,1)S(1)} %convert_element_type.66), channel_id=1, source_target_pairs={{0,2},{1,3},{2,4},{3,5},{4,6},{5,7},{6,0},{7,1},{8,10},{9,11},{10,... | collective-permute-start | bytes 1179656 | tf_op jit(solution)/shard_map/ppermute | solution.py:670
  17.3 70.1 %collective-permute-start.7 = (bf16[12,128,128]{2,1,0:T(8,128)(2,1)S(1)}, bf16[12,128,128]{2,1,0:T(8,128)(2,1)S(1)}, u32[]{:S(2)}, u32[]{:S(2)}) collective-permute-start(bf16[12,128,128]{2,1,0:T(8,128)(2,1)S(1)} %convert_element_type.66), channel_id=1, source_target_pairs={{0,4},{1,5},{2,6},{3,7},{4,0},{5,1},{6,2},{7,3},{8,12},{9,13},{10,... | collective-permute-start | bytes 1179656 | tf_op jit(solution)/shard_map/ppermute | solution.py:670
  18.5 75.8 %collective-permute-start.11 = (bf16[12,128,128]{2,1,0:T(8,128)(2,1)S(1)}, bf16[12,128,128]{2,1,0:T(8,128)(2,1)S(1)}, u32[]{:S(2)}, u32[]{:S(2)}) collective-permute-start(bf16[12,128,128]{2,1,0:T(8,128)(2,1)S(1)} %convert_element_type.66), channel_id=1, source_target_pairs={{0,6},{1,7},{2,0},{3,1},{4,2},{5,3},{6,4},{7,5},{8,14},{9,15},{10,... | collective-permute-start | bytes 1179656 | tf_op jit(solution)/shard_map/ppermute | solution.py:670
  44.7 51.0 %collective-permute-start.4 = (bf16[12,128,128]{2,1,0:T(8,128)(2,1)S(1)}, bf16[12,128,128]{2,1,0:T(8,128)(2,1)S(1)}, u32[]{:S(2)}, u32[]{:S(2)}) collective-permute-start(bf16[12,128,128]{2,1,0:T(8,128)(2,1)S(1)} %collective-permute-done.3), channel_id=1, source_target_pairs={{0,8},{8,0},{16,24},{24,16},{1,9},{9,1},{17,25},{25,17},{2,10},{10... | collective-permute-start | bytes 1179656 | tf_op jit(solution)/shard_map/ppermute | solution.py:756
  45.3 53.1 %collective-permute-start.2 = (bf16[12,128,128]{2,1,0:T(8,128)(2,1)S(1)}, bf16[12,128,128]{2,1,0:T(8,128)(2,1)S(1)}, u32[]{:S(2)}, u32[]{:S(2)}) collective-permute-start(bf16[12,128,128]{2,1,0:T(8,128)(2,1)S(1)} %collective-permute-done), channel_id=1, source_target_pairs={{0,16},{8,24},{16,0},{24,8},{1,17},{9,25},{17,1},{25,9},{2,18},{10... | collective-permute-start | bytes 1179656 | tf_op jit(solution)/shard_map/ppermute | solution.py:756
  87.3 12.8 %collective-permute-start.5 = (bf16[12,128,128]{2,1,0:T(8,128)(2,1)S(1)}, bf16[12,128,128]{2,1,0:T(8,128)(2,1)S(1)}, u32[]{:S(2)}, u32[]{:S(2)}) collective-permute-start(bf16[12,128,128]{2,1,0:T(8,128)(2,1)S(1)} %collective-permute-done.3), channel_id=1, source_target_pairs={{0,16},{8,24},{16,0},{24,8},{1,17},{9,25},{17,1},{25,9},{2,18},{10... | collective-permute-start | bytes 1179656 | tf_op jit(solution)/shard_map/ppermute | solution.py:756
  94.3 12.0 %collective-permute-start.8 = (bf16[12,128,128]{2,1,0:T(8,128)(2,1)S(1)}, bf16[12,128,128]{2,1,0:T(8,128)(2,1)S(1)}, u32[]{:S(2)}, u32[]{:S(2)}) collective-permute-start(bf16[12,128,128]{2,1,0:T(8,128)(2,1)S(1)} %collective-permute-done.7), channel_id=1, source_target_pairs={{0,8},{8,0},{16,24},{24,16},{1,9},{9,1},{17,25},{25,17},{2,10},{10... | collective-permute-start | bytes 1179656 | tf_op jit(solution)/shard_map/ppermute | solution.py:756
  95.6 22.2 %collective-permute-start.9 = (bf16[12,128,128]{2,1,0:T(8,128)(2,1)S(1)}, bf16[12,128,128]{2,1,0:T(8,128)(2,1)S(1)}, u32[]{:S(2)}, u32[]{:S(2)}) collective-permute-start(bf16[12,128,128]{2,1,0:T(8,128)(2,1)S(1)} %collective-permute-done.7), channel_id=1, source_target_pairs={{0,16},{8,24},{16,0},{24,8},{1,17},{9,25},{17,1},{25,9},{2,18},{10... | collective-permute-start | bytes 1179656 | tf_op jit(solution)/shard_map/ppermute | solution.py:756
  96.9 17.8 %collective-permute-start.12 = (bf16[12,128,128]{2,1,0:T(8,128)(2,1)S(1)}, bf16[12,128,128]{2,1,0:T(8,128)(2,1)S(1)}, u32[]{:S(2)}, u32[]{:S(2)}) collective-permute-start(bf16[12,128,128]{2,1,0:T(8,128)(2,1)S(1)} %collective-permute-done.11), channel_id=1, source_target_pairs={{0,8},{8,0},{16,24},{24,16},{1,9},{9,1},{17,25},{25,17},{2,10},{10... | collective-permute-start | bytes 1179656 | tf_op jit(solution)/shard_map/ppermute | solution.py:756
  98.4 16.8 %collective-permute-start.13 = (bf16[12,128,128]{2,1,0:T(8,128)(2,1)S(1)}, bf16[12,128,128]{2,1,0:T(8,128)(2,1)S(1)}, u32[]{:S(2)}, u32[]{:S(2)}) collective-permute-start(bf16[12,128,128]{2,1,0:T(8,128)(2,1)S(1)} %collective-permute-done.11), channel_id=1, source_target_pairs={{0,16},{8,24},{16,0},{24,8},{1,17},{9,25},{17,1},{25,9},{2,18},{10... | collective-permute-start | bytes 1179656 | tf_op jit(solution)/shard_map/ppermute | solution.py:756
  100.1 17.8 %copy-start.9 = (bf16[48,128,128]{2,1,0:T(8,128)(2,1)}, bf16[48,128,128]{2,1,0:T(8,128)(2,1)S(1)}, u32[]{:S(2)}) copy-start(bf16[48,128,128]{2,1,0:T(8,128)(2,1)S(1)} %pad_maximum_fusion.refs_0_) | copy-start | bytes 4718596
  100.1 34.9 %collective-permute-start.15 = (bf16[48,128,128]{2,1,0:T(8,128)(2,1)S(1)}, bf16[48,128,128]{2,1,0:T(8,128)(2,1)}, u32[]{:S(2)}, u32[]{:S(2)}) collective-permute-start(bf16[48,128,128]{2,1,0:T(8,128)(2,1)S(1)} %pad_maximum_fusion.refs_0_), channel_id=1, source_target_pairs={{0,1},{1,0},{2,3},{3,2},{4,5},{5,4},{6,7},{7,6},{8,9},{9,8},{10,11... | collective-permute-start | bytes 4718600 | tf_op jit(solution)/shard_map/ppermute | solution.py:670
  106.3 16.9 %collective-permute-start.6 = (bf16[12,128,128]{2,1,0:T(8,128)(2,1)S(1)}, bf16[12,128,128]{2,1,0:T(8,128)(2,1)S(1)}, u32[]{:S(2)}, u32[]{:S(2)}) collective-permute-start(bf16[12,128,128]{2,1,0:T(8,128)(2,1)S(1)} %collective-permute-done.5), channel_id=1, source_target_pairs={{0,8},{8,0},{16,24},{24,16},{1,9},{9,1},{17,25},{25,17},{2,10},{10... | collective-permute-start | bytes 1179656 | tf_op jit(solution)/shard_map/ppermute | solution.py:756
  114.7 9.2 %collective-permute-start.10 = (bf16[12,128,128]{2,1,0:T(8,128)(2,1)S(1)}, bf16[12,128,128]{2,1,0:T(8,128)(2,1)S(1)}, u32[]{:S(2)}, u32[]{:S(2)}) collective-permute-start(bf16[12,128,128]{2,1,0:T(8,128)(2,1)S(1)} %collective-permute-done.8), channel_id=1, source_target_pairs={{0,16},{8,24},{16,0},{24,8},{1,17},{9,25},{17,1},{25,9},{2,18},{10... | collective-permute-start | bytes 1179656 | tf_op jit(solution)/shard_map/ppermute | solution.py:756
  115.3 15.1 %collective-permute-start.14 = (bf16[12,128,128]{2,1,0:T(8,128)(2,1)S(1)}, bf16[12,128,128]{2,1,0:T(8,128)(2,1)S(1)}, u32[]{:S(2)}, u32[]{:S(2)}) collective-permute-start(bf16[12,128,128]{2,1,0:T(8,128)(2,1)S(1)} %collective-permute-done.13), channel_id=1, source_target_pairs={{0,8},{8,0},{16,24},{24,16},{1,9},{9,1},{17,25},{25,17},{2,10},{10... | collective-permute-start | bytes 1179656 | tf_op jit(solution)/shard_map/ppermute | solution.py:756
  117.9 13.3 %copy-start.11 = (bf16[384,1536]{1,0:T(8,128)(2,1)S(1)}, bf16[384,1536]{1,0:T(8,128)(2,1)}, u32[]{:S(2)}) copy-start(bf16[384,1536]{1,0:T(8,128)(2,1)} %param.15) | copy-start | bytes 3538948
  123.9 11.6 %collective-permute-start.16 = (bf16[48,128,128]{2,1,0:T(8,128)(2,1)}, bf16[48,128,128]{2,1,0:T(8,128)(2,1)}, u32[]{:S(2)}, u32[]{:S(2)}) collective-permute-start(bf16[48,128,128]{2,1,0:T(8,128)(2,1)} %constant_dynamic-update-slice_fusion.refs_1_), channel_id=1, source_target_pairs={{0,1},{1,0},{2,3},{3,2},{4,5},{5,4},{6,7},{7,6},{8,9},{9,8},{10,11... | collective-permute-start | bytes 4718600 | tf_op jit(solution)/shard_map/ppermute | solution.py:670
  124.7 13.2 %collective-permute-start.17 = (bf16[48,128,128]{2,1,0:T(8,128)(2,1)}, bf16[48,128,128]{2,1,0:T(8,128)(2,1)}, u32[]{:S(2)}, u32[]{:S(2)}) collective-permute-start(bf16[48,128,128]{2,1,0:T(8,128)(2,1)} %constant_dynamic-update-slice_fusion.4.refs_2_), channel_id=1, source_target_pairs={{0,1},{1,0},{2,3},{3,2},{4,5},{5,4},{6,7},{7,6},{8,9},{9,8},{10,11... | collective-permute-start | bytes 4718600 | tf_op jit(solution)/shard_map/ppermute | solution.py:670
  131.2 6.8 collective-permute-start.18
  131.5 33.1 %copy-start.10 = (bf16[384,1664]{1,0:T(8,128)(2,1)}, bf16[384,1664]{1,0:T(8,128)(2,1)S(1)}, u32[]{:S(2)}) copy-start(bf16[384,1664]{1,0:T(8,128)(2,1)S(1)} %pad_maximum_fusion.3.packed_ref.refs_0_.refs_4_) | copy-start | bytes 3833860
  131.5 107.5 %collective-permute-start.19 = (bf16[384,1664]{1,0:T(8,128)(2,1)S(1)}, bf16[384,1664]{1,0:T(8,128)(2,1)}, u32[]{:S(2)}, u32[]{:S(2)}) collective-permute-start(bf16[384,1664]{1,0:T(8,128)(2,1)S(1)} %pad_maximum_fusion.3.packed_ref.refs_0_.refs_4_), channel_id=1, source_target_pairs={{0,8},{8,0},{16,24},{24,16},{1,9},{9,1},{17,25},{25,17},{2,10},{10... | collective-permute-start | bytes 3833864 | tf_op jit(solution)/shard_map/ppermute | solution.py:756
  135.0 123.7 %collective-permute-start.20 = (bf16[384,1664]{1,0:T(8,128)(2,1)S(1)}, bf16[384,1664]{1,0:T(8,128)(2,1)S(1)}, u32[]{:S(2)}, u32[]{:S(2)}) collective-permute-start(bf16[384,1664]{1,0:T(8,128)(2,1)S(1)} %pad_maximum_fusion.3.packed_ref.refs_0_.refs_4_), channel_id=1, source_target_pairs={{0,16},{8,24},{16,0},{24,8},{1,17},{9,25},{17,1},{25,9},{2,18},{10... | collective-permute-start | bytes 3833864 | tf_op jit(solution)/shard_map/ppermute | solution.py:756
  135.5 143.5 %collective-permute-start.21 = (bf16[384,1664]{1,0:T(8,128)(2,1)S(1)}, bf16[384,1664]{1,0:T(8,128)(2,1)}, u32[]{:S(2)}, u32[]{:S(2)}) collective-permute-start(bf16[384,1664]{1,0:T(8,128)(2,1)S(1)} %pad_maximum_fusion.3.packed_ref.refs_0_.refs_4_), channel_id=1, source_target_pairs={{0,24},{8,16},{16,8},{24,0},{1,25},{9,17},{17,9},{25,1},{2,26},{10... | collective-permute-start | bytes 3833864 | tf_op jit(solution)/shard_map/ppermute | solution.py:756
  137.9 27.3 %copy-start.22 = (s32[1,576]{1,0:T(1,128)S(1)}, s32[1,576]{1,0:T(1,128)}, u32[]{:S(2)}) copy-start(s32[1,576]{1,0:T(1,128)} %param.27) | copy-start | bytes 6916
  164.6 74.9 %collective-permute-start.22 = (bf16[384,1536]{1,0:T(8,128)(2,1)}, bf16[384,1536]{1,0:T(8,128)(2,1)}, u32[]{:S(2)}, u32[]{:S(2)}) collective-permute-start(bf16[384,1536]{1,0:T(8,128)(2,1)} %get-tuple-element.46.rows_ref.refs_0_), channel_id=1, source_target_pairs={{0,8},{8,0},{16,24},{24,16},{1,9},{9,1},{17,25},{25,17},{2,10},{10... | collective-permute-start | bytes 3538952 | tf_op jit(solution)/shard_map/ppermute | solution.py:756
  170.2 88.5 %collective-permute-start.23 = (bf16[384,1536]{1,0:T(8,128)(2,1)}, bf16[384,1536]{1,0:T(8,128)(2,1)}, u32[]{:S(2)}, u32[]{:S(2)}) collective-permute-start(bf16[384,1536]{1,0:T(8,128)(2,1)} %get-tuple-element.46.rows_ref.refs_0_), channel_id=1, source_target_pairs={{0,16},{8,24},{16,0},{24,8},{1,17},{9,25},{17,1},{25,9},{2,18},{10... | collective-permute-start | bytes 3538952 | tf_op jit(solution)/shard_map/ppermute | solution.py:756
  238.9 40.1 %collective-permute-start.24 = (bf16[384,1536]{1,0:T(8,128)(2,1)}, bf16[384,1536]{1,0:T(8,128)(2,1)}, u32[]{:S(2)}, u32[]{:S(2)}) collective-permute-start(bf16[384,1536]{1,0:T(8,128)(2,1)} %get-tuple-element.46.rows_ref.refs_0_), channel_id=1, source_target_pairs={{0,24},{8,16},{16,8},{24,0},{1,25},{9,17},{17,9},{25,1},{2,26},{10... | collective-permute-start | bytes 3538952 | tf_op jit(solution)/shard_map/ppermute | solution.py:756
  364.0 29.0 %collective-permute-start.28 = (bf16[384,1536]{1,0:T(8,128)(2,1)S(1)}, bf16[384,1536]{1,0:T(8,128)(2,1)}, u32[]{:S(2)}, u32[]{:S(2)}) collective-permute-start(bf16[384,1536]{1,0:T(8,128)(2,1)S(1)} %copy-done.24), channel_id=1, source_target_pairs={{0,8},{8,0},{16,24},{24,16},{1,9},{9,1},{17,25},{25,17},{2,10},{10... | collective-permute-start | bytes 3538952 | tf_op jit(solution)/shard_map/ppermute | solution.py:756
  365.4 52.8 %collective-permute-start.29 = (bf16[384,1536]{1,0:T(8,128)(2,1)S(1)}, bf16[384,1536]{1,0:T(8,128)(2,1)}, u32[]{:S(2)}, u32[]{:S(2)}) collective-permute-start(bf16[384,1536]{1,0:T(8,128)(2,1)S(1)} %copy-done.25), channel_id=1, source_target_pairs={{0,16},{8,24},{16,0},{24,8},{1,17},{9,25},{17,1},{25,9},{2,18},{10... | collective-permute-start | bytes 3538952 | tf_op jit(solution)/shard_map/ppermute | solution.py:756
  366.9 51.3 %collective-permute-start.30 = (bf16[384,1536]{1,0:T(8,128)(2,1)S(1)}, bf16[384,1536]{1,0:T(8,128)(2,1)}, u32[]{:S(2)}, u32[]{:S(2)}) collective-permute-start(bf16[384,1536]{1,0:T(8,128)(2,1)S(1)} %copy-done.26), channel_id=1, source_target_pairs={{0,24},{8,16},{16,8},{24,0},{1,25},{9,17},{17,9},{25,1},{2,26},{10... | collective-permute-start | bytes 3538952 | tf_op jit(solution)/shard_map/ppermute | solution.py:756
  469.0 10.9 %collective-permute-start.36 = (bf16[192,128,128]{2,1,0:T(8,128)(2,1)}, bf16[192,128,128]{2,1,0:T(8,128)(2,1)S(1)}, u32[]{:S(2)}, u32[]{:S(2)}) collective-permute-start(bf16[192,128,128]{2,1,0:T(8,128)(2,1)} %get-tuple-element.69), channel_id=1, source_target_pairs={{0,1},{1,0},{2,3},{3,2},{4,5},{5,4},{6,7},{7,6},{8,9},{9,8},{10,11... | collective-permute-start | bytes 18874376 | tf_op jit(solution)/shard_map/ppermute | solution.py:670
  493.1 26.2 %copy-start.20 = (f32[2,1536]{1,0:T(2,128)S(1)}, f32[2,1536]{1,0:T(2,128)}, u32[]{:S(2)}) copy-start(f32[2,1536]{1,0:T(2,128)} %get-tuple-element.67) | copy-start | bytes 36868
  493.1 36.1 %copy-start.5 = (bf16[24,128,128]{2,1,0:T(8,128)(2,1)S(1)}, bf16[24,128,128]{2,1,0:T(8,128)(2,1)}, u32[]{:S(2)}) copy-start(bf16[24,128,128]{2,1,0:T(8,128)(2,1)} %get-tuple-element.99) | copy-start | bytes 2359300
  493.1 36.1 %copy-start.6 = (bf16[24,128,128]{2,1,0:T(8,128)(2,1)S(1)}, bf16[24,128,128]{2,1,0:T(8,128)(2,1)}, u32[]{:S(2)}) copy-start(bf16[24,128,128]{2,1,0:T(8,128)(2,1)} %get-tuple-element.100) | copy-start | bytes 2359300
  493.1 39.6 %collective-permute-start.37 = (bf16[48,128,128]{2,1,0:T(8,128)(2,1)S(1)}, bf16[48,128,128]{2,1,0:T(8,128)(2,1)}, u32[]{:S(2)}, u32[]{:S(2)}) collective-permute-start(bf16[48,128,128]{2,1,0:T(8,128)(2,1)S(1)} %pad_maximum_fusion.1), channel_id=1, source_target_pairs={{0,8},{8,0},{16,24},{24,16},{1,9},{9,1},{17,25},{25,17},{2,10},{10... | collective-permute-start | bytes 4718600 | tf_op jit(solution)/shard_map/ppermute | solution.py:756
  515.7 41.0 %collective-permute-start.27 = (bf16[384,1536]{1,0:T(8,128)(2,1)}, bf16[384,1536]{1,0:T(8,128)(2,1)S(1)}, u32[]{:S(2)}, u32[]{:S(2)}) collective-permute-start(bf16[384,1536]{1,0:T(8,128)(2,1)} %get-tuple-element.56), channel_id=1, source_target_pairs={{0,24},{8,16},{16,8},{24,0},{1,25},{9,17},{17,9},{25,1},{2,26},{10... | collective-permute-start | bytes 3538952 | tf_op jit(solution)/shard_map/ppermute | solution.py:756
  517.3 54.4 %collective-permute-start.26 = (bf16[384,1536]{1,0:T(8,128)(2,1)}, bf16[384,1536]{1,0:T(8,128)(2,1)S(1)}, u32[]{:S(2)}, u32[]{:S(2)}) collective-permute-start(bf16[384,1536]{1,0:T(8,128)(2,1)} %get-tuple-element.55), channel_id=1, source_target_pairs={{0,16},{8,24},{16,0},{24,8},{1,17},{9,25},{17,1},{25,9},{2,18},{10... | collective-permute-start | bytes 3538952 | tf_op jit(solution)/shard_map/ppermute | solution.py:756
  517.8 62.5 %collective-permute-start.25 = (bf16[384,1536]{1,0:T(8,128)(2,1)}, bf16[384,1536]{1,0:T(8,128)(2,1)S(1)}, u32[]{:S(2)}, u32[]{:S(2)}) collective-permute-start(bf16[384,1536]{1,0:T(8,128)(2,1)} %get-tuple-element.54), channel_id=1, source_target_pairs={{0,8},{8,0},{16,24},{24,16},{1,9},{9,1},{17,25},{25,17},{2,10},{10... | collective-permute-start | bytes 3538952 | tf_op jit(solution)/shard_map/ppermute | solution.py:756
  519.2 1.2 collective-permute-start.31
  520.4 6.2 collective-permute-start.32
  526.7 5.1 collective-permute-start.33
  529.2 5.0 copy-start.4
  531.8 73.6 %collective-permute-start.40 = (bf16[48,128,128]{2,1,0:T(8,128)(2,1)S(1)}, bf16[48,128,128]{2,1,0:T(8,128)(2,1)S(1)}, u32[]{:S(2)}, u32[]{:S(2)}) collective-permute-start(bf16[48,128,128]{2,1,0:T(8,128)(2,1)S(1)} %pad_maximum_fusion.2), channel_id=1, source_target_pairs={{0,16},{8,24},{16,0},{24,8},{1,17},{9,25},{17,1},{25,9},{2,18},{10... | collective-permute-start | bytes 4718600 | tf_op jit(solution)/shard_map/ppermute | solution.py:756
  532.7 49.3 %collective-permute-start.34 = (f32[2,1536]{1,0:T(2,128)S(1)}, f32[2,1536]{1,0:T(2,128)S(1)}, u32[]{:S(2)}, u32[]{:S(2)}) collective-permute-start(f32[2,1536]{1,0:T(2,128)S(1)} %add.303), channel_id=1, source_target_pairs={{0,8},{8,0},{16,24},{24,16},{1,9},{9,1},{17,25},{25,17},{2,10},{10... | collective-permute-start | bytes 36872 | tf_op jit(solution)/shard_map/ppermute | solution.py:756
  534.2 46.1 %copy-start.8 = (f32[384,1536]{1,0:T(8,128)S(1)}, f32[384,1536]{1,0:T(8,128)}, u32[]{:S(2)}) copy-start(f32[384,1536]{1,0:T(8,128)} %get-tuple-element.45.middle_ref) | copy-start | bytes 7077892
  536.5 43.8 %copy-start.12 = (bf16[384,1536]{1,0:T(8,128)(2,1)S(1)}, bf16[384,1536]{1,0:T(8,128)(2,1)}, u32[]{:S(2)}) copy-start(bf16[384,1536]{1,0:T(8,128)(2,1)} %get-tuple-element.53) | copy-start | bytes 3538948
  556.7 64.4 %collective-permute-start.38 = (bf16[24,128,128]{2,1,0:T(8,128)(2,1)S(1)}, bf16[24,128,128]{2,1,0:T(8,128)(2,1)S(1)}, u32[]{:S(2)}, u32[]{:S(2)}) collective-permute-start(bf16[24,128,128]{2,1,0:T(8,128)(2,1)S(1)} %slice.133), channel_id=1, source_target_pairs={{0,16},{8,24},{16,0},{24,8},{1,17},{9,25},{17,1},{25,9},{2,18},{10... | collective-permute-start | bytes 2359304 | tf_op jit(solution)/shard_map/ppermute | solution.py:756
  580.3 25.1 %copy-start.1 = (bf16[24,128,128]{2,1,0:T(8,128)(2,1)S(1)}, bf16[24,128,128]{2,1,0:T(8,128)(2,1)}, u32[]{:S(2)}) copy-start(bf16[24,128,128]{2,1,0:T(8,128)(2,1)} %get-tuple-element.98) | copy-start | bytes 2359300
  580.3 25.1 %copy-start.2 = (bf16[24,128,128]{2,1,0:T(8,128)(2,1)S(1)}, bf16[24,128,128]{2,1,0:T(8,128)(2,1)}, u32[]{:S(2)}) copy-start(bf16[24,128,128]{2,1,0:T(8,128)(2,1)} %get-tuple-element.101) | copy-start | bytes 2359300
  582.1 38.9 %collective-permute-start.35 = (f32[2,1536]{1,0:T(2,128)S(1)}, f32[2,1536]{1,0:T(2,128)S(1)}, u32[]{:S(2)}, u32[]{:S(2)}) collective-permute-start(f32[2,1536]{1,0:T(2,128)S(1)} %add.304), channel_id=1, source_target_pairs={{0,16},{8,24},{16,0},{24,8},{1,17},{9,25},{17,1},{25,9},{2,18},{10... | collective-permute-start | bytes 36872 | tf_op jit(solution)/shard_map/ppermute | solution.py:756
  606.0 17.6 %collective-permute-start.41 = (bf16[24,128,128]{2,1,0:T(8,128)(2,1)S(1)}, bf16[24,128,128]{2,1,0:T(8,128)(2,1)S(1)}, u32[]{:S(2)}, u32[]{:S(2)}) collective-permute-start(bf16[24,128,128]{2,1,0:T(8,128)(2,1)S(1)} %slice.141), channel_id=1, source_target_pairs={{0,8},{8,0},{16,24},{24,16},{1,9},{9,1},{17,25},{25,17},{2,10},{10... | collective-permute-start | bytes 2359304 | tf_op jit(solution)/shard_map/ppermute | solution.py:756
  621.1 8.5 %copy-start.16 = (f32[2,1536]{1,0:T(2,128)}, f32[2,1536]{1,0:T(2,128)S(1)}, u32[]{:S(2)}) copy-start(f32[2,1536]{1,0:T(2,128)S(1)} %get-tuple-element.97) | copy-start | bytes 36868
  622.2 7.4 %copy-start.19 = (f32[2,1536]{1,0:T(2,128)S(1)}, f32[2,1536]{1,0:T(2,128)}, u32[]{:S(2)}) copy-start(f32[2,1536]{1,0:T(2,128)} %gains_ref.3) | copy-start | bytes 36868
  622.2 14.6 %collective-permute-start.39 = (bf16[12,128,128]{2,1,0:T(8,128)(2,1)S(1)}, bf16[12,128,128]{2,1,0:T(8,128)(2,1)S(1)}, u32[]{:S(2)}, u32[]{:S(2)}) collective-permute-start(bf16[12,128,128]{2,1,0:T(8,128)(2,1)S(1)} %get-tuple-element.108), channel_id=1, source_target_pairs={{0,2},{1,3},{2,4},{3,5},{4,6},{5,7},{6,0},{7,1},{8,10},{9,11},{10,... | collective-permute-start | bytes 1179656 | tf_op jit(solution)/shard_map/ppermute | solution.py:670
  623.9 32.2 %collective-permute-start.42 = (bf16[12,128,128]{2,1,0:T(8,128)(2,1)S(1)}, bf16[12,128,128]{2,1,0:T(8,128)(2,1)S(1)}, u32[]{:S(2)}, u32[]{:S(2)}) collective-permute-start(bf16[12,128,128]{2,1,0:T(8,128)(2,1)S(1)} %get-tuple-element.107), channel_id=1, source_target_pairs={{0,4},{1,5},{2,6},{3,7},{4,0},{5,1},{6,2},{7,3},{8,12},{9,13},{10,... | collective-permute-start | bytes 1179656 | tf_op jit(solution)/shard_map/ppermute | solution.py:670
  629.5 32.2 %collective-permute-start.43 = (bf16[12,128,128]{2,1,0:T(8,128)(2,1)S(1)}, bf16[12,128,128]{2,1,0:T(8,128)(2,1)S(1)}, u32[]{:S(2)}, u32[]{:S(2)}) collective-permute-start(bf16[12,128,128]{2,1,0:T(8,128)(2,1)S(1)} %get-tuple-element.106), channel_id=1, source_target_pairs={{0,6},{1,7},{2,0},{3,1},{4,2},{5,3},{6,4},{7,5},{8,14},{9,15},{10,... | collective-permute-start | bytes 1179656 | tf_op jit(solution)/shard_map/ppermute | solution.py:670
  636.8 24.9 %copy-start.13 = (bf16[12,128,128]{2,1,0:T(8,128)(2,1)}, bf16[12,128,128]{2,1,0:T(8,128)(2,1)S(1)}, u32[]{:S(2)}) copy-start(bf16[12,128,128]{2,1,0:T(8,128)(2,1)S(1)} %collective-permute-done.39.refs_1_) | copy-start | bytes 1179652
  656.1 5.7 copy-start.14
  (9 other events, 19.4 us)
Sparse Core Ops, SparseCore 0:
  11.6 190.8 all-gather.1
  362.9 189.1 reduce-scatter.1

commit v2 on v1

--- a/solution.py
+++ b/solution.py
@@ -23,309 +23,6 @@
 STEP_SIZE = 0.3
 
 
-def rope_tables(positions):
-    frequency = 10000.0 ** (-2.0 * jnp.arange(HD // 2, dtype=jnp.float32) / HD)
-    angles = positions[:, None] * frequency[None, :]
-    return (jnp.cos(angles), jnp.sin(angles))
-
-
-def dot_nn(left, right):
-    return lax.dot_general(left, right, (((1,), (0,)), ((), ())), preferred_element_type=F32)
-
-
-def dot_nt(left, right):
-    return lax.dot_general(left, right, (((1,), (1,)), ((), ())), preferred_element_type=F32)
-
-
-def dot_tn(left, right):
-    return lax.dot_general(left, right, (((0,), (0,)), ((), ())), preferred_element_type=F32)
-
-
-def params(**more):
-    return pltpu.CompilerParams(vmem_limit_bytes=VMEM_BYTES, **more)
-
-
-def whole(memory_space):
-    return pl.BlockSpec(memory_space=memory_space)
-
-
-def held(shape):
-    return pl.BlockSpec(shape, lambda *_: (0,) * len(shape))
-
-
-def inverse_of(dealing):
-    slot_count = dealing.shape[0]
-    return (
-        jnp.zeros((slot_count,), jnp.int32)
-        .at[dealing]
-        .set(jnp.arange(slot_count, dtype=jnp.int32), unique_indices=True)
-    )
-
-
-def assemble_experts(blocks, inverse):
-    across, wide, tall = D // BLOCK, 2 * FF // BLOCK, FF // BLOCK
-    first, second = across * wide, tall * across
-
-    def kernel(inverse_ref, blocks_ref, gateup_ref, down_ref, gateup_two, down_two, sems):
-        def out(expert):
-            half = expert % 2
-            return [
-                pltpu.make_async_copy(gateup_two.at[half], gateup_ref.at[expert], sems.at[2 + half]),
-                pltpu.make_async_copy(down_two.at[half], down_ref.at[expert], sems.at[2 + half]),
-            ]
-
-        for expert in range(EXP_DEV):
-            base, half = expert * (first + second), expert % 2
-            if expert >= 2:
-                for copy in out(expert - 2):
-                    copy.wait()
-
-            def gateup_block(i, _):
-                pltpu.make_async_copy(
-                    blocks_ref.at[inverse_ref[base + i]],
-                    block_at(gateup_two.at[half], i // wide, i % wide),
-                    sems.at[half],
-                ).start()
-                return 0
-
-            def down_block(i, _):
-                pltpu.make_async_copy(
-                    blocks_ref.at[inverse_ref[base + first + i]],
-                    block_at(down_two.at[half], i // across, i % across),
-                    sems.at[half],
-                ).start()
-                return 0
-
-            lax.fori_loop(0, first, gateup_block, 0, unroll=4)
-            lax.fori_loop(0, second, down_block, 0, unroll=4)
-            pltpu.make_async_copy(gateup_two.at[half], gateup_two.at[half], sems.at[half]).wait()
-            pltpu.make_async_copy(down_two.at[half], down_two.at[half], sems.at[half]).wait()
-            for copy in out(expert):
-                copy.start()
-        for expert in (EXP_DEV - 2, EXP_DEV - 1):
-            for copy in out(expert):
-                copy.wait()
-
-    return pl.pallas_call(
-        kernel,
-        name="assemble_experts",
-        out_shape=(
-            jax.ShapeDtypeStruct((EXP_DEV, D, 2 * FF), BF16),
-            jax.ShapeDtypeStruct((EXP_DEV, FF, D), BF16),
-        ),
-        in_specs=[whole(pltpu.SMEM), whole(pl.ANY)],
-        out_specs=(whole(pl.ANY), whole(pl.ANY)),
-        scratch_shapes=[
-            pltpu.VMEM((2, D, 2 * FF), BF16),
-            pltpu.VMEM((2, FF, D), BF16),
-            pltpu.SemaphoreType.DMA((4,)),
-        ],
-        compiler_params=params(),
-        cost_estimate=pl.CostEstimate(flops=0, bytes_accessed=4 * blocks.size, transcendentals=0),
-    )(inverse, blocks)
-
-
-def weight_of(packed, expert):
-    lane = lax.broadcasted_iota(jnp.int32, packed.shape, 1)
-    return jnp.sum(jnp.where(lane == expert, packed.astype(F32), 0.0), axis=1, keepdims=True)
-
-
-def expert_front(group, rows, packed, w_gateup, w_down):
-    count = rows.shape[0]
-
-    def kernel(group_ref, rows_ref, packed_ref, gateup_ref, down_ref, hidden_ref, both_ref, out_ref, total):
-        step = pl.program_id(0)
-        weight = weight_of(packed_ref[:, D:], group_ref[0] * EXP_DEV + step)
-        gate_up = dot_nn(rows_ref[...], gateup_ref[0])
-        gate, up = gate_up[:, :FF], gate_up[:, FF:]
-        sigmoid = jax.nn.sigmoid(gate)
-        silu = gate * sigmoid
-        hidden_ref[0] = (silu * up).astype(BF16)
-        grad_rows = (weight * packed_ref[:, :D].astype(F32)).astype(BF16)
-        grad_hidden = dot_nt(grad_rows, down_ref[0])
-        both_ref[0, :, :FF] = (grad_hidden * up * sigmoid * (1.0 + gate * (1.0 - sigmoid))).astype(BF16)
-        both_ref[0, :, FF:] = (grad_hidden * silu).astype(BF16)
-        route = dot_nt(both_ref[0], gateup_ref[0]).astype(BF16).astype(F32)
-
-        @pl.when(step == 0)
-        def _():
-            total[...] = route
-
-        @pl.when(step > 0)
-        def _():
-            total[...] += route
-
-        @pl.when(step == EXP_DEV - 1)
-        def _():
-            out_ref[...] = total[...].astype(BF16)
-
-    return pl.pallas_call(
-        kernel,
-        name="expert_front",
-        grid=(EXP_DEV,),
-        out_shape=(
-            jax.ShapeDtypeStruct((EXP_DEV, count, FF), BF16),
-            jax.ShapeDtypeStruct((EXP_DEV, count, 2 * FF), BF16),
-            jax.ShapeDtypeStruct((count, D), BF16),
-        ),
-        in_specs=[
-            whole(pltpu.SMEM),
-            held((count, D)),
-            held((count, D + LANES)),
-            pl.BlockSpec((1, D, 2 * FF), lambda j: (j, 0, 0)),
-            pl.BlockSpec((1, FF, D), lambda j: (j, 0, 0)),
-        ],
-        out_specs=(
-            pl.BlockSpec((1, count, FF), lambda j: (j, 0, 0)),
-            pl.BlockSpec((1, count, 2 * FF), lambda j: (j, 0, 0)),
-            held((count, D)),
-        ),
-        scratch_shapes=[pltpu.VMEM((count, D), F32)],
-        compiler_params=params(dimension_semantics=("arbitrary",)),
-        cost_estimate=pl.CostEstimate(
-            flops=EXP_DEV * 2 * 5 * count * D * FF,
-            bytes_accessed=EXP_DEV * 3 * D * FF * 2,
-            transcendentals=EXP_DEV * count * FF,
-        ),
-    )(group, rows, packed, w_gateup, w_down)
-
-
-def expert_weight_grads(group, inverse, rows, packed, hidden, both):
-    parts = len(rows)
-    count = rows[0].shape[0]
-    slots = inverse.shape[0]
-    across, wide, tall = D // BLOCK, 2 * FF // BLOCK, FF // BLOCK
-    first, second = across * wide, tall * across
-    tile = 256
-
-    def kernel(group_ref, inverse_ref, *refs):
-        rows_refs, packed_refs = refs[:parts], refs[parts : 2 * parts]
-        hidden_refs, both_refs = refs[2 * parts : 3 * parts], refs[3 * parts : 4 * parts]
-        out_ref, stage_gateup, stage_down, sems = refs[4 * parts :]
-        step = pl.program_id(0)
-        base = step * (first + second)
-
-        def wait_gateup():
-            pltpu.make_async_copy(stage_gateup, stage_gateup, sems.at[0]).wait()
-
-        def wait_down():
-            pltpu.make_async_copy(stage_down, stage_down, sems.at[1]).wait()
-
-        pl.when(step > 0)(wait_gateup)
-        for at in range(0, 2 * FF, tile):
-            span = slice(at, at + tile)
-            stage_gateup[:, span] = sum(
-                dot_tn(x[...], b[0, :, span]) for x, b in zip(rows_refs, both_refs)
-            ).astype(BF16)
-
-        def gateup_block(i, _):
-            row, col = i // wide, i % wide
-            pltpu.make_async_copy(
-                stage_gateup.at[pl.ds(pl.multiple_of(row * BLOCK, BLOCK), BLOCK), pl.ds(pl.multiple_of(col * BLOCK, BLOCK), BLOCK)],
-                out_ref.at[inverse_ref[base + i]],
-                sems.at[0],
-            ).start()
-            return 0
-
-        lax.fori_loop(0, first, gateup_block, 0, unroll=8)
-        pl.when(step > 0)(wait_down)
-        weights = [
-            weight_of(p[:, D:], group_ref[0] * EXP_DEV + step) for p in packed_refs
-        ]
-        for at in range(0, D, tile):
-            span = slice(at, at + tile)
-            stage_down[:, span] = sum(
-                dot_tn(h[0], (w * p[:, span].astype(F32)).astype(BF16))
-                for h, p, w in zip(hidden_refs, packed_refs, weights)
-            ).astype(BF16)
-
-        def down_block(i, _):
-            row, col = i // across, i % across
-            pltpu.make_async_copy(
-                stage_down.at[pl.ds(pl.multiple_of(row * BLOCK, BLOCK), BLOCK), pl.ds(pl.multiple_of(col * BLOCK, BLOCK), BLOCK)],
-                out_ref.at[inverse_ref[base + first + i]],
-                sems.at[1],
-            ).start()
-            return 0
-
-        lax.fori_loop(0, second, down_block, 0, unroll=8)
-
-        @pl.when(step == EXP_DEV - 1)
-        def _():
-            wait_gateup()
-            wait_down()
-
-    return pl.pallas_call(
-        kernel,
-        name="expert_weight_grads",
-        grid=(EXP_DEV,),
-        out_shape=jax.ShapeDtypeStruct((slots, BLOCK, BLOCK), BF16),
-        in_specs=[whole(pltpu.SMEM), whole(pltpu.SMEM)]
-        + [held((count, D))] * parts
-        + [held((count, D + LANES))] * parts
-        + [pl.BlockSpec((1, count, FF), lambda j: (j, 0, 0))] * parts
-        + [pl.BlockSpec((1, count, 2 * FF), lambda j: (j, 0, 0))] * parts,
-        out_specs=whole(pl.ANY),
-        scratch_shapes=[
-            pltpu.VMEM((D, 2 * FF), BF16),
-            pltpu.VMEM((FF, D), BF16),
-            pltpu.SemaphoreType.DMA((2,)),
-        ],
-        compiler_params=params(dimension_semantics=("arbitrary",)),
-        cost_estimate=pl.CostEstimate(
-            flops=EXP_DEV * 2 * 3 * parts * count * D * FF,
-            bytes_accessed=EXP_DEV * 3 * (parts * count * FF + D * FF) * 2,
-            transcendentals=0,
-        ),
-    )(group, inverse, *rows, *packed, *hidden, *both)
-
-
-def expert_outputs(group, packed, hidden, w_down):
-    parts = len(packed)
-    count = packed[0].shape[0]
-
-    def kernel(group_ref, *refs):
-        packed_refs, hidden_refs = refs[:parts], refs[parts : 2 * parts]
-        down_ref = refs[2 * parts]
-        out_refs, totals = refs[2 * parts + 1 : 3 * parts + 1], refs[3 * parts + 1 :]
-        step = pl.program_id(0)
-        for packed_ref, hidden_ref, out_ref, total in zip(packed_refs, hidden_refs, out_refs, totals):
-            weight = weight_of(packed_ref[...], group_ref[0] * EXP_DEV + step)
-            produced = dot_nn(hidden_ref[0], down_ref[0]).astype(BF16).astype(F32)
-            term = weight * produced
-
-            @pl.when(step == 0)
-            def _():
-                total[...] = term
-
-            @pl.when(step > 0)
-            def _():
-                total[...] += term
-
-            @pl.when(step == EXP_DEV - 1)
-            def _():
-                out_ref[...] = total[...].astype(BF16)
-
-    return pl.pallas_call(
-        kernel,
-        name="expert_outputs",
-        grid=(EXP_DEV,),
-        out_shape=tuple(jax.ShapeDtypeStruct((count, D), BF16) for _ in range(parts)),
-        in_specs=[whole(pltpu.SMEM)]
-        + [pl.BlockSpec((count, LANES), lambda j: (0, D // LANES))] * parts
-        + [pl.BlockSpec((1, count, FF), lambda j: (j, 0, 0))] * parts
-        + [pl.BlockSpec((1, FF, D), lambda j: (j, 0, 0))],
-        out_specs=tuple(held((count, D)) for _ in range(parts)),
-        scratch_shapes=[pltpu.VMEM((count, D), F32)] * parts,
-        compiler_params=params(dimension_semantics=("arbitrary",)),
-        cost_estimate=pl.CostEstimate(
-            flops=EXP_DEV * 2 * parts * count * D * FF,
-            bytes_accessed=EXP_DEV * (parts * count * FF + D * FF) * 2,
-            transcendentals=0,
-        ),
-    )(group, *packed, *hidden, w_down)
-
-
 QUERY_END = H * HD
 KEYVAL_END = QUERY_END + 2 * KV * HD
 ACROSS = D // BLOCK
@@ -333,6 +30,326 @@
 KEYVAL_COLS = (KEYVAL_END - QUERY_END) // BLOCK
 OUT_COLS = D // BLOCK
 ALL_COLS = QUERY_COLS + KEYVAL_COLS + OUT_COLS
+
+
+def rope_tables(positions):
+    frequency = 10000.0 ** (-2.0 * jnp.arange(HD // 2, dtype=jnp.float32) / HD)
+    angles = positions[:, None] * frequency[None, :]
+    return (jnp.cos(angles), jnp.sin(angles))
+
+
+def dot_nn(left, right):
+    return lax.dot_general(left, right, (((1,), (0,)), ((), ())), preferred_element_type=F32)
+
+
+def dot_nt(left, right):
+    return lax.dot_general(left, right, (((1,), (1,)), ((), ())), preferred_element_type=F32)
+
+
+def dot_tn(left, right):
+    return lax.dot_general(left, right, (((0,), (0,)), ((), ())), preferred_element_type=F32)
+
+
+def params(**more):
+    return pltpu.CompilerParams(vmem_limit_bytes=VMEM_BYTES, **more)
+
+
+def cost(microseconds):
+    return pl.CostEstimate(flops=int(microseconds * 1.15e9), bytes_accessed=1024, transcendentals=0)
+
+
+def whole(memory_space):
+    return pl.BlockSpec(memory_space=memory_space)
+
+
+def held(shape):
+    return pl.BlockSpec(shape, lambda *_: (0,) * len(shape))
+
+
+def inverse_of(dealing):
+    place = jnp.arange(dealing.shape[0], dtype=jnp.int32)
+    return jnp.sum(jnp.where(dealing[None, :] == place[:, None], place[None, :], 0), axis=1)
+
+
+def weight_of(packed, expert):
+    lane = lax.broadcasted_iota(jnp.int32, packed.shape, 1)
+    return jnp.sum(jnp.where(lane == expert, packed.astype(F32), 0.0), axis=1, keepdims=True)
+
+
+def aligned(block):
+    return block * BLOCK if isinstance(block, int) else pl.multiple_of(block * BLOCK, BLOCK)
+
+
+def block_at(ref, row, col):
+    return ref.at[
+        pl.ds(aligned(row), BLOCK),
+        pl.ds(aligned(col), BLOCK),
+    ]
+
+
+def stacked_copies(sources, target, sem):
+    count = sources[0].shape[-2]
+    return [
+        pltpu.make_async_copy(
+            source, target.at[pl.ds(i * count, count), :], sem
+        )
+        for i, source in enumerate(sources)
+    ]
+
+
+def expert_step(weight, rows, packed, matrix):
+    gate_up = dot_nn(rows[...], matrix[:, : 2 * FF])
+    grad_hidden = dot_nt(packed[:, :FF], matrix[:FF, 2 * FF :])
+    for at in range(FF, D, FF):
+        grad_hidden = grad_hidden + dot_nt(packed[:, at : at + FF], matrix[at : at + FF, 2 * FF :])
+    gate, up = gate_up[:, :FF], gate_up[:, FF:]
+    sigmoid = 0.5 * jnp.tanh(0.5 * gate) + 0.5
+    silu = gate * sigmoid
+    hidden = (silu * up * weight).astype(BF16)
+    slope = grad_hidden * sigmoid * weight
+    both = jnp.concatenate(
+        [(slope * up * (1.0 + gate - silu)).astype(BF16), (slope * gate).astype(BF16)], axis=1
+    )
+    return hidden, both, dot_nt(both, matrix[:, : 2 * FF])
+
+
+def expert_front(group, inverse, blocks, rows, packed):
+    parts = len(rows)
+    count = rows[0].shape[0]
+    across, wide, tall = D // BLOCK, 2 * FF // BLOCK, FF // BLOCK
+    first, second = across * wide, tall * across
+
+    def kernel(group_ref, inverse_ref, blocks_ref, *refs):
+        refs = list(refs)
+        take = lambda n: [refs.pop(0) for _ in range(n)]
+        rows_refs, packed_refs = take(parts), take(parts)
+        hidden_refs, both_refs, out_refs = take(parts), take(parts), take(parts)
+        kept_ref, rows_all, packed_all, total, matrices, block_sems, keep_sems, sems = refs
+        step = pl.program_id(0)
+        half = step % 2
+
+        def bring(expert, half):
+            base = expert * (first + second)
+
+            for i in range(first + second):
+                row, col = i // wide, i % wide
+                if i >= first:
+                    down = (i - first) % across
+                    row, col = down // tall * tall + (i - first) // across, wide + down % tall
+                pltpu.make_async_copy(
+                    blocks_ref.at[inverse_ref[base + i]],
+                    block_at(matrices.at[half], row, col),
+                    block_sems.at[half],
+                ).start()
+
+        def keep(expert, half):
+            return pltpu.make_async_copy(
+                matrices.at[half, :, pl.ds(2 * FF, FF)], kept_ref.at[expert], keep_sems.at[half]
+            )
+
+        loads = [
+            pltpu.make_async_copy(source, target.at[i], sems.at[n, i])
+            for i in range(parts)
+            for n, (source, target) in enumerate(
+                ((rows_refs[i], rows_all), (packed_refs[i], packed_all))
+            )
+        ]
+
+        @pl.when(step == 0)
+        def _():
+            for load in loads[:2]:
+                load.start()
+            bring(0, 0)
+            for load in loads[2:]:
+                load.start()
+
+        @pl.when(step > 0)
+        def _():
+            keep(step - 1, 1 - half).wait()
+
+        @pl.when(step < EXP_DEV - 1)
+        def _():
+            bring(step + 1, 1 - half)
+
+        matrix = matrices.at[half]
+        pltpu.make_async_copy(matrix, matrix, block_sems.at[half]).wait()
+        keep(step, half).start()
+
+        @pl.when(step == 0)
+        def _():
+            total[...] = jnp.zeros_like(total)
+            for load in loads:
+                load.wait()
+
+        for i in range(parts):
+            weight = weight_of(packed_all[i, :, D:], group_ref[0] * EXP_DEV + step)
+            hidden, both, route = expert_step(weight, rows_all.at[i], packed_all.at[i], matrix)
+            hidden_refs[i][0] = hidden
+            both_refs[i][0] = both
+            total[i] += route
+
+        @pl.when(step == EXP_DEV - 1)
+        def _():
+            for i in range(parts):
+                out_refs[i][...] = total[i].astype(BF16)
+            keep(step, half).wait()
+
+    any_space, smem = whole(pl.ANY), whole(pltpu.SMEM)
+    out = pl.pallas_call(
+        kernel,
+        name="expert_front",
+        grid=(EXP_DEV,),
+        out_shape=(
+            [jax.ShapeDtypeStruct((EXP_DEV, count, FF), BF16)] * parts
+            + [jax.ShapeDtypeStruct((EXP_DEV, count, 2 * FF), BF16)] * parts
+            + [jax.ShapeDtypeStruct((count, D), BF16)] * parts
+            + [jax.ShapeDtypeStruct((EXP_DEV, D, FF), BF16)]
+        ),
+        in_specs=[smem] * 2 + [any_space] * (1 + 2 * parts),
+        out_specs=(
+            [pl.BlockSpec((1, count, FF), lambda j: (j, 0, 0))] * parts
+            + [pl.BlockSpec((1, count, 2 * FF), lambda j: (j, 0, 0))] * parts
+            + [held((count, D))] * parts
+            + [any_space]
+        ),
+        scratch_shapes=[
+            pltpu.VMEM((parts, count, D), BF16),
+            pltpu.VMEM((parts, count, D + LANES), BF16),
+            pltpu.VMEM((parts, count, D), F32),
+            pltpu.VMEM((2, D, 3 * FF), BF16),
+            pltpu.SemaphoreType.DMA((2,)),
+            pltpu.SemaphoreType.DMA((2,)),
+            pltpu.SemaphoreType.DMA((2, parts)),
+        ],
+        compiler_params=params(dimension_semantics=("arbitrary",)),
+        cost_estimate=cost(100),
+    )(group, inverse, blocks, *rows, *packed)
+    return out[:parts], out[parts : 2 * parts], out[2 * parts : 3 * parts], out[-1]
+
+
+def expert_weight_grads(positions, rows, packed, hidden, both):
+    parts = len(rows)
+    count = rows[0].shape[0]
+    total_rows = parts * count
+    slots = positions.shape[0]
+    across, wide, tall = D // BLOCK, 2 * FF // BLOCK, FF // BLOCK
+    first, second = across * wide, tall * across
+    tile = 256
+
+    def kernel(position_ref, *refs):
+        refs = list(refs)
+        take = lambda n: [refs.pop(0) for _ in range(n)]
+        rows_refs, packed_refs, hidden_refs, both_refs = take(parts), take(parts), take(parts), take(parts)
+        out_ref, rows_all, packed_all, hidden_two, both_two, stage_gateup, stage_down, sems = refs
+        step = pl.program_id(0)
+        half = step % 2
+        base = step * (first + second)
+
+        def loads(expert, half):
+            return stacked_copies([r.at[expert] for r in hidden_refs], hidden_two.at[half], sems.at[2 + half]) + stacked_copies(
+                [r.at[expert] for r in both_refs], both_two.at[half], sems.at[4 + half]
+            )
+
+        once = stacked_copies(rows_refs, rows_all, sems.at[6]) + stacked_copies(packed_refs, packed_all, sems.at[7])
+
+        @pl.when(step == 0)
+        def _():
+            for load in once[:parts] + loads(0, 0) + once[parts:]:
+                load.start()
+
+        for load in loads(step, half):
+            load.wait()
+
+        @pl.when(step < EXP_DEV - 1)
+        def _():
+            for load in loads(step + 1, 1 - half):
+                load.start()
+
+        @pl.when(step == 0)
+        def _():
+            for load in once[:parts]:
+                load.wait()
+
+        def wait_gateup():
+            pltpu.make_async_copy(stage_gateup, stage_gateup, sems.at[0]).wait()
+
+        def wait_down():
+            pltpu.make_async_copy(stage_down, stage_down, sems.at[1]).wait()
+
+        def send(stage, sem, start, blocks, columns):
+            for i in range(blocks):
+                pltpu.make_async_copy(
+                    block_at(stage, i // columns, i % columns), out_ref.at[position_ref[start + i]], sem
+                ).start()
+
+        pl.when(step > 0)(wait_gateup)
+        for at in range(0, 2 * FF, tile):
+            stage_gateup[:, at : at + tile] = dot_tn(
+                rows_all[...], both_two[half, :, at : at + tile]
+            ).astype(BF16)
+        send(stage_gateup, sems.at[0], base, first, wide)
+        pl.when(step > 0)(wait_down)
+
+        @pl.when(step == 0)
+        def _():
+            for load in once[parts:]:
+                load.wait()
+
+        for at in range(0, D, tile):
+            stage_down[:, at : at + tile] = dot_tn(
+                hidden_two[half], packed_all[:, at : at + tile]
+            ).astype(BF16)
+        send(stage_down, sems.at[1], base + first, second, across)
+
+        @pl.when(step == EXP_DEV - 1)
+        def _():
+            wait_gateup()
+            wait_down()
+
+    any_space, smem = whole(pl.ANY), whole(pltpu.SMEM)
+    return pl.pallas_call(
+        kernel,
+        name="expert_weight_grads",
+        grid=(EXP_DEV,),
+        out_shape=jax.ShapeDtypeStruct((slots, BLOCK, BLOCK), BF16),
+        in_specs=[smem] + [any_space] * (4 * parts),
+        out_specs=any_space,
+        scratch_shapes=[
+            pltpu.VMEM((total_rows, D), BF16),
+            pltpu.VMEM((total_rows, D + LANES), BF16),
+            pltpu.VMEM((2, total_rows, FF), BF16),
+            pltpu.VMEM((2, total_rows, 2 * FF), BF16),
+            pltpu.VMEM((D, 2 * FF), BF16),
+            pltpu.VMEM((FF, D), BF16),
+            pltpu.SemaphoreType.DMA((8,)),
+        ],
+        compiler_params=params(dimension_semantics=("arbitrary",)),
+        cost_estimate=cost(100),
+    )(positions, *rows, *packed, *hidden, *both)
+
+
+def expert_outputs(hidden, matrices):
+    parts = len(hidden)
+    count = hidden[0].shape[1]
+
+    def kernel(*refs):
+        hidden_refs, matrix_ref, out_refs = refs[:parts], refs[parts], refs[parts + 1 :]
+        for hidden_ref, out_ref in zip(hidden_refs, out_refs):
+            out_ref[...] = sum(
+                dot_nn(hidden_ref[expert], matrix_ref[expert]) for expert in range(EXP_DEV)
+            ).astype(BF16)
+
+    return pl.pallas_call(
+        kernel,
+        name="expert_outputs",
+        grid=(D // FF,),
+        out_shape=tuple(jax.ShapeDtypeStruct((count, D), BF16) for _ in range(parts)),
+        in_specs=[held((EXP_DEV, count, FF))] * parts
+        + [pl.BlockSpec((EXP_DEV, FF, FF), lambda j: (0, j, 0))],
+        out_specs=tuple(pl.BlockSpec((count, FF), lambda j: (0, j)) for _ in range(parts)),
+        compiler_params=params(dimension_semantics=("arbitrary",)),
+        cost_estimate=cost(30),
+    )(*hidden, matrices)
 
 
 def attention_places(natural):
@@ -354,13 +371,6 @@
         ),
     )
     return row.astype(jnp.int32), col.astype(jnp.int32)
-
-
-def block_at(ref, row, col):
-    return ref.at[
-        pl.ds(pl.multiple_of(row * BLOCK, BLOCK), BLOCK),
-        pl.ds(pl.multiple_of(col * BLOCK, BLOCK), BLOCK),
-    ]
 
 
 def turn(values, cosine, sine):
@@ -470,11 +480,7 @@
             pltpu.SemaphoreType.DMA((2,)),
         ],
         compiler_params=params(),
-        cost_estimate=pl.CostEstimate(
-            flops=2 * count * D * ALL_COLS * BLOCK + 4 * H * count * count * HD,
-            bytes_accessed=4 * D * ALL_COLS * BLOCK,
-            transcendentals=H * count * count,
-        ),
+        cost_estimate=cost(100),
     )(lengths, block_rows, block_cols, tokens, gains, cosine, sine, *pieces)
 
 
@@ -600,11 +606,7 @@
             pltpu.SemaphoreType.DMA((3,)),
         ],
         compiler_params=params(),
-        cost_estimate=pl.CostEstimate(
-            flops=4 * count * D * ALL_COLS * BLOCK + 10 * H * count * count * HD,
-            bytes_accessed=4 * D * ALL_COLS * BLOCK,
-            transcendentals=H * count * count,
-        ),
+        cost_estimate=cost(400),
     )(lengths, positions, tokens, packed, gains, cosine, sine, middle, mixed, q, k, v, *partials, w_all)
 
 
@@ -658,11 +660,7 @@
         in_specs=[one] * terms + [two, two, one],
         out_specs=(one, two, one),
         compiler_params=params(dimension_semantics=("arbitrary",)),
-        cost_estimate=pl.CostEstimate(
-            flops=slots * 7 * 2 * BLOCK**3,
-            bytes_accessed=slots * BLOCK * BLOCK * (2 * terms + 36),
-            transcendentals=0,
-        ),
+        cost_estimate=cost(10),
     )(*gradient, statistics, inverse_roots, master)
 
 
@@ -685,24 +683,26 @@
     return one, two, three
 
 
-def gather_attention(own, deal):
+def gather_attention(own, deal, before):
     size, groups = lax.axis_size("shard"), lax.axis_size("expert")
     slots = own.shape[0]
     by_device = deal.reshape(groups, size, slots)
     if groups != 4 or size != 8:
-        return [lax.all_gather(own, ("expert", "shard"), axis=0, tiled=True)], deal
+        return [lax.all_gather(own, ("expert", "shard"), axis=0, tiled=True)], deal, before
     me_e, me_s = lax.axis_index("expert"), lax.axis_index("shard")
     pieces, names, far_names = [], [], []
-    lines = [own] + [along(own, d) for d in range(1, size // 2)]
-    for d, line in enumerate(lines):
-        four = jnp.concatenate([line, *two_ways(line, d % 2 == 1)], axis=0)
+    lines = [along(own, d) for d in range(1, size // 2)]
+    fours = [jnp.concatenate([own, *two_ways(own, False)], axis=0)]
+    lines, before = lax.optimization_barrier((lines, before))
+    fours += [jnp.concatenate([line, *two_ways(line, d % 2 == 0)], axis=0) for d, line in enumerate(lines)]
+    for d, four in enumerate(fours):
         pieces.append(four)
         source = (me_s - 2 * d) % size
         for m in range(groups):
             names.append(by_device[me_e ^ m, source])
             far_names.append(by_device[me_e ^ m, source ^ 1])
     pieces += [sibling(piece) for piece in pieces]
-    return pieces, jnp.concatenate(names + far_names)
+    return pieces, jnp.concatenate(names + far_names), before
 
 
 def attention_positions(deal, slots):
@@ -775,7 +775,6 @@
     row_count = tokens.shape[0]
     groups = lax.axis_size("expert")
     group = lax.axis_index("expert").astype(jnp.int32).reshape(1)
-    pieces, natural = gather_attention(attn_master.astype(BF16), attn_deal)
     expert_all = lax.all_gather(expert_master.astype(BF16), "shard", axis=0, tiled=True)
     places = jnp.arange(row_count)
     valid_rows = places < lengths[0]
@@ -785,7 +784,9 @@
         jnp.where(routes[:, k, None] == expert_lane, route_gates[:, k, None], jnp.zeros((), BF16))
         for k in range(TOP)
     )
-    packed = [swap(jnp.concatenate([grad_low, weights_row], axis=1), m) for m in range(groups)]
+    packed = jnp.concatenate([grad_low, weights_row], axis=1)
+    packed = [swap(packed, m) for m in range(groups)]
+    pieces, natural, packed[1:3] = gather_attention(attn_master.astype(BF16), attn_deal, packed[1:3])
     cosine, sine = rope_tables(jnp.arange(row_count, dtype=F32))
     cosine = jnp.concatenate([cosine] * 4, axis=1)
     sine = jnp.concatenate([-sine, sine] * 2, axis=1)
@@ -793,25 +794,22 @@
     normed_two, middle, mixed, q, k, v, w_all = attention_front(
         lengths, block_rows, block_cols, tokens, norm_gains, cosine, sine, pieces
     )
+    rows = [swap(normed_two, m) for m in range(groups)]
     expert_inverse = inverse_of(expert_deal[0])
-    w_gateup, w_down = assemble_experts(expert_all, expert_inverse)
-    rows = [swap(normed_two, m) for m in range(groups)]
-    fronts = {}
-    for m in [*range(1, groups), 0]:
-        fronts[m] = expert_front(group, rows[m], packed[m], w_gateup, w_down)
-    hidden = [fronts[m][0] for m in range(groups)]
-    both = [fronts[m][1] for m in range(groups)]
-    partials = [swap(fronts[m][2], m) for m in range(groups)]
-    expert_term = expert_weight_grads(group, expert_inverse, rows, packed, hidden, both)
-    moe_parts = expert_outputs(group, packed, hidden, w_down)
-    moe_sum = sum(swap(moe_parts[m], m).astype(F32) for m in range(groups))
-    output = (middle + moe_sum).astype(BF16)
+    hidden, both, partials, w_down = expert_front(group, expert_inverse, expert_all, rows, packed)
+    partials = [swap(partial, m) for m, partial in enumerate(partials)]
+    expert_term = expert_weight_grads(expert_inverse, rows, packed, hidden, both)
+    moe_parts = expert_outputs(hidden, w_down)
+    mixed, moe_parts = lax.optimization_barrier((mixed, moe_parts))
+    moe_parts = [swap(part, m) for m, part in enumerate(moe_parts)]
     slots = attn_master.shape[0]
     positions = attention_positions(attn_deal, slots)
     near = positions.shape[0] // (2 if groups == 4 and lax.axis_size("shard") == 8 else 1)
     input_grad, gain_parts, near_blocks, far_blocks = attention_back(
         lengths, positions, tokens, packed[0], norm_gains, cosine, sine, middle, mixed, q, k, v, w_all, partials, near
     )
+    near_blocks, far_blocks, moe_parts = lax.optimization_barrier((near_blocks, far_blocks, moe_parts))
+    output = (middle + sum(part.astype(F32) for part in moe_parts)).astype(BF16)
     attn_terms = scatter_attention(near_blocks, far_blocks, slots)
     expert_term = lax.psum_scatter(expert_term, "shard", scatter_dimension=0, tiled=True)
     gain_grads = sum_everywhere(gain_parts)
@@ -821,6 +819,7 @@
     expert_grads, expert_stats_new, expert_new = shampoo(
         [expert_term], expert_stats, expert_roots, expert_master
     )
+    attn_terms, expert_new = lax.optimization_barrier((attn_terms, expert_new))
     attn_grads, attn_stats_new, attn_new = shampoo(attn_terms, attn_stats, attn_roots, attn_master)
     return (
         output,

time: 703 us -> 574 us (0.82)
  Pallas kernels: 286 us -> 223 us
  waiting for transfers between devices: 297 us -> 253 us
  local copies, waits for them, and re-layouts: 28.5 us -> 12.5 us
  starting transfers between devices: 48.3 us -> 34 us
    pallas_call x6 -> x2, Pallas kernels: 125 us -> 79.4 us  [the longest x1 64.2 us: expert_front(): pl.pallas_call(kernel, name='expert_front', grid=(EXP_DEV,), out_shape=[j...]
    all_gather x1, waiting for transfers between devices: 31.8 us -> 0.01 us  [per_device(): lax.all_gather(expert_master.astype(BF16), 'shard', axis=0, tiled=True)]
    ppermute x14, waiting for transfers between devices: 117 us -> 100 us  [move(): return lax.ppermute(array, 'shard', pairs)]
    pallas_call x1, Pallas kernels: 54.2 us -> 38.4 us  [expert_weight_grads(): pl.pallas_call(kernel, name='expert_weight_grads', grid=(EXP_DEV,), out_s...]
    ppermute x14, starting transfers between devices: 19.2 us -> 4.72 us  [move(): return lax.ppermute(array, 'shard', pairs)]
    scatter x2 -> x0, local copies, waits for them, and re-layouts: 8.04 us -> none  [inverse_of(): return jnp.zeros((slot_count,), jnp.int32).at[dealing].set(jnp.arange(slo...]
  transfers between devices with their start and end apart: 46 -> 46, of which waited for: 22 -> 23; matrix products, arithmetic and copies ran while one was open for 6% -> 6% of each run, Pallas kernels for 26% -> 20%
where the time goes in v2:
time: 574 us; the launch traced here: 563 us
  waiting for transfers between devices  253 us (44%)
  Pallas kernels  223 us (39%)
  starting transfers between devices  34 us (6%)
  other arithmetic  24.1 us (4%)
  between operations  15.8 us (3%)
  local copies, waits for them, and re-layouts  12.5 us (2%)
    ppermute x30, waiting for transfers between devices, swap(): lax.ppermute(array, 'expert', [(i, i ^ mask) for i in range(lax.axis_size...  153 us
    ppermute x14, waiting for transfers between devices, move(): return lax.ppermute(array, 'shard', pairs)  100 us
    pallas_call x1, Pallas kernels, expert_front(): pl.pallas_call(kernel, name='expert_front', grid=(EXP_DEV,), out_shape=[j...  64.2 us
    pallas_call x1, Pallas kernels, attention_back(): pl.pallas_call(kernel, name='attention_back', out_shape=(jax.ShapeDtypeSt...  50.7 us
    pallas_call x1, Pallas kernels, expert_weight_grads(): pl.pallas_call(kernel, name='expert_weight_grads', grid=(EXP_DEV,), out_s...  38.4 us
    ppermute x30, starting transfers between devices, swap(): lax.ppermute(array, 'expert', [(i, i ^ mask) for i in range(lax.axis_size...  29.2 us
    pallas_call x2, Pallas kernels, shampoo(): pl.pallas_call(kernel, name='shampoo', grid=(slots // many,), out_shape=(...  28.6 us
    pallas_call x1, Pallas kernels, attention_front(): pl.pallas_call(kernel, name='attention_front', out_shape=(jax.ShapeDtypeS...  26.5 us
  transfers between devices with their start and end apart: 46, of which 23 were waited for; matrix products, arithmetic and copies ran while one was open for 6% of the time, Pallas kernels for 20%

profile of v2, /device:TPU:8, one launch (start us, length us, event | category | flops | bytes accessed | tf_op | source)
XLA Modules:
  0.0 562.8 jit_solution(1874751786781322468)
XLA Ops:
  7.2 4.2 convert_element_type.67
  12.4 1.1 fusion.10
  13.8 1.6 collective-permute-start.6
  15.4 1.5 collective-permute-start.7
  16.9 1.6 collective-permute-start.3
  18.6 1.2 collective-permute-start.4
  20.3 26.2 %collective-permute-done.3 = bf16[12,128,128]{2,1,0:T(8,128)(2,1)S(1)} collective-permute-done((bf16[12,128,128]{2,1,0:T(8,128)(2,1)S(1)}, bf16[12,128,128]{2,1,0:T(8,128)(2,1)S(1)}, u32[]{:S(2)}, u32[]{:S(2)}) %collective-permute-start.3) | collective-permute-done | bytes 393248 | tf_op jit(solution)/shard_map/ppermute | solution.py:668
  46.6 43.0 %collective-permute-done.4 = bf16[12,128,128]{2,1,0:T(8,128)(2,1)S(1)} collective-permute-done((bf16[12,128,128]{2,1,0:T(8,128)(2,1)S(1)}, bf16[12,128,128]{2,1,0:T(8,128)(2,1)S(1)}, u32[]{:S(2)}, u32[]{:S(2)}) %collective-permute-start.4) | collective-permute-done | bytes 393248 | tf_op jit(solution)/shard_map/ppermute | solution.py:668
  89.6 2.0 collective-permute-start.2
  91.6 4.0 collective-permute-done.5
  96.2 1.2 collective-permute-start.15
  97.4 7.3 %collective-permute-done.2 = bf16[12,128,128]{2,1,0:T(8,128)(2,1)S(1)} collective-permute-done((bf16[12,128,128]{2,1,0:T(8,128)(2,1)S(1)}, bf16[12,128,128]{2,1,0:T(8,128)(2,1)S(1)}, u32[]{:S(2)}, u32[]{:S(2)}) %collective-permute-start.2) | collective-permute-done | bytes 393248 | tf_op jit(solution)/shard_map/ppermute | solution.py:756
  105.0 1.1 constant_dynamic-update-slice_fusion.3
  106.1 1.9 collective-permute-start.8
  108.0 0.8 constant_dynamic-update-slice_fusion.11
  108.8 0.8 constant_dynamic-update-slice_fusion.10
  109.6 3.6 collective-permute-done.15
  113.2 0.8 constant_dynamic-update-slice_fusion.9
  114.0 3.1 collective-permute-done.11
  117.9 7.6 %collective-permute-done.8 = bf16[12,128,128]{2,1,0:T(8,128)(2,1)S(1)} collective-permute-done((bf16[12,128,128]{2,1,0:T(8,128)(2,1)S(1)}, bf16[12,128,128]{2,1,0:T(8,128)(2,1)S(1)}, u32[]{:S(2)}, u32[]{:S(2)}) %collective-permute-start.8) | collective-permute-done | bytes 393248 | tf_op jit(solution)/shard_map/ppermute | solution.py:756
  127.8 1.8 collective-permute-done.12
  129.6 0.8 constant_dynamic-update-slice_fusion.5
  130.4 3.6 collective-permute-done.16
  136.0 4.2 collective-permute-done.10
  140.2 0.8 constant_dynamic-update-slice_fusion.refs_1_
  141.0 1.2 collective-permute-start.24
  143.3 1.1 pad_maximum_fusion.4
  145.1 26.5 %attention_front.1 = (bf16[384,1536]{1,0:T(8,128)(2,1)}, f32[384,1536]{1,0:T(8,128)}, bf16[384,1536]{1,0:T(8,128)(2,1)}, bf16[24,384,64]{2,1,0:T(8,128)(2,1)}, b...) custom-call(s32[1]{0:T(128)} %copy.33.length_ref, ...), custom_call_target="tpu_custom_call" | custom-call | flops 115000000512 | bytes 1024 | tf_op jit(solution)/shard_map/attention_front/pallas_call | solution.py:463
  171.7 0.8 collective-permute-start.21
  172.5 1.6 collective-permute-start.22
  174.1 1.1 collective-permute-start.23
  175.4 0.8 select_reduce_fusion.inverse_ref.position_ref
  176.9 23.9 %collective-permute-done.21.refs_1_ = bf16[384,1536]{1,0:T(8,128)(2,1)S(1)} collective-permute-done((bf16[384,1536]{1,0:T(8,128)(2,1)}, bf16[384,1536]{1,0:T(8,128)(2,1)S(1)}, u32[]{:S(2)}, u32[]{:S(2)}) %collective-permute-start.21) | collective-permute-done | bytes 1179680 | tf_op jit(solution)/shard_map/ppermute | solution.py:756
  200.8 25.2 %collective-permute-done.22.refs_2_ = bf16[384,1536]{1,0:T(8,128)(2,1)} collective-permute-done((bf16[384,1536]{1,0:T(8,128)(2,1)}, bf16[384,1536]{1,0:T(8,128)(2,1)}, u32[]{:S(2)}, u32[]{:S(2)}) %collective-permute-start.22) | collective-permute-done | bytes 1179680 | tf_op jit(solution)/shard_map/ppermute | solution.py:756
  225.9 64.2 %expert_front.1 = (bf16[4,384,512]{2,1,0:T(8,128)(2,1)}, bf16[4,384,512]{2,1,0:T(8,128)(2,1)}, bf16[4,384,512]{2,1,0:T(8,128)(2,1)}, bf16[4,384,512]{2,1,0:T(8,1...) custom-call(s32[1]{0:T(128)} %bitcast.33.group_ref, ...), custom_call_target="tpu_custom_call" | custom-call | flops 115000000512 | bytes 1024 | tf_op jit(solution)/shard_map/expert_front/pallas_call | solution.py:198
  290.1 38.4 %expert_weight_grads.1 = bf16[576,128,128]{2,1,0:T(8,128)(2,1)} custom-call(s32[576]{0:T(1024)} %select_reduce_fusion.inverse_ref.position_ref, bf16[384,1536]{1,0:T(8,128)(2,1)} %get-tuple-element.70.refs_0_, bf16[384,1536]{1,0:T(8,128)(2,1)} %copy-done.15, bf16[384,1536]{1,0:T(8,128)(2,1)} %collective-permute-done.22.refs_2_, ...), custom_call_target="tpu_custom_call" | custom-call | flops 115000000512 | bytes 1024 | tf_op jit(solution)/shard_map/expert_weight_grads/pallas_call | solution.py:310
  328.5 1.5 collective-permute-start.25
  330.0 1.2 collective-permute-start.26
  331.3 1.4 collective-permute-start.27
  332.7 15.2 %expert_outputs.1 = (bf16[384,1536]{1,0:T(8,128)(2,1)}, bf16[384,1536]{1,0:T(8,128)(2,1)}, bf16[384,1536]{1,0:T(8,128)(2,1)}, bf16[384,1536]{1,0:T(8,128)(2,1)}) custom-call(bf16[4,384,512]{2,1,0:T(8,128)(2,1)} %get-tuple-element.73.refs_0_.refs_8_, bf16[4,384,512]{2,1,0:T(8,128)(2,1)} %get-tuple-element.74.refs_1_.refs_9_, ...), custom_call_target="tpu_custom_call" | custom-call | flops 34500001792 | bytes 1024 | tf_op jit(solution)/shard_map/expert_outputs/pallas_call | solution.py:342
  347.8 1.3 collective-permute-start.28
  349.1 1.2 collective-permute-start.29
  350.4 7.4 %collective-permute-done.25.refs_1_ = bf16[384,1536]{1,0:T(8,128)(2,1)S(1)} collective-permute-done((bf16[384,1536]{1,0:T(8,128)(2,1)}, bf16[384,1536]{1,0:T(8,128)(2,1)S(1)}, u32[]{:S(2)}, u32[]{:S(2)}) %collective-permute-start.25) | collective-permute-done | bytes 1179680 | tf_op jit(solution)/shard_map/ppermute | solution.py:756
  357.7 1.5 collective-permute-start.30
  359.2 25.1 %collective-permute-done.26.refs_2_ = bf16[384,1536]{1,0:T(8,128)(2,1)} collective-permute-done((bf16[384,1536]{1,0:T(8,128)(2,1)S(1)}, bf16[384,1536]{1,0:T(8,128)(2,1)}, u32[]{:S(2)}, u32[]{:S(2)}) %collective-permute-start.26) | collective-permute-done | bytes 1179680 | tf_op jit(solution)/shard_map/ppermute | solution.py:756
  384.3 50.7 %attention_back.1 = (f32[384,1536]{1,0:T(8,128)}, f32[2,1536]{1,0:T(2,128)}, bf16[192,128,128]{2,1,0:T(8,128)(2,1)}, bf16[192,128,128]{2,1,0:T(8,128)(2,1)}) custom-call(s32[1]{0:T(128)} %copy.33.length_ref, s32[384]{0:T(512)} %fusion.30.position_ref, bf16[384,1536]{1,0:T(8,128)(2,1)} %tokens_ref.3, bf16[384,1664]{1,0:T(8,128)(2,1)} %copy-done.2, ...), custom_call_target="tpu_custom_call" | custom-call | flops 460000002048 | bytes 1024 | tf_op jit(solution)/shard_map/attention_back/pallas_call | solution.py:590
  435.1 10.5 %collective-permute-done.36 = bf16[192,128,128]{2,1,0:T(8,128)(2,1)} collective-permute-done((bf16[192,128,128]{2,1,0:T(8,128)(2,1)}, bf16[192,128,128]{2,1,0:T(8,128)(2,1)}, u32[]{:S(2)}, u32[]{:S(2)}) %collective-permute-start.36) | collective-permute-done | bytes 6291488 | tf_op jit(solution)/shard_map/ppermute | solution.py:668
  445.6 7.7 %add_convert_fusion = bf16[192,128,128]{2,1,0:T(8,128)(2,1)S(1)} fusion(bf16[192,128,128]{2,1,0:T(8,128)(2,1)} %collective-permute-done.36, bf16[192,128,128]{2,1,0:T(8,128)(2,1)} %get-tuple-element.103), kind=kLoop, calls=%fused_computation | loop fusion | flops 12582912 | bytes 18874368 | tf_op jit(solution)/shard_map/convert_element_type | solution.py:722
  453.3 1.4 slice_bitcast_fusion.3
  454.8 1.3 collective-permute-start.40
  456.3 0.9 collective-permute-start.37
  457.1 1.2 collective-permute-done.31
  458.4 4.1 collective-permute-done.32
  462.6 5.0 collective-permute-done.33
  467.6 1.3 collective-permute-start.34
  468.9 24.0 %collective-permute-done.34 = f32[2,1536]{1,0:T(2,128)S(1)} collective-permute-done((f32[2,1536]{1,0:T(2,128)S(1)}, f32[2,1536]{1,0:T(2,128)S(1)}, u32[]{:S(2)}, u32[]{:S(2)}) %collective-permute-start.34) | collective-permute-done | bytes 12320 | tf_op jit(solution)/shard_map/ppermute | solution.py:756
  493.6 3.9 add_convert_fusion.3
  498.2 1.4 collective-permute-start.41
  501.6 14.9 %collective-permute-done.41 = bf16[24,128,128]{2,1,0:T(8,128)(2,1)S(1)} collective-permute-done((bf16[24,128,128]{2,1,0:T(8,128)(2,1)S(1)}, bf16[24,128,128]{2,1,0:T(8,128)(2,1)S(1)}, u32[]{:S(2)}, u32[]{:S(2)}) %collective-permute-start.41) | collective-permute-done | bytes 786464 | tf_op jit(solution)/shard_map/ppermute | solution.py:756
  516.9 1.0 collective-permute-start.43
  518.7 0.8 fusion.77
  520.1 22.8 %shampoo.2 = (f32[72,128,128]{2,1,0:T(8,128)}, f32[72,2,128,128]{3,2,1,0:T(8,128)}, f32[72,128,128]{2,1,0:T(8,128)}) custom-call(bf16[72,128,128]{2,1,0:T(8,128)(2,1)} %reduce-scatter.2.cloned.1.call-done.refs_0_, f32[72,2,128,128]{3,2,1,0:T(8,128)} %refs_1_.1, f32[72,2,128,128]{3,2,1,0:T(8,128)} %refs_2_.1, f32[72,128,128]{2,1,0:T(8,128)} %refs_3_.1), custom_call_target="tpu_custom_call" | custom-call | flops 11500000256 | bytes 1024 | tf_op jit(solution)/shard_map/shampoo/pallas_call | solution.py:651
  542.9 6.0 %collective-permute-done.43.refs_3_ = bf16[12,128,128]{2,1,0:T(8,128)(2,1)S(1)} collective-permute-done((bf16[12,128,128]{2,1,0:T(8,128)(2,1)S(1)}, bf16[12,128,128]{2,1,0:T(8,128)(2,1)S(1)}, u32[]{:S(2)}, u32[]{:S(2)}) %collective-permute-start.43) | collective-permute-done | bytes 393248 | tf_op jit(solution)/shard_map/ppermute | solution.py:668
  549.7 5.8 %shampoo.3 = (f32[12,128,128]{2,1,0:T(8,128)}, f32[12,2,128,128]{3,2,1,0:T(8,128)}, f32[12,128,128]{2,1,0:T(8,128)}) custom-call(bf16[12,128,128]{2,1,0:T(8,128)(2,1)} %get-tuple-element.110.refs_0_, bf16[12,128,128]{2,1,0:T(8,128)(2,1)} %copy-done.21, bf16[12,128,128]{2,1,0:T(8,128)(2,1)} %copy-done.19, bf16[12,128,128]{2,1,0:T(8,128)(2,1)} %copy-done.20, ...), custom_call_target="tpu_custom_call" | custom-call | flops 11500000256 | bytes 1024 | tf_op jit(solution)/shard_map/shampoo/pallas_call | solution.py:651
  (132 shorter events, 15.9 us)
Async XLA Ops:
  7.2 218.8 %all-gather.2.cloned.1.call-start = ((), (), s32[]{:S(2)}) async-start(), calls=%async_computation.1 | async-start | bytes 21233664 | tf_op jit(solution)/shard_map/all_gather | solution.py:778
  11.4 0.9 copy-start.8
  11.4 2.1 copy-start.3
  11.5 508.6 %reduce-scatter.2.cloned.1.call-start = ((), (), s32[]{:S(2)}) async-start(), calls=%async_computation.2 | async-start | bytes 21233664 | tf_op jit(solution)/shard_map/reduce_scatter | solution.py:814
  13.7 3.2 copy-start.5
  13.8 127.2 %copy-start.2 = (bf16[384,1664]{1,0:T(8,128)(2,1)}, bf16[384,1664]{1,0:T(8,128)(2,1)S(1)}, u32[]{:S(2)}) copy-start(bf16[384,1664]{1,0:T(8,128)(2,1)S(1)} %pad_maximum_fusion.3.refs_4_.packed_ref) | copy-start | bytes 3833860
  13.8 81.8 %collective-permute-start.6 = (bf16[384,1664]{1,0:T(8,128)(2,1)S(1)}, bf16[384,1664]{1,0:T(8,128)(2,1)S(1)}, u32[]{:S(2)}, u32[]{:S(2)}) collective-permute-start(bf16[384,1664]{1,0:T(8,128)(2,1)S(1)} %pad_maximum_fusion.3.refs_4_.packed_ref), channel_id=1, source_target_pairs={{0,8},{8,0},{16,24},{24,16},{1,9},{9,1},{17,25},{25,17},{2,10},{10... | collective-permute-start | bytes 3833864 | tf_op jit(solution)/shard_map/ppermute | solution.py:756
  15.4 80.2 %collective-permute-start.7 = (bf16[384,1664]{1,0:T(8,128)(2,1)S(1)}, bf16[384,1664]{1,0:T(8,128)(2,1)S(1)}, u32[]{:S(2)}, u32[]{:S(2)}) collective-permute-start(bf16[384,1664]{1,0:T(8,128)(2,1)S(1)} %pad_maximum_fusion.3.refs_4_.packed_ref), channel_id=1, source_target_pairs={{0,16},{8,24},{16,0},{24,8},{1,17},{9,25},{17,1},{25,9},{2,18},{10... | collective-permute-start | bytes 3833864 | tf_op jit(solution)/shard_map/ppermute | solution.py:756
  16.9 29.6 %collective-permute-start.3 = (bf16[12,128,128]{2,1,0:T(8,128)(2,1)S(1)}, bf16[12,128,128]{2,1,0:T(8,128)(2,1)S(1)}, u32[]{:S(2)}, u32[]{:S(2)}) collective-permute-start(bf16[12,128,128]{2,1,0:T(8,128)(2,1)S(1)} %convert_element_type.66), channel_id=1, source_target_pairs={{0,2},{1,3},{2,4},{3,5},{4,6},{5,7},{6,0},{7,1},{8,10},{9,11},{10,... | collective-permute-start | bytes 1179656 | tf_op jit(solution)/shard_map/ppermute | solution.py:668
  18.6 71.0 %collective-permute-start.4 = (bf16[12,128,128]{2,1,0:T(8,128)(2,1)S(1)}, bf16[12,128,128]{2,1,0:T(8,128)(2,1)S(1)}, u32[]{:S(2)}, u32[]{:S(2)}) collective-permute-start(bf16[12,128,128]{2,1,0:T(8,128)(2,1)S(1)} %convert_element_type.66), channel_id=1, source_target_pairs={{0,4},{1,5},{2,6},{3,7},{4,0},{5,1},{6,2},{7,3},{8,12},{9,13},{10,... | collective-permute-start | bytes 1179656 | tf_op jit(solution)/shard_map/ppermute | solution.py:668
  19.8 69.8 %collective-permute-start = (bf16[12,128,128]{2,1,0:T(8,128)(2,1)S(1)}, bf16[12,128,128]{2,1,0:T(8,128)(2,1)S(1)}, u32[]{:S(2)}, u32[]{:S(2)}) collective-permute-start(bf16[12,128,128]{2,1,0:T(8,128)(2,1)S(1)} %convert_element_type.66), channel_id=1, source_target_pairs={{0,8},{8,0},{16,24},{24,16},{1,9},{9,1},{17,25},{25,17},{2,10},{10... | collective-permute-start | bytes 1179656 | tf_op jit(solution)/shard_map/ppermute | solution.py:756
  46.6 49.0 %collective-permute-start.5 = (bf16[12,128,128]{2,1,0:T(8,128)(2,1)S(1)}, bf16[12,128,128]{2,1,0:T(8,128)(2,1)S(1)}, u32[]{:S(2)}, u32[]{:S(2)}) collective-permute-start(bf16[12,128,128]{2,1,0:T(8,128)(2,1)S(1)} %convert_element_type.66), channel_id=1, source_target_pairs={{0,6},{1,7},{2,0},{3,1},{4,2},{5,3},{6,4},{7,5},{8,14},{9,15},{10,... | collective-permute-start | bytes 1179656 | tf_op jit(solution)/shard_map/ppermute | solution.py:668
  89.6 7.8 %collective-permute-start.1 = (bf16[12,128,128]{2,1,0:T(8,128)(2,1)S(1)}, bf16[12,128,128]{2,1,0:T(8,128)(2,1)S(1)}, u32[]{:S(2)}, u32[]{:S(2)}) collective-permute-start(bf16[12,128,128]{2,1,0:T(8,128)(2,1)S(1)} %convert_element_type.66), channel_id=1, source_target_pairs={{0,16},{8,24},{16,0},{24,8},{1,17},{9,25},{17,1},{25,9},{2,18},{10... | collective-permute-start | bytes 1179656 | tf_op jit(solution)/shard_map/ppermute | solution.py:756
  89.6 15.2 %collective-permute-start.2 = (bf16[12,128,128]{2,1,0:T(8,128)(2,1)S(1)}, bf16[12,128,128]{2,1,0:T(8,128)(2,1)S(1)}, u32[]{:S(2)}, u32[]{:S(2)}) collective-permute-start(bf16[12,128,128]{2,1,0:T(8,128)(2,1)S(1)} %collective-permute-done), channel_id=1, source_target_pairs={{0,16},{8,24},{16,0},{24,8},{1,17},{9,25},{17,1},{25,9},{2,18},{10... | collective-permute-start | bytes 1179656 | tf_op jit(solution)/shard_map/ppermute | solution.py:756
  95.6 1.8 copy-start.13
  95.6 1.8 copy-start.14
  95.6 13.2 %collective-permute-start.14 = (bf16[12,128,128]{2,1,0:T(8,128)(2,1)S(1)}, bf16[12,128,128]{2,1,0:T(8,128)(2,1)S(1)}, u32[]{:S(2)}, u32[]{:S(2)}) collective-permute-start(bf16[12,128,128]{2,1,0:T(8,128)(2,1)S(1)} %collective-permute-done.5), channel_id=1, source_target_pairs={{0,8},{8,0},{16,24},{24,16},{1,9},{9,1},{17,25},{25,17},{2,10},{10... | collective-permute-start | bytes 1179656 | tf_op jit(solution)/shard_map/ppermute | solution.py:756
  96.2 17.0 %collective-permute-start.15 = (bf16[12,128,128]{2,1,0:T(8,128)(2,1)S(1)}, bf16[12,128,128]{2,1,0:T(8,128)(2,1)S(1)}, u32[]{:S(2)}, u32[]{:S(2)}) collective-permute-start(bf16[12,128,128]{2,1,0:T(8,128)(2,1)S(1)} %collective-permute-done.5), channel_id=1, source_target_pairs={{0,16},{8,24},{16,0},{24,8},{1,17},{9,25},{17,1},{25,9},{2,18},{10... | collective-permute-start | bytes 1179656 | tf_op jit(solution)/shard_map/ppermute | solution.py:756
  105.0 4.6 copy-start.1
  105.0 12.1 %collective-permute-start.11 = (bf16[12,128,128]{2,1,0:T(8,128)(2,1)S(1)}, bf16[12,128,128]{2,1,0:T(8,128)(2,1)S(1)}, u32[]{:S(2)}, u32[]{:S(2)}) collective-permute-start(bf16[12,128,128]{2,1,0:T(8,128)(2,1)S(1)} %collective-permute-done.4), channel_id=1, source_target_pairs={{0,8},{8,0},{16,24},{24,16},{1,9},{9,1},{17,25},{25,17},{2,10},{10... | collective-permute-start | bytes 1179656 | tf_op jit(solution)/shard_map/ppermute | solution.py:756
  106.1 19.4 %collective-permute-start.8 = (bf16[12,128,128]{2,1,0:T(8,128)(2,1)S(1)}, bf16[12,128,128]{2,1,0:T(8,128)(2,1)S(1)}, u32[]{:S(2)}, u32[]{:S(2)}) collective-permute-start(bf16[12,128,128]{2,1,0:T(8,128)(2,1)S(1)} %collective-permute-done.3), channel_id=1, source_target_pairs={{0,8},{8,0},{16,24},{24,16},{1,9},{9,1},{17,25},{25,17},{2,10},{10... | collective-permute-start | bytes 1179656 | tf_op jit(solution)/shard_map/ppermute | solution.py:756
  108.0 17.5 %collective-permute-start.9 = (bf16[12,128,128]{2,1,0:T(8,128)(2,1)S(1)}, bf16[12,128,128]{2,1,0:T(8,128)(2,1)S(1)}, u32[]{:S(2)}, u32[]{:S(2)}) collective-permute-start(bf16[12,128,128]{2,1,0:T(8,128)(2,1)S(1)} %collective-permute-done.3), channel_id=1, source_target_pairs={{0,16},{8,24},{16,0},{24,8},{1,17},{9,25},{17,1},{25,9},{2,18},{10... | collective-permute-start | bytes 1179656 | tf_op jit(solution)/shard_map/ppermute | solution.py:756
  108.8 36.3 %collective-permute-start.17 = (bf16[48,128,128]{2,1,0:T(8,128)(2,1)S(1)}, bf16[48,128,128]{2,1,0:T(8,128)(2,1)}, u32[]{:S(2)}, u32[]{:S(2)}) collective-permute-start(bf16[48,128,128]{2,1,0:T(8,128)(2,1)S(1)} %pad_maximum_fusion.refs_0_), channel_id=1, source_target_pairs={{0,1},{1,0},{2,3},{3,2},{4,5},{5,4},{6,7},{7,6},{8,9},{9,8},{10,11... | collective-permute-start | bytes 4718600 | tf_op jit(solution)/shard_map/ppermute | solution.py:668
  113.2 16.4 %collective-permute-start.12 = (bf16[12,128,128]{2,1,0:T(8,128)(2,1)S(1)}, bf16[12,128,128]{2,1,0:T(8,128)(2,1)S(1)}, u32[]{:S(2)}, u32[]{:S(2)}) collective-permute-start(bf16[12,128,128]{2,1,0:T(8,128)(2,1)S(1)} %collective-permute-done.4), channel_id=1, source_target_pairs={{0,16},{8,24},{16,0},{24,8},{1,17},{9,25},{17,1},{25,9},{2,18},{10... | collective-permute-start | bytes 1179656 | tf_op jit(solution)/shard_map/ppermute | solution.py:756
  117.1 16.9 %collective-permute-start.16 = (bf16[12,128,128]{2,1,0:T(8,128)(2,1)S(1)}, bf16[12,128,128]{2,1,0:T(8,128)(2,1)S(1)}, u32[]{:S(2)}, u32[]{:S(2)}) collective-permute-start(bf16[12,128,128]{2,1,0:T(8,128)(2,1)S(1)} %collective-permute-done.15), channel_id=1, source_target_pairs={{0,8},{8,0},{16,24},{24,16},{1,9},{9,1},{17,25},{25,17},{2,10},{10... | collective-permute-start | bytes 1179656 | tf_op jit(solution)/shard_map/ppermute | solution.py:756
  125.5 9.8 %collective-permute-start.13 = (bf16[12,128,128]{2,1,0:T(8,128)(2,1)S(1)}, bf16[12,128,128]{2,1,0:T(8,128)(2,1)S(1)}, u32[]{:S(2)}, u32[]{:S(2)}) collective-permute-start(bf16[12,128,128]{2,1,0:T(8,128)(2,1)S(1)} %collective-permute-done.11), channel_id=1, source_target_pairs={{0,16},{8,24},{16,0},{24,8},{1,17},{9,25},{17,1},{25,9},{2,18},{10... | collective-permute-start | bytes 1179656 | tf_op jit(solution)/shard_map/ppermute | solution.py:756
  125.5 14.7 %collective-permute-start.10 = (bf16[12,128,128]{2,1,0:T(8,128)(2,1)S(1)}, bf16[12,128,128]{2,1,0:T(8,128)(2,1)S(1)}, u32[]{:S(2)}, u32[]{:S(2)}) collective-permute-start(bf16[12,128,128]{2,1,0:T(8,128)(2,1)S(1)} %collective-permute-done.9), channel_id=1, source_target_pairs={{0,8},{8,0},{16,24},{24,16},{1,9},{9,1},{17,25},{25,17},{2,10},{10... | collective-permute-start | bytes 1179656 | tf_op jit(solution)/shard_map/ppermute | solution.py:756
  127.8 14.4 %copy-start.11 = (s32[384]{0:T(512)S(1)}, s32[384]{0:T(512)}, u32[]{:S(2)}) copy-start(s32[384]{0:T(512)} %param.23) | copy-start | bytes 4612
  134.7 10.4 %collective-permute-start.20 = (bf16[48,128,128]{2,1,0:T(8,128)(2,1)}, bf16[48,128,128]{2,1,0:T(8,128)(2,1)}, u32[]{:S(2)}, u32[]{:S(2)}) collective-permute-start(bf16[48,128,128]{2,1,0:T(8,128)(2,1)} %constant_dynamic-update-slice_fusion.8.refs_3_), channel_id=1, source_target_pairs={{0,1},{1,0},{2,3},{3,2},{4,5},{5,4},{6,7},{7,6},{8,9},{9,8},{10,11... | collective-permute-start | bytes 4718600 | tf_op jit(solution)/shard_map/ppermute | solution.py:668
  136.0 9.0 %collective-permute-start.19 = (bf16[48,128,128]{2,1,0:T(8,128)(2,1)}, bf16[48,128,128]{2,1,0:T(8,128)(2,1)}, u32[]{:S(2)}, u32[]{:S(2)}) collective-permute-start(bf16[48,128,128]{2,1,0:T(8,128)(2,1)} %constant_dynamic-update-slice_fusion.4.refs_2_), channel_id=1, source_target_pairs={{0,1},{1,0},{2,3},{3,2},{4,5},{5,4},{6,7},{7,6},{8,9},{9,8},{10,11... | collective-permute-start | bytes 4718600 | tf_op jit(solution)/shard_map/ppermute | solution.py:668
  141.0 4.1 collective-permute-start.18
  141.0 35.9 %collective-permute-start.24 = (bf16[384,1664]{1,0:T(8,128)(2,1)S(1)}, bf16[384,1664]{1,0:T(8,128)(2,1)}, u32[]{:S(2)}, u32[]{:S(2)}) collective-permute-start(bf16[384,1664]{1,0:T(8,128)(2,1)S(1)} %pad_maximum_fusion.3.refs_4_.packed_ref), channel_id=1, source_target_pairs={{0,24},{8,16},{16,8},{24,0},{1,25},{9,17},{17,9},{25,1},{2,26},{10... | collective-permute-start | bytes 3833864 | tf_op jit(solution)/shard_map/ppermute | solution.py:756
  145.1 30.1 %copy-start.12 = (s32[1,576]{1,0:T(1,128)S(1)}, s32[1,576]{1,0:T(1,128)}, u32[]{:S(2)}) copy-start(s32[1,576]{1,0:T(1,128)} %param.27) | copy-start | bytes 6916
  171.7 29.1 %collective-permute-start.21 = (bf16[384,1536]{1,0:T(8,128)(2,1)}, bf16[384,1536]{1,0:T(8,128)(2,1)S(1)}, u32[]{:S(2)}, u32[]{:S(2)}) collective-permute-start(bf16[384,1536]{1,0:T(8,128)(2,1)} %get-tuple-element.70.refs_0_), channel_id=1, source_target_pairs={{0,8},{8,0},{16,24},{24,16},{1,9},{9,1},{17,25},{25,17},{2,10},{10... | collective-permute-start | bytes 3538952 | tf_op jit(solution)/shard_map/ppermute | solution.py:756
  172.5 53.4 %collective-permute-start.22 = (bf16[384,1536]{1,0:T(8,128)(2,1)}, bf16[384,1536]{1,0:T(8,128)(2,1)}, u32[]{:S(2)}, u32[]{:S(2)}) collective-permute-start(bf16[384,1536]{1,0:T(8,128)(2,1)} %get-tuple-element.70.refs_0_), channel_id=1, source_target_pairs={{0,16},{8,24},{16,0},{24,8},{1,17},{9,25},{17,1},{25,9},{2,18},{10... | collective-permute-start | bytes 3538952 | tf_op jit(solution)/shard_map/ppermute | solution.py:756
  174.1 51.8 %collective-permute-start.23 = (bf16[384,1536]{1,0:T(8,128)(2,1)}, bf16[384,1536]{1,0:T(8,128)(2,1)}, u32[]{:S(2)}, u32[]{:S(2)}) collective-permute-start(bf16[384,1536]{1,0:T(8,128)(2,1)} %get-tuple-element.70.refs_0_), channel_id=1, source_target_pairs={{0,24},{8,16},{16,8},{24,0},{1,25},{9,17},{17,9},{25,1},{2,26},{10... | collective-permute-start | bytes 3538952 | tf_op jit(solution)/shard_map/ppermute | solution.py:756
  200.8 25.2 %copy-start.15 = (bf16[384,1536]{1,0:T(8,128)(2,1)}, bf16[384,1536]{1,0:T(8,128)(2,1)S(1)}, u32[]{:S(2)}) copy-start(bf16[384,1536]{1,0:T(8,128)(2,1)S(1)} %collective-permute-done.21.refs_1_) | copy-start | bytes 3538948
  328.5 1.5 copy-start.17
  328.5 2.8 copy-start.16
  328.5 29.2 %collective-permute-start.25 = (bf16[384,1536]{1,0:T(8,128)(2,1)}, bf16[384,1536]{1,0:T(8,128)(2,1)S(1)}, u32[]{:S(2)}, u32[]{:S(2)}) collective-permute-start(bf16[384,1536]{1,0:T(8,128)(2,1)} %get-tuple-element.87), channel_id=1, source_target_pairs={{0,8},{8,0},{16,24},{24,16},{1,9},{9,1},{17,25},{25,17},{2,10},{10... | collective-permute-start | bytes 3538952 | tf_op jit(solution)/shard_map/ppermute | solution.py:756
  330.0 54.3 %collective-permute-start.26 = (bf16[384,1536]{1,0:T(8,128)(2,1)S(1)}, bf16[384,1536]{1,0:T(8,128)(2,1)}, u32[]{:S(2)}, u32[]{:S(2)}) collective-permute-start(bf16[384,1536]{1,0:T(8,128)(2,1)S(1)} %copy-done.17), channel_id=1, source_target_pairs={{0,16},{8,24},{16,0},{24,8},{1,17},{9,25},{17,1},{25,9},{2,18},{10... | collective-permute-start | bytes 3538952 | tf_op jit(solution)/shard_map/ppermute | solution.py:756
  331.3 53.1 %collective-permute-start.27 = (bf16[384,1536]{1,0:T(8,128)(2,1)S(1)}, bf16[384,1536]{1,0:T(8,128)(2,1)}, u32[]{:S(2)}, u32[]{:S(2)}) collective-permute-start(bf16[384,1536]{1,0:T(8,128)(2,1)S(1)} %copy-done.16), channel_id=1, source_target_pairs={{0,24},{8,16},{16,8},{24,0},{1,25},{9,17},{17,9},{25,1},{2,26},{10... | collective-permute-start | bytes 3538952 | tf_op jit(solution)/shard_map/ppermute | solution.py:756
  347.8 87.2 %collective-permute-start.28 = (bf16[384,1536]{1,0:T(8,128)(2,1)}, bf16[384,1536]{1,0:T(8,128)(2,1)}, u32[]{:S(2)}, u32[]{:S(2)}) collective-permute-start(bf16[384,1536]{1,0:T(8,128)(2,1)} %get-tuple-element.94), channel_id=1, source_target_pairs={{0,8},{8,0},{16,24},{24,16},{1,9},{9,1},{17,25},{25,17},{2,10},{10... | collective-permute-start | bytes 3538952 | tf_op jit(solution)/shard_map/ppermute | solution.py:756
  349.1 85.9 %collective-permute-start.29 = (bf16[384,1536]{1,0:T(8,128)(2,1)}, bf16[384,1536]{1,0:T(8,128)(2,1)}, u32[]{:S(2)}, u32[]{:S(2)}) collective-permute-start(bf16[384,1536]{1,0:T(8,128)(2,1)} %get-tuple-element.95), channel_id=1, source_target_pairs={{0,16},{8,24},{16,0},{24,8},{1,17},{9,25},{17,1},{25,9},{2,18},{10... | collective-permute-start | bytes 3538952 | tf_op jit(solution)/shard_map/ppermute | solution.py:756
  357.7 26.6 %copy-start.18 = (bf16[384,1536]{1,0:T(8,128)(2,1)}, bf16[384,1536]{1,0:T(8,128)(2,1)S(1)}, u32[]{:S(2)}) copy-start(bf16[384,1536]{1,0:T(8,128)(2,1)S(1)} %collective-permute-done.25.refs_1_) | copy-start | bytes 3538948
  357.7 77.3 %collective-permute-start.30 = (bf16[384,1536]{1,0:T(8,128)(2,1)}, bf16[384,1536]{1,0:T(8,128)(2,1)}, u32[]{:S(2)}, u32[]{:S(2)}) collective-permute-start(bf16[384,1536]{1,0:T(8,128)(2,1)} %get-tuple-element.96), channel_id=1, source_target_pairs={{0,24},{8,16},{16,8},{24,0},{1,25},{9,17},{17,9},{25,1},{2,26},{10... | collective-permute-start | bytes 3538952 | tf_op jit(solution)/shard_map/ppermute | solution.py:756
  435.0 10.6 %collective-permute-start.36 = (bf16[192,128,128]{2,1,0:T(8,128)(2,1)}, bf16[192,128,128]{2,1,0:T(8,128)(2,1)}, u32[]{:S(2)}, u32[]{:S(2)}) collective-permute-start(bf16[192,128,128]{2,1,0:T(8,128)(2,1)} %get-tuple-element.104), channel_id=1, source_target_pairs={{0,1},{1,0},{2,3},{3,2},{4,5},{5,4},{6,7},{7,6},{8,9},{9,8},{10,11... | collective-permute-start | bytes 18874376 | tf_op jit(solution)/shard_map/ppermute | solution.py:668
  454.6 39.0 %copy-start.4 = (bf16[384,1536]{1,0:T(8,128)(2,1)S(1)}, bf16[384,1536]{1,0:T(8,128)(2,1)}, u32[]{:S(2)}) copy-start(bf16[384,1536]{1,0:T(8,128)(2,1)} %get-tuple-element.97) | copy-start | bytes 3538948
  454.8 42.9 %collective-permute-start.40 = (bf16[48,128,128]{2,1,0:T(8,128)(2,1)S(1)}, bf16[48,128,128]{2,1,0:T(8,128)(2,1)S(1)}, u32[]{:S(2)}, u32[]{:S(2)}) collective-permute-start(bf16[48,128,128]{2,1,0:T(8,128)(2,1)S(1)} %pad_maximum_fusion.2), channel_id=1, source_target_pairs={{0,16},{8,24},{16,0},{24,8},{1,17},{9,25},{17,1},{25,9},{2,18},{10... | collective-permute-start | bytes 4718600 | tf_op jit(solution)/shard_map/ppermute | solution.py:756
  456.1 1.0 copy-start.10
  456.1 37.5 %copy-start = (f32[384,1536]{1,0:T(8,128)S(1)}, f32[384,1536]{1,0:T(8,128)}, u32[]{:S(2)}) copy-start(f32[384,1536]{1,0:T(8,128)} %get-tuple-element.68.middle_ref) | copy-start | bytes 7077892
  456.3 43.4 %collective-permute-start.37 = (bf16[48,128,128]{2,1,0:T(8,128)(2,1)S(1)}, bf16[48,128,128]{2,1,0:T(8,128)(2,1)S(1)}, u32[]{:S(2)}, u32[]{:S(2)}) collective-permute-start(bf16[48,128,128]{2,1,0:T(8,128)(2,1)S(1)} %pad_maximum_fusion.1), channel_id=1, source_target_pairs={{0,8},{8,0},{16,24},{24,16},{1,9},{9,1},{17,25},{25,17},{2,10},{10... | collective-permute-start | bytes 4718600 | tf_op jit(solution)/shard_map/ppermute | solution.py:756
  457.1 1.2 collective-permute-start.31
  458.3 4.2 collective-permute-start.32
  462.5 5.1 collective-permute-start.33
  467.6 25.4 %collective-permute-start.34 = (f32[2,1536]{1,0:T(2,128)S(1)}, f32[2,1536]{1,0:T(2,128)S(1)}, u32[]{:S(2)}, u32[]{:S(2)}) collective-permute-start(f32[2,1536]{1,0:T(2,128)S(1)} %add.280), channel_id=1, source_target_pairs={{0,8},{8,0},{16,24},{24,16},{1,9},{9,1},{17,25},{25,17},{2,10},{10... | collective-permute-start | bytes 36872 | tf_op jit(solution)/shard_map/ppermute | solution.py:756
  493.0 4.5 collective-permute-start.35
  497.6 3.3 copy-start.6
  498.2 18.3 %collective-permute-start.41 = (bf16[24,128,128]{2,1,0:T(8,128)(2,1)S(1)}, bf16[24,128,128]{2,1,0:T(8,128)(2,1)S(1)}, u32[]{:S(2)}, u32[]{:S(2)}) collective-permute-start(bf16[24,128,128]{2,1,0:T(8,128)(2,1)S(1)} %slice.141), channel_id=1, source_target_pairs={{0,8},{8,0},{16,24},{24,16},{1,9},{9,1},{17,25},{25,17},{2,10},{10... | collective-permute-start | bytes 2359304 | tf_op jit(solution)/shard_map/ppermute | solution.py:756
  500.3 18.2 %collective-permute-start.38 = (bf16[24,128,128]{2,1,0:T(8,128)(2,1)S(1)}, bf16[24,128,128]{2,1,0:T(8,128)(2,1)S(1)}, u32[]{:S(2)}, u32[]{:S(2)}) collective-permute-start(bf16[24,128,128]{2,1,0:T(8,128)(2,1)S(1)} %slice.133), channel_id=1, source_target_pairs={{0,16},{8,24},{16,0},{24,8},{1,17},{9,25},{17,1},{25,9},{2,18},{10... | collective-permute-start | bytes 2359304 | tf_op jit(solution)/shard_map/ppermute | solution.py:756
  516.8 26.0 %collective-permute-start.42 = (bf16[12,128,128]{2,1,0:T(8,128)(2,1)S(1)}, bf16[12,128,128]{2,1,0:T(8,128)(2,1)S(1)}, u32[]{:S(2)}, u32[]{:S(2)}) collective-permute-start(bf16[12,128,128]{2,1,0:T(8,128)(2,1)S(1)} %get-tuple-element.147), channel_id=1, source_target_pairs={{0,4},{1,5},{2,6},{3,7},{4,0},{5,1},{6,2},{7,3},{8,12},{9,13},{10,... | collective-permute-start | bytes 1179656 | tf_op jit(solution)/shard_map/ppermute | solution.py:668
  516.9 32.0 %collective-permute-start.43 = (bf16[12,128,128]{2,1,0:T(8,128)(2,1)S(1)}, bf16[12,128,128]{2,1,0:T(8,128)(2,1)S(1)}, u32[]{:S(2)}, u32[]{:S(2)}) collective-permute-start(bf16[12,128,128]{2,1,0:T(8,128)(2,1)S(1)} %get-tuple-element.146), channel_id=1, source_target_pairs={{0,6},{1,7},{2,0},{3,1},{4,2},{5,3},{6,4},{7,5},{8,14},{9,15},{10,... | collective-permute-start | bytes 1179656 | tf_op jit(solution)/shard_map/ppermute | solution.py:668
  519.5 29.4 %collective-permute-start.39 = (bf16[12,128,128]{2,1,0:T(8,128)(2,1)S(1)}, bf16[12,128,128]{2,1,0:T(8,128)(2,1)S(1)}, u32[]{:S(2)}, u32[]{:S(2)}) collective-permute-start(bf16[12,128,128]{2,1,0:T(8,128)(2,1)S(1)} %get-tuple-element.148), channel_id=1, source_target_pairs={{0,2},{1,3},{2,4},{3,5},{4,6},{5,7},{6,0},{7,1},{8,10},{9,11},{10,... | collective-permute-start | bytes 1179656 | tf_op jit(solution)/shard_map/ppermute | solution.py:668
  542.9 6.0 %copy-start.19 = (bf16[12,128,128]{2,1,0:T(8,128)(2,1)}, bf16[12,128,128]{2,1,0:T(8,128)(2,1)S(1)}, u32[]{:S(2)}) copy-start(bf16[12,128,128]{2,1,0:T(8,128)(2,1)S(1)} %collective-permute-done.42.refs_2_) | copy-start | bytes 1179652
  (4 other events, 3.2 us)
Sparse Core Ops, SparseCore 0:
  11.6 192.1 all-gather.1
  328.7 183.7 reduce-scatter.1

commit v3 on v2

--- a/solution.py
+++ b/solution.py
@@ -14,7 +14,7 @@
 BLOCK = 128
 EXP_DEV = 4
 LANES = 128
-VMEM_BYTES = 60 * 1024 * 1024
+VMEM_BYTES = 63 * 1024 * 1024
 BF16 = jnp.bfloat16
 F32 = jnp.float32
 
@@ -110,7 +110,7 @@
     both = jnp.concatenate(
         [(slope * up * (1.0 + gate - silu)).astype(BF16), (slope * gate).astype(BF16)], axis=1
     )
-    return hidden, both, dot_nt(both, matrix[:, : 2 * FF])
+    return hidden, both
 
 
 def expert_front(group, inverse, blocks, rows, packed):
@@ -122,9 +122,9 @@
     def kernel(group_ref, inverse_ref, blocks_ref, *refs):
         refs = list(refs)
         take = lambda n: [refs.pop(0) for _ in range(n)]
-        rows_refs, packed_refs = take(parts), take(parts)
-        hidden_refs, both_refs, out_refs = take(parts), take(parts), take(parts)
-        kept_ref, rows_all, packed_all, total, matrices, block_sems, keep_sems, sems = refs
+        rows_refs, packed_refs = take(parts), take(len(packed))
+        hidden_refs, both_refs = take(parts), take(parts)
+        out_ref, kept_ref, rows_all, packed_all, total, matrices, block_sems, keep_sems, sems = refs
         step = pl.program_id(0)
         half = step % 2
 
@@ -143,24 +143,21 @@
                 ).start()
 
         def keep(expert, half):
-            return pltpu.make_async_copy(
-                matrices.at[half, :, pl.ds(2 * FF, FF)], kept_ref.at[expert], keep_sems.at[half]
-            )
+            return pltpu.make_async_copy(matrices.at[half], kept_ref.at[expert], keep_sems.at[half])
 
         loads = [
-            pltpu.make_async_copy(source, target.at[i], sems.at[n, i])
+            load
             for i in range(parts)
-            for n, (source, target) in enumerate(
-                ((rows_refs[i], rows_all), (packed_refs[i], packed_all))
-            )
+            for load in [pltpu.make_async_copy(rows_refs[i], rows_all.at[i], sems.at[0, i])]
+            + stacked_copies([ref.at[group_ref[0] ^ i] for ref in packed_refs], packed_all.at[i], sems.at[1, i])
         ]
 
         @pl.when(step == 0)
         def _():
-            for load in loads[:2]:
+            for load in loads[:3]:
                 load.start()
             bring(0, 0)
-            for load in loads[2:]:
+            for load in loads[3:]:
                 load.start()
 
         @pl.when(step > 0)
@@ -183,15 +180,16 @@
 
         for i in range(parts):
             weight = weight_of(packed_all[i, :, D:], group_ref[0] * EXP_DEV + step)
-            hidden, both, route = expert_step(weight, rows_all.at[i], packed_all.at[i], matrix)
+            hidden, both = expert_step(weight, rows_all.at[i], packed_all.at[i], matrix)
             hidden_refs[i][0] = hidden
             both_refs[i][0] = both
-            total[i] += route
+            if i > 0:
+                total[i - 1] += dot_nt(both, matrix[:, : 2 * FF])
 
         @pl.when(step == EXP_DEV - 1)
         def _():
-            for i in range(parts):
-                out_refs[i][...] = total[i].astype(BF16)
+            for i in range(1, parts):
+                out_ref[group_ref[0] ^ i] = total[i - 1].astype(BF16)
             keep(step, half).wait()
 
     any_space, smem = whole(pl.ANY), whole(pltpu.SMEM)
@@ -202,20 +200,20 @@
         out_shape=(
             [jax.ShapeDtypeStruct((EXP_DEV, count, FF), BF16)] * parts
             + [jax.ShapeDtypeStruct((EXP_DEV, count, 2 * FF), BF16)] * parts
-            + [jax.ShapeDtypeStruct((count, D), BF16)] * parts
-            + [jax.ShapeDtypeStruct((EXP_DEV, D, FF), BF16)]
+            + [jax.ShapeDtypeStruct((parts, count, D), BF16)]
+            + [jax.ShapeDtypeStruct((EXP_DEV, D, 3 * FF), BF16)]
         ),
-        in_specs=[smem] * 2 + [any_space] * (1 + 2 * parts),
+        in_specs=[smem] * 2 + [any_space] * (1 + parts + len(packed)),
         out_specs=(
             [pl.BlockSpec((1, count, FF), lambda j: (j, 0, 0))] * parts
             + [pl.BlockSpec((1, count, 2 * FF), lambda j: (j, 0, 0))] * parts
-            + [held((count, D))] * parts
+            + [held((parts, count, D))]
             + [any_space]
         ),
         scratch_shapes=[
             pltpu.VMEM((parts, count, D), BF16),
             pltpu.VMEM((parts, count, D + LANES), BF16),
-            pltpu.VMEM((parts, count, D), F32),
+            pltpu.VMEM((parts - 1, count, D), F32),
             pltpu.VMEM((2, D, 3 * FF), BF16),
             pltpu.SemaphoreType.DMA((2,)),
             pltpu.SemaphoreType.DMA((2,)),
@@ -224,10 +222,10 @@
         compiler_params=params(dimension_semantics=("arbitrary",)),
         cost_estimate=cost(100),
     )(group, inverse, blocks, *rows, *packed)
-    return out[:parts], out[parts : 2 * parts], out[2 * parts : 3 * parts], out[-1]
-
-
-def expert_weight_grads(positions, rows, packed, hidden, both):
+    return out[:parts], out[parts : 2 * parts], out[-2], out[-1]
+
+
+def expert_weight_grads(group, positions, rows, packed, hidden, both):
     parts = len(rows)
     count = rows[0].shape[0]
     total_rows = parts * count
@@ -236,10 +234,10 @@
     first, second = across * wide, tall * across
     tile = 256
 
-    def kernel(position_ref, *refs):
+    def kernel(group_ref, position_ref, *refs):
         refs = list(refs)
         take = lambda n: [refs.pop(0) for _ in range(n)]
-        rows_refs, packed_refs, hidden_refs, both_refs = take(parts), take(parts), take(parts), take(parts)
+        rows_refs, packed_refs, hidden_refs, both_refs = take(parts), take(len(packed)), take(parts), take(parts)
         out_ref, rows_all, packed_all, hidden_two, both_two, stage_gateup, stage_down, sems = refs
         step = pl.program_id(0)
         half = step % 2
@@ -250,7 +248,9 @@
                 [r.at[expert] for r in both_refs], both_two.at[half], sems.at[4 + half]
             )
 
-        once = stacked_copies(rows_refs, rows_all, sems.at[6]) + stacked_copies(packed_refs, packed_all, sems.at[7])
+        once = stacked_copies(rows_refs, rows_all, sems.at[6]) + stacked_copies(
+            [ref.at[group_ref[0] ^ i] for i in range(parts) for ref in packed_refs], packed_all, sems.at[7]
+        )
 
         @pl.when(step == 0)
         def _():
@@ -312,7 +312,7 @@
         name="expert_weight_grads",
         grid=(EXP_DEV,),
         out_shape=jax.ShapeDtypeStruct((slots, BLOCK, BLOCK), BF16),
-        in_specs=[smem] + [any_space] * (4 * parts),
+        in_specs=[smem] * 2 + [any_space] * (3 * parts + len(packed)),
         out_specs=any_space,
         scratch_shapes=[
             pltpu.VMEM((total_rows, D), BF16),
@@ -325,17 +325,40 @@
         ],
         compiler_params=params(dimension_semantics=("arbitrary",)),
         cost_estimate=cost(100),
-    )(positions, *rows, *packed, *hidden, *both)
-
-
-def expert_outputs(hidden, matrices):
+    )(group, positions, *rows, *packed, *hidden, *both)
+
+
+def expert_route(both, matrices):
+    count = both.shape[1]
+
+    def kernel(both_ref, matrix_ref, out_ref):
+        out_ref[...] = sum(
+            dot_nt(both_ref[expert], matrix_ref[expert]) for expert in range(EXP_DEV)
+        ).astype(BF16)
+
+    return pl.pallas_call(
+        kernel,
+        name="expert_route",
+        grid=(D // FF,),
+        out_shape=jax.ShapeDtypeStruct((count, D), BF16),
+        in_specs=[
+            held((EXP_DEV, count, 2 * FF)),
+            pl.BlockSpec((EXP_DEV, FF, 2 * FF), lambda j: (0, j, 0)),
+        ],
+        out_specs=pl.BlockSpec((count, FF), lambda j: (0, j)),
+        compiler_params=params(dimension_semantics=("arbitrary",)),
+        cost_estimate=cost(4),
+    )(both, matrices)
+
+
+def expert_outputs(group, hidden, matrices):
     parts = len(hidden)
     count = hidden[0].shape[1]
 
-    def kernel(*refs):
-        hidden_refs, matrix_ref, out_refs = refs[:parts], refs[parts], refs[parts + 1 :]
-        for hidden_ref, out_ref in zip(hidden_refs, out_refs):
-            out_ref[...] = sum(
+    def kernel(group_ref, *refs):
+        hidden_refs, matrix_ref, out_ref = refs[:parts], refs[parts], refs[parts + 1]
+        for i, hidden_ref in enumerate(hidden_refs):
+            out_ref[group_ref[0] ^ i] = sum(
                 dot_nn(hidden_ref[expert], matrix_ref[expert]) for expert in range(EXP_DEV)
             ).astype(BF16)
 
@@ -343,13 +366,13 @@
         kernel,
         name="expert_outputs",
         grid=(D // FF,),
-        out_shape=tuple(jax.ShapeDtypeStruct((count, D), BF16) for _ in range(parts)),
-        in_specs=[held((EXP_DEV, count, FF))] * parts
-        + [pl.BlockSpec((EXP_DEV, FF, FF), lambda j: (0, j, 0))],
-        out_specs=tuple(pl.BlockSpec((count, FF), lambda j: (0, j)) for _ in range(parts)),
+        out_shape=jax.ShapeDtypeStruct((parts, count, D), BF16),
+        in_specs=[whole(pltpu.SMEM)] + [held((EXP_DEV, count, FF))] * parts
+        + [pl.BlockSpec((EXP_DEV, FF, FF), lambda j: (0, j, 2))],
+        out_specs=pl.BlockSpec((parts, count, FF), lambda j: (0, 0, j)),
         compiler_params=params(dimension_semantics=("arbitrary",)),
-        cost_estimate=cost(30),
-    )(*hidden, matrices)
+        cost_estimate=cost(300),
+    )(group, *hidden, matrices)
 
 
 def attention_places(natural):
@@ -383,14 +406,21 @@
     return values * cosine + partner * sine
 
 
-def softmax_of(queries, keys, length):
-    count = queries.shape[0]
-    scores = dot_nt(queries, keys) * HD ** (-0.5)
-    at_row = lax.broadcasted_iota(jnp.int32, (count, count), 0)
-    at_col = lax.broadcasted_iota(jnp.int32, (count, count), 1)
-    scores = jnp.where((at_col <= at_row) & (at_col < length), scores, -1e30)
+def score_bias(length, first, heads, columns):
+    shape = (heads * BLOCK, columns)
+    at_row = first + lax.broadcasted_iota(jnp.int32, shape, 0) % BLOCK
+    at_col = lax.broadcasted_iota(jnp.int32, shape, 1)
+    return jnp.where((at_col <= at_row) & (at_col < length), 0.0, -1e30)
+
+
+def softmax_of(queries, keys, bias):
+    scores = dot_nt(queries, keys) + bias
     weights = jnp.exp(scores - jnp.max(scores, axis=1, keepdims=True))
     return weights * (1.0 / jnp.sum(weights, axis=1, keepdims=True))
+
+
+def head_rows(ref, head, heads, first):
+    return ref[pl.ds(head, heads), first : first + BLOCK, :].reshape(heads * BLOCK, HD)
 
 
 def unit_rows(values):
@@ -404,8 +434,8 @@
 
     def kernel(length_ref, row_ref, col_ref, tokens_ref, gains_ref, cosine_ref, sine_ref, *refs):
         piece_refs = refs[: len(pieces)]
-        normed_ref, middle_ref, mixed_ref, q_ref, k_ref, v_ref, all_ref = refs[len(pieces) : -3]
-        weights, heads, sems = refs[-3:]
+        normed_ref, middle_ref, mixed_ref, q_ref, k_ref, v_ref, all_ref = refs[len(pieces) : -4]
+        weights, heads, bias_ref, sems = refs[-4:]
         offset = 0
         for piece in piece_refs:
 
@@ -432,6 +462,8 @@
                 column = at + half * LANES
                 if column < QUERY_END + KV * HD:
                     pair = turn(pair, cosine, sine)
+                if column < QUERY_END:
+                    pair = pair * HD ** (-0.5)
                 pair = pair.astype(BF16)
                 if column < QUERY_END:
                     target, head = q_ref, column // HD
@@ -441,15 +473,23 @@
                     target, head = v_ref, (column - QUERY_END - KV * HD) // HD
                 target[head] = pair[:, :HD]
                 target[head + 1] = pair[:, HD:]
-        length = length_ref[0]
+        for first in range(0, count, BLOCK):
+            bias_ref[first // BLOCK] = score_bias(length_ref[0], first, group_size, count)
 
         def attend(j, _):
-            for h in range(group_size):
-                probs = softmax_of(q_ref[j * group_size + h], k_ref[j], length).astype(BF16)
-                heads[j * group_size + h] = dot_nn(probs, v_ref[j]).astype(BF16)
+            for first in range(0, count, BLOCK):
+                seen = slice(0, first + BLOCK)
+                probs = softmax_of(
+                    head_rows(q_ref, j * group_size, group_size, first),
+                    k_ref[j, seen],
+                    bias_ref[first // BLOCK, :, seen],
+                ).astype(BF16)
+                heads[pl.ds(j * group_size, group_size), first : first + BLOCK, :] = (
+                    dot_nn(probs, v_ref[j, seen]).astype(BF16).reshape(group_size, BLOCK, HD)
+                )
             return 0
 
-        lax.fori_loop(0, KV, attend, 0)
+        lax.fori_loop(0, KV, attend, 0, unroll=2)
         for pair in range(H // 2):
             mixed_ref[:, pair * LANES : (pair + 1) * LANES] = jnp.concatenate(
                 [heads[2 * pair], heads[2 * pair + 1]], axis=1
@@ -477,6 +517,7 @@
         scratch_shapes=[
             pltpu.VMEM((D, ALL_COLS * BLOCK), BF16),
             pltpu.VMEM((H, count, HD), BF16),
+            pltpu.VMEM((count // BLOCK, group_size * BLOCK, count), F32),
             pltpu.SemaphoreType.DMA((2,)),
         ],
         compiler_params=params(),
@@ -484,17 +525,16 @@
     )(lengths, block_rows, block_cols, tokens, gains, cosine, sine, *pieces)
 
 
-def attention_back(lengths, positions, tokens, packed, gains, cosine, sine, middle, mixed, q, k, v, w_all, partials, near):
+def attention_back(lengths, positions, tokens, packed, gains, cosine, sine, middle, mixed, q, k, v, w_all, group, own, partials, near):
     count = tokens.shape[0]
     group_size = H // KV
     blocks = positions.shape[0]
-    parts = len(partials)
-
-    def kernel(length_ref, position_ref, tokens_ref, packed_ref, gains_ref, cosine_ref, sine_ref, middle_ref, mixed_ref,
+    parts = partials.shape[0]
+
+    def kernel(group_ref, length_ref, position_ref, tokens_ref, packed_ref, gains_ref, cosine_ref, sine_ref, middle_ref, mixed_ref,
                q_ref, k_ref, v_ref, *refs):
-        partial_refs = refs[:parts]
-        all_ref, input_grad_ref, gain_ref, near_ref, far_ref = refs[parts : parts + 5]
-        weights, stage, grad_heads, grad_columns, sems = refs[parts + 5 :]
+        own_ref, partial_ref, all_ref, input_grad_ref, gain_ref, near_ref, far_ref = refs[:7]
+        weights, stage, grad_heads, grad_columns, bias_ref, sems = refs[7:]
         bring_out = pltpu.make_async_copy(all_ref.at[:, pl.ds(KEYVAL_END, D)], weights.at[:, pl.ds(KEYVAL_END, D)], sems.at[0])
         bring_in = pltpu.make_async_copy(all_ref.at[:, pl.ds(0, KEYVAL_END)], weights.at[:, pl.ds(0, KEYVAL_END)], sems.at[1])
         bring_out.start()
@@ -517,9 +557,9 @@
 
             lax.fori_loop(0, ACROSS * columns, one, 0, unroll=4)
 
-        grad_normed = partial_refs[0][...].astype(F32)
-        for ref in partial_refs[1:]:
-            grad_normed = grad_normed + ref[...].astype(F32)
+        grad_normed = own_ref[...].astype(F32)
+        for i in range(1, parts):
+            grad_normed = grad_normed + partial_ref[group_ref[0] ^ i].astype(F32)
         unit, scale = unit_rows(middle_ref[...])
         gain_ref[1:2, :] = jnp.sum(grad_normed * unit, axis=0, keepdims=True)
         scaled = grad_normed * gains_ref[1:2, :]
@@ -538,27 +578,38 @@
             product = dot_nt(grad_attn, weights[at : at + 2 * LANES, KEYVAL_END:]).astype(BF16)
             for part in range(2 * LANES // HD):
                 grad_heads[at // HD + part] = product[:, part * HD : (part + 1) * HD]
-        length = length_ref[0]
+        for first in range(0, count, BLOCK):
+            bias_ref[first // BLOCK] = score_bias(length_ref[0], first, group_size, count)
 
         def attend(j, _):
-            keys, values = k_ref[j], v_ref[j]
-            grad_keys = jnp.zeros((count, HD), F32)
-            grad_values = jnp.zeros((count, HD), F32)
-            for h in range(group_size):
-                head = j * group_size + h
-                queries, grad_mixed = q_ref[head], grad_heads[head]
-                probs = softmax_of(queries, keys, length)
-                grad_values = grad_values + dot_tn(probs.astype(BF16), grad_mixed)
+            blocks_here = count // BLOCK
+            grad_keys, grad_values = [0.0] * blocks_here, [0.0] * blocks_here
+            for block in range(blocks_here):
+                first = block * BLOCK
+                seen = slice(0, first + BLOCK)
+                keys, values = k_ref[j, seen], v_ref[j, seen]
+                queries = head_rows(q_ref, j * group_size, group_size, first)
+                grad_mixed = head_rows(grad_heads, j * group_size, group_size, first)
+                probs = softmax_of(queries, keys, bias_ref[block, :, seen])
+                more_values = dot_tn(probs.astype(BF16), grad_mixed)
                 grad_probs = dot_nt(grad_mixed, values)
                 inner = jnp.sum(probs * grad_probs, axis=1, keepdims=True)
                 grad_scores = (probs * (grad_probs - inner)).astype(BF16)
-                grad_columns[head] = dot_nn(grad_scores, keys) * HD ** (-0.5)
-                grad_keys = grad_keys + dot_tn(grad_scores, queries)
-            grad_columns[H + j] = grad_keys * HD ** (-0.5)
-            grad_columns[H + KV + j] = grad_values
+                grad_columns[pl.ds(j * group_size, group_size), first : first + BLOCK, :] = (
+                    dot_nn(grad_scores, keys) * HD ** (-0.5)
+                ).reshape(group_size, BLOCK, HD)
+                more_keys = dot_tn(grad_scores, queries)
+                for i in range(block + 1):
+                    rows = slice(i * BLOCK, (i + 1) * BLOCK)
+                    grad_keys[i] = grad_keys[i] + more_keys[rows]
+                    grad_values[i] = grad_values[i] + more_values[rows]
+            for i in range(blocks_here):
+                rows = slice(i * BLOCK, (i + 1) * BLOCK)
+                grad_columns[H + j, rows] = grad_keys[i]
+                grad_columns[H + KV + j, rows] = grad_values[i]
             return 0
 
-        lax.fori_loop(0, KV, attend, 0)
+        lax.fori_loop(0, KV, attend, 0, unroll=2)
         cosine, sine = cosine_ref[...], -sine_ref[...]
         residual = tokens_ref[...].astype(F32)
         unit_one, scale_one = unit_rows(residual)
@@ -596,18 +647,19 @@
             jax.ShapeDtypeStruct((near, BLOCK, BLOCK), BF16),
             jax.ShapeDtypeStruct((max(blocks - near, 1), BLOCK, BLOCK), BF16),
         ),
-        in_specs=[whole(pltpu.SMEM)] * 2 + [vmem] * (10 + parts) + [any_space],
+        in_specs=[whole(pltpu.SMEM)] * 3 + [vmem] * 12 + [any_space],
         out_specs=(vmem, vmem, any_space, any_space),
         scratch_shapes=[
             pltpu.VMEM((D, ALL_COLS * BLOCK), BF16),
             pltpu.VMEM((D, ALL_COLS * BLOCK), BF16),
             pltpu.VMEM((H, count, HD), BF16),
             pltpu.VMEM((H + 2 * KV, count, HD), F32),
+            pltpu.VMEM((count // BLOCK, group_size * BLOCK, count), F32),
             pltpu.SemaphoreType.DMA((3,)),
         ],
         compiler_params=params(),
-        cost_estimate=cost(400),
-    )(lengths, positions, tokens, packed, gains, cosine, sine, middle, mixed, q, k, v, *partials, w_all)
+        cost_estimate=cost(150),
+    )(group, lengths, positions, tokens, packed, gains, cosine, sine, middle, mixed, q, k, v, own, partials, w_all)
 
 
 def split_low(values):
@@ -615,36 +667,40 @@
     return high, (values - high.astype(F32)).astype(BF16)
 
 
+def batched(left, right, left_dim, right_dim):
+    return lax.dot_general(
+        left, right, (((left_dim,), (right_dim,)), ((0,), (0,))), preferred_element_type=F32
+    )
+
+
+def block_mean(values):
+    return jnp.mean(values, axis=(1, 2), keepdims=True)
+
+
 def shampoo(gradient, statistics, inverse_roots, master):
     terms = len(gradient)
     slots = master.shape[0]
-    many = next(n for n in (6, 4, 3, 2, 1) if slots % n == 0)
+    many = max(n for n in range(1, 19) if slots % n == 0 and (n == 1 or slots // n > 1))
 
     def kernel(*refs):
-        term_refs = refs[:terms]
         stats_ref, roots_ref, master_ref, grad_ref, stats_out, master_out = refs[terms:]
-        for i in range(many):
-            total = term_refs[0][i].astype(F32)
-            for ref in term_refs[1:]:
-                total = total + ref[i].astype(F32)
-            low = total.astype(BF16)
-            grad = low.astype(F32)
-            grad_ref[i] = grad
-            scale = 0.5 / (jnp.mean(grad * grad) + 1e-06)
-            stats_out[i, 0] = 0.5 * stats_ref[i, 0] + scale * dot_nt(low, low)
-            stats_out[i, 1] = 0.5 * stats_ref[i, 1] + scale * dot_tn(low, low)
-            left_high, left_low = split_low(roots_ref[i, 0])
-            turned_high, turned_low = split_low(dot_nn(left_high, low) + dot_nn(left_low, low))
-            right_high, right_low = split_low(roots_ref[i, 1])
-            turned = (
-                dot_nn(turned_high, right_high)
-                + dot_nn(turned_low, right_high)
-                + dot_nn(turned_high, right_low)
-            )
-            direction = turned * lax.rsqrt(jnp.mean(turned * turned) + 1e-06)
-            own = master_ref[i]
-            spread = jnp.sqrt(jnp.mean(own * own))
-            master_out[i] = own - STEP_SIZE * spread * direction
+        low = sum(ref[...].astype(F32) for ref in refs[:terms]).astype(BF16)
+        grad = low.astype(F32)
+        grad_ref[...] = grad
+        scale = 0.5 / (block_mean(grad * grad) + 1e-06)
+        stats_out[:, 0] = 0.5 * stats_ref[:, 0] + scale * batched(low, low, 2, 2)
+        stats_out[:, 1] = 0.5 * stats_ref[:, 1] + scale * batched(low, low, 1, 1)
+        left = jnp.concatenate(split_low(roots_ref[:, 0]), axis=2)
+        turned = jnp.concatenate(
+            split_low(batched(left, jnp.concatenate([low, low], axis=1), 2, 1)), axis=2
+        )
+        high, rest = split_low(roots_ref[:, 1])
+        turned = batched(turned, jnp.concatenate([high, high], axis=1), 2, 1) + batched(
+            turned[:, :, :BLOCK], rest, 2, 1
+        )
+        direction = turned * lax.rsqrt(block_mean(turned * turned) + 1e-06)
+        own = master_ref[...]
+        master_out[...] = own - STEP_SIZE * jnp.sqrt(block_mean(own * own)) * direction
 
     one = pl.BlockSpec((many, BLOCK, BLOCK), lambda i: (i, 0, 0))
     two = pl.BlockSpec((many, 2, BLOCK, BLOCK), lambda i: (i, 0, 0, 0))
@@ -677,24 +733,35 @@
     return move(array, [(i, (i + 2 * distance) % size) for i in range(size)])
 
 
+def give_back(parts):
+    return lax.all_to_all(parts, "expert", split_axis=0, concat_axis=0, tiled=True)
+
+
+def spread(array):
+    copies = jnp.broadcast_to(array[None], (lax.axis_size("expert"), *array.shape))
+    return lax.all_to_all(copies, "expert", split_axis=0, concat_axis=0, tiled=True)
+
+
 def two_ways(array, other_first):
     one, two = swap(array, 1), swap(array, 2)
     three = swap(two, 1) if other_first else swap(one, 2)
     return one, two, three
 
 
-def gather_attention(own, deal, before):
+def gather_attention(own, deal, later):
     size, groups = lax.axis_size("shard"), lax.axis_size("expert")
     slots = own.shape[0]
     by_device = deal.reshape(groups, size, slots)
     if groups != 4 or size != 8:
-        return [lax.all_gather(own, ("expert", "shard"), axis=0, tiled=True)], deal, before
+        pieces = [lax.all_gather(own, ("expert", "shard"), axis=0, tiled=True)]
+        return pieces, deal, later
     me_e, me_s = lax.axis_index("expert"), lax.axis_index("shard")
+    lines = [along(own, d) for d in range(1, size // 2)]
+    beside = [swap(own, 1), swap(own, 2)]
+    lines, beside, later = lax.optimization_barrier((lines, beside, later))
+    fours = [jnp.concatenate([own, *beside, swap(beside[0], 2)], axis=0)]
+    fours += [jnp.concatenate([line, *two_ways(line, d % 2 == 0)], axis=0) for d, line in enumerate(lines)]
     pieces, names, far_names = [], [], []
-    lines = [along(own, d) for d in range(1, size // 2)]
-    fours = [jnp.concatenate([own, *two_ways(own, False)], axis=0)]
-    lines, before = lax.optimization_barrier((lines, before))
-    fours += [jnp.concatenate([line, *two_ways(line, d % 2 == 0)], axis=0) for d, line in enumerate(lines)]
     for d, four in enumerate(fours):
         pieces.append(four)
         source = (me_s - 2 * d) % size
@@ -702,7 +769,7 @@
             names.append(by_device[me_e ^ m, source])
             far_names.append(by_device[me_e ^ m, source ^ 1])
     pieces += [sibling(piece) for piece in pieces]
-    return pieces, jnp.concatenate(names + far_names), before
+    return pieces, jnp.concatenate(names + far_names), later
 
 
 def attention_positions(deal, slots):
@@ -715,7 +782,10 @@
     me = lax.axis_index("shard")
     core = (owner % 2) ^ (me % 2)
     distance = ((owner % size) // 2 - me // 2) % (size // 2)
-    return ((((core * groups + mask) * (size // 2)) + distance) * slots + within).astype(jnp.int32)
+    part = distance // (size // 4)
+    first, second = jnp.where(part == 0, mask % 2, mask // 2), jnp.where(part == 0, mask // 2, mask % 2)
+    place = ((core * 2 + 1 - first) * 2 + part) * 2 + second
+    return ((place * (size // 4) + distance % (size // 4)) * slots + within).astype(jnp.int32)
 
 
 def add_low(left, right):
@@ -726,28 +796,41 @@
     size, groups = lax.axis_size("shard"), lax.axis_size("expert")
     if groups != 4 or size != 8:
         return [lax.psum_scatter(near, ("expert", "shard"), scatter_dimension=0, tiled=True)]
-    half = size // 4
-    total = add_low(near, sibling(far)).reshape(groups, 2, half * slots, BLOCK, BLOCK)
-    lines = []
+    quarter = near.shape[0] // 4
+    far_first, far_rest = sibling(far[: 2 * quarter]), sibling(far[2 * quarter :])
+    terms = []
     for part, (first, second) in enumerate(((1, 2), (2, 1))):
-        mine = jnp.concatenate([total[0, part], total[second, part]], axis=0)
-        theirs = jnp.concatenate([total[first, part], total[3, part]], axis=0)
-        mine = add_low(mine, swap(theirs, first))
-        mine, theirs = mine[: half * slots], mine[half * slots :]
-        lines.append(add_low(mine, swap(theirs, second)))
-    terms = [line[i * slots : (i + 1) * slots] for line in lines for i in range(half)]
-    return [terms[0]] + [along(terms[d], d) for d in range(1, size // 2)]
-
-
-def sum_everywhere(values):
+        here = slice(part * quarter, (part + 1) * quarter)
+        there = slice((2 + part) * quarter, (3 + part) * quarter)
+        mine = add_low(near[there], far_rest[here])
+        mine = add_low(mine, swap(add_low(near[here], far_first[here]), first))
+        stay, leave = mine[: quarter // 2], mine[quarter // 2 :]
+        line = add_low(stay, swap(leave, second))
+        terms += [line[i : i + slots] for i in range(0, line.shape[0], slots)]
+    return terms
+
+
+def scatter_line(terms):
+    return terms[:1] + [along(term, d) for d, term in enumerate(terms) if d > 0]
+
+
+def sum_across(values):
     size, groups = lax.axis_size("shard"), lax.axis_size("expert")
     if groups != 4 or size != 8:
         return lax.psum(values, ("expert", "shard"))
-    for mask in (1, 2, 4):
-        values = values + move(values, [(i, i ^ mask) for i in range(size)])
+    values = values + sibling(values)
     for mask in (1, 2):
         values = values + swap(values, mask)
     return values
+
+
+def sum_line(values):
+    size, groups = lax.axis_size("shard"), lax.axis_size("expert")
+    if groups != 4 or size != 8:
+        return values
+    line = jnp.stack([values] + [along(values, d) for d in range(1, size // 2)])
+    place = lax.axis_index("shard") // 2
+    return sum(line[(place - z) % (size // 2)] for z in range(size // 2))
 
 
 def swap(array, mask):
@@ -775,7 +858,6 @@
     row_count = tokens.shape[0]
     groups = lax.axis_size("expert")
     group = lax.axis_index("expert").astype(jnp.int32).reshape(1)
-    expert_all = lax.all_gather(expert_master.astype(BF16), "shard", axis=0, tiled=True)
     places = jnp.arange(row_count)
     valid_rows = places < lengths[0]
     grad_low = jnp.where(valid_rows[:, None], cotangent, jnp.zeros_like(cotangent))
@@ -785,8 +867,14 @@
         for k in range(TOP)
     )
     packed = jnp.concatenate([grad_low, weights_row], axis=1)
-    packed = [swap(packed, m) for m in range(groups)]
-    pieces, natural, packed[1:3] = gather_attention(attn_master.astype(BF16), attn_deal, packed[1:3])
+    half = row_count // 2
+    packed_top = spread(packed[:half])
+    pieces, natural, expert_low = gather_attention(
+        attn_master.astype(BF16), attn_deal, expert_master.astype(BF16)
+    )
+    pieces, packed_bottom = lax.optimization_barrier((pieces, packed[half:]))
+    packed_all = [packed_top, spread(packed_bottom)]
+    expert_all = lax.all_gather(expert_low, "shard", axis=0, tiled=True)
     cosine, sine = rope_tables(jnp.arange(row_count, dtype=F32))
     cosine = jnp.concatenate([cosine] * 4, axis=1)
     sine = jnp.concatenate([-sine, sine] * 2, axis=1)
@@ -796,23 +884,27 @@
     )
     rows = [swap(normed_two, m) for m in range(groups)]
     expert_inverse = inverse_of(expert_deal[0])
-    hidden, both, partials, w_down = expert_front(group, expert_inverse, expert_all, rows, packed)
-    partials = [swap(partial, m) for m, partial in enumerate(partials)]
-    expert_term = expert_weight_grads(expert_inverse, rows, packed, hidden, both)
-    moe_parts = expert_outputs(hidden, w_down)
+    hidden, both, partials, matrices = expert_front(group, expert_inverse, expert_all, rows, packed_all)
+    partials = give_back(partials)
+    expert_term = expert_weight_grads(group, expert_inverse, rows, packed_all, hidden, both)
+    moe_parts = expert_outputs(group, hidden, matrices)
+    own_partial = expert_route(both[0], matrices)
     mixed, moe_parts = lax.optimization_barrier((mixed, moe_parts))
-    moe_parts = [swap(part, m) for m, part in enumerate(moe_parts)]
+    moe_parts = give_back(moe_parts)
     slots = attn_master.shape[0]
     positions = attention_positions(attn_deal, slots)
     near = positions.shape[0] // (2 if groups == 4 and lax.axis_size("shard") == 8 else 1)
     input_grad, gain_parts, near_blocks, far_blocks = attention_back(
-        lengths, positions, tokens, packed[0], norm_gains, cosine, sine, middle, mixed, q, k, v, w_all, partials, near
+        lengths, positions, tokens, packed, norm_gains, cosine, sine, middle, mixed, q, k, v, w_all, group, own_partial, partials, near
     )
     near_blocks, far_blocks, moe_parts = lax.optimization_barrier((near_blocks, far_blocks, moe_parts))
-    output = (middle + sum(part.astype(F32) for part in moe_parts)).astype(BF16)
+    output = (middle + jnp.sum(moe_parts.astype(F32), axis=0)).astype(BF16)
     attn_terms = scatter_attention(near_blocks, far_blocks, slots)
     expert_term = lax.psum_scatter(expert_term, "shard", scatter_dimension=0, tiled=True)
-    gain_grads = sum_everywhere(gain_parts)
+    attn_terms, gain_parts = lax.optimization_barrier((attn_terms, gain_parts))
+    gain_grads = sum_line(sum_across(gain_parts))
+    expert_term, attn_terms, gain_grads = lax.optimization_barrier((expert_term, attn_terms, gain_grads))
+    attn_terms = scatter_line(attn_terms)
     new_gains = norm_gains - STEP_SIZE * gain_grads * lax.rsqrt(
         jnp.mean(gain_grads * gain_grads, axis=-1, keepdims=True) + 1e-06
     )

time: 574 us -> 563 us (0.981); the launches traced: 563 us -> 558 us
  waiting for transfers between devices: 253 us -> 225 us
  starting transfers between devices: 34 us -> 59.3 us
  Pallas kernels: 223 us -> 212 us
  local copies, waits for them, and re-layouts: 12.5 us -> 20.8 us
    ppermute x14 -> x16, waiting for transfers between devices: 100 us -> 51.5 us  [move(): return lax.ppermute(array, 'shard', pairs)]
    all_to_all x0 -> x4, starting transfers between devices: none -> 18.6 us  [the longest x2 10.2 us: give_back(): lax.all_to_all(parts, 'expert', split_axis=0, concat_axis=0, tiled=True)]
    reduce_scatter x1, waiting for transfers between devices: 0.01 us -> 15.2 us  [per_device(): lax.psum_scatter(expert_term, 'shard', scatter_dimension=0, tiled=True)]
    ppermute x14 -> x16, starting transfers between devices: 4.72 us -> 15.8 us  [move(): return lax.ppermute(array, 'shard', pairs)]
    pallas_call x0 -> x1, Pallas kernels: none -> 9.95 us  [expert_route(): pl.pallas_call(kernel, name='expert_route', grid=(D // FF,), out_shape=ja...]
    pallas_call x2, Pallas kernels: 28.6 us -> 20.1 us  [shampoo(): pl.pallas_call(kernel, name='shampoo', grid=(slots // many,), out_shape=(...]
    all_to_all x0 -> x4, waiting for transfers between devices: none -> 7.76 us  [the longest x2 7.76 us: give_back(): lax.all_to_all(parts, 'expert', split_axis=0, concat_axis=0, tiled=True)]
    ppermute x30 -> x21, starting transfers between devices: 29.2 us -> 24.8 us  [swap(): lax.ppermute(array, 'expert', [(i, i ^ mask) for i in range(lax.axis_size...]
  transfers between devices with their start and end apart: 46 -> 43, of which waited for: 23 -> 25; matrix products, arithmetic and copies ran while one was open for 6% -> 8% of each run, Pallas kernels for 20% -> 27%
where the time goes in v3:
time: 563 us; the launch traced here: 558 us
  waiting for transfers between devices  225 us (40%)
  Pallas kernels  212 us (38%)
  starting transfers between devices  59.3 us (11%)
  other arithmetic  25.3 us (4%)
  local copies, waits for them, and re-layouts  20.8 us (4%)
  between operations  15.5 us (3%)
    ppermute x21, waiting for transfers between devices, swap(): lax.ppermute(array, 'expert', [(i, i ^ mask) for i in range(lax.axis_size...  150 us
    pallas_call x1, Pallas kernels, expert_front(): pl.pallas_call(kernel, name='expert_front', grid=(EXP_DEV,), out_shape=[j...  58.9 us
    ppermute x16, waiting for transfers between devices, move(): return lax.ppermute(array, 'shard', pairs)  51.5 us
    pallas_call x1, Pallas kernels, attention_back(): pl.pallas_call(kernel, name='attention_back', out_shape=(jax.ShapeDtypeSt...  45.2 us
    pallas_call x1, Pallas kernels, expert_weight_grads(): pl.pallas_call(kernel, name='expert_weight_grads', grid=(EXP_DEV,), out_s...  38.4 us
    ppermute x21, starting transfers between devices, swap(): lax.ppermute(array, 'expert', [(i, i ^ mask) for i in range(lax.axis_size...  24.8 us
    pallas_call x1, Pallas kernels, attention_front(): pl.pallas_call(kernel, name='attention_front', out_shape=(jax.ShapeDtypeS...  24.6 us
    pallas_call x2, Pallas kernels, shampoo(): pl.pallas_call(kernel, name='shampoo', grid=(slots // many,), out_shape=(...  20.1 us
  transfers between devices with their start and end apart: 43, of which 25 were waited for; matrix products, arithmetic and copies ran while one was open for 8% of the time, Pallas kernels for 27%

profile of v3, /device:TPU:8, one launch (start us, length us, event | category | flops | bytes accessed | tf_op | source)
XLA Modules:
  0.0 557.5 jit_solution(3086807863613324800)
XLA Ops:
  8.4 1.6 collective-permute-start
  11.2 1.9 collective-permute-start.2
  13.1 1.5 collective-permute-start.3
  14.6 1.5 collective-permute-start.4
  16.1 4.2 convert_element_type.85
  20.3 16.1 %collective-permute-done = bf16[12,128,128]{2,1,0:T(8,128)(2,1)S(1)} collective-permute-done((bf16[12,128,128]{2,1,0:T(8,128)(2,1)S(1)}, bf16[12,128,128]{2,1,0:T(8,128)(2,1)S(1)}, u32[]{:S(2)}, u32[]{:S(2)}) %collective-permute-start) | collective-permute-done | bytes 393248 | tf_op jit(solution)/shard_map/ppermute | solution.py:724
  36.4 7.3 %collective-permute-done.1 = bf16[12,128,128]{2,1,0:T(8,128)(2,1)} collective-permute-done((bf16[12,128,128]{2,1,0:T(8,128)(2,1)S(1)}, bf16[12,128,128]{2,1,0:T(8,128)(2,1)}, u32[]{:S(2)}, u32[]{:S(2)}) %collective-permute-start.1) | collective-permute-done | bytes 393248 | tf_op jit(solution)/shard_map/ppermute | solution.py:724
  43.7 1.8 collective-permute-done.2
  47.7 1.6 collective-permute-start.9
  49.3 1.5 collective-permute-start.5
  50.9 1.6 broadcast_in_dim.157
  52.5 3.7 all-to-all-start
  56.3 2.0 collective-permute-start.10
  58.3 1.5 collective-permute-start.6
  60.3 2.1 constant_dynamic-update-slice_fusion.3
  63.4 1.8 constant_dynamic-update-slice_fusion.6
  65.1 10.1 %collective-permute-done.5 = bf16[12,128,128]{2,1,0:T(8,128)(2,1)} collective-permute-done((bf16[12,128,128]{2,1,0:T(8,128)(2,1)}, bf16[12,128,128]{2,1,0:T(8,128)(2,1)}, u32[]{:S(2)}, u32[]{:S(2)}) %collective-permute-start.5) | collective-permute-done | bytes 393248 | tf_op jit(solution)/shard_map/ppermute | solution.py:839
  75.3 1.5 collective-permute-start.13
  76.8 2.5 pad_maximum_fusion.1.refs_0_
  79.3 16.7 %collective-permute-done.6 = bf16[12,128,128]{2,1,0:T(8,128)(2,1)S(1)} collective-permute-done((bf16[12,128,128]{2,1,0:T(8,128)(2,1)}, bf16[12,128,128]{2,1,0:T(8,128)(2,1)S(1)}, u32[]{:S(2)}, u32[]{:S(2)}) %collective-permute-start.6) | collective-permute-done | bytes 393248 | tf_op jit(solution)/shard_map/ppermute | solution.py:839
  96.7 9.0 %collective-permute-done.7 = bf16[12,128,128]{2,1,0:T(8,128)(2,1)S(1)} collective-permute-done((bf16[12,128,128]{2,1,0:T(8,128)(2,1)}, bf16[12,128,128]{2,1,0:T(8,128)(2,1)S(1)}, u32[]{:S(2)}, u32[]{:S(2)}) %collective-permute-start.7) | collective-permute-done | bytes 393248 | tf_op jit(solution)/shard_map/ppermute | solution.py:839
  105.7 1.5 collective-permute-start.11
  108.6 5.6 %collective-permute-done.13 = bf16[12,128,128]{2,1,0:T(8,128)(2,1)S(1)} collective-permute-done((bf16[12,128,128]{2,1,0:T(8,128)(2,1)S(1)}, bf16[12,128,128]{2,1,0:T(8,128)(2,1)S(1)}, u32[]{:S(2)}, u32[]{:S(2)}) %collective-permute-start.13) | collective-permute-done | bytes 393248 | tf_op jit(solution)/shard_map/ppermute | solution.py:839
  116.5 4.8 collective-permute-done.11
  123.4 1.5 collective-permute-done.14
  128.6 1.8 collective-permute-done.18.refs_7_
  130.3 1.8 broadcast_in_dim.158
  132.7 4.7 all-to-all-start.1
  137.4 24.6 %attention_front.1 = (bf16[384,1536]{1,0:T(8,128)(2,1)}, f32[384,1536]{1,0:T(8,128)}, bf16[384,1536]{1,0:T(8,128)(2,1)}, bf16[24,384,64]{2,1,0:T(8,128)(2,1)}, b...) custom-call(s32[1]{0:T(128)} %copy.33.length_ref, ...), custom_call_target="tpu_custom_call" | custom-call | flops 115000000512 | bytes 1024 | tf_op jit(solution)/shard_map/attention_front/pallas_call | solution.py:503
  162.0 2.2 collective-permute-start.19
  164.2 1.5 collective-permute-start.20
  167.4 2.5 pad_maximum_fusion.packed_ref
  169.8 24.0 %collective-permute-done.19.refs_1_ = bf16[384,1536]{1,0:T(8,128)(2,1)} collective-permute-done((bf16[384,1536]{1,0:T(8,128)(2,1)}, bf16[384,1536]{1,0:T(8,128)(2,1)}, u32[]{:S(2)}, u32[]{:S(2)}) %collective-permute-start.19) | collective-permute-done | bytes 1179680 | tf_op jit(solution)/shard_map/ppermute | solution.py:839
  193.9 25.4 %collective-permute-done.21.refs_3_ = bf16[384,1536]{1,0:T(8,128)(2,1)} collective-permute-done((bf16[384,1536]{1,0:T(8,128)(2,1)}, bf16[384,1536]{1,0:T(8,128)(2,1)}, u32[]{:S(2)}, u32[]{:S(2)}) %collective-permute-start.21) | collective-permute-done | bytes 1179680 | tf_op jit(solution)/shard_map/ppermute | solution.py:839
  219.3 58.9 %expert_front.1 = (bf16[4,384,512]{2,1,0:T(8,128)(2,1)}, bf16[4,384,512]{2,1,0:T(8,128)(2,1)}, bf16[4,384,512]{2,1,0:T(8,128)(2,1)}, bf16[4,384,512]{2,1,0:T(8,1...) custom-call(s32[1]{0:T(128)} %bitcast.33.group_ref, ...), custom_call_target="tpu_custom_call" | custom-call | flops 115000000512 | bytes 1024 | tf_op jit(solution)/shard_map/expert_front/pallas_call | solution.py:196
  278.2 5.0 all-to-all-start.2
  283.2 38.4 %expert_weight_grads.1 = bf16[576,128,128]{2,1,0:T(8,128)(2,1)} custom-call(s32[1]{0:T(128)} %bitcast.33.group_ref, s32[576]{0:T(1024)} %select_reduce_fusion.inverse_ref.position_ref, bf16[384,1536]{1,0:T(8,128)(2,1)} %get-tuple-element.89.refs_0_, bf16[384,1536]{1,0:T(8,128)(2,1)} %collective-permute-done.19.refs_1_, ...), custom_call_target="tpu_custom_call" | custom-call | flops 115000000512 | bytes 1024 | tf_op jit(solution)/shard_map/expert_weight_grads/pallas_call | solution.py:310
  321.6 14.9 %expert_outputs.1 = bf16[4,384,1536]{2,1,0:T(8,128)(2,1)} custom-call(s32[1]{0:T(128)} %bitcast.33.group_ref, bf16[4,384,512]{2,1,0:T(8,128)(2,1)} %get-tuple-element.91.refs_0_.refs_6_, bf16[4,384,512]{2,1,0:T(8,128)(2,1)} %get-tuple-element.92.refs_1_.refs_7_, bf16[4,384,512]{2,1,0:T(8,128)(2,1)} %get-tuple-element.93.refs_2_.refs_8_, ...), custom_call_target="tpu_custom_call" | custom-call | flops 344999985152 | bytes 1024 | tf_op jit(solution)/shard_map/expert_outputs/pallas_call | solution.py:365
  336.5 9.9 %expert_route.1.refs_0_ = bf16[384,1536]{1,0:T(8,128)(2,1)} custom-call(bf16[4,384,1024]{2,1,0:T(8,128)(2,1)} %get-tuple-element.100.both_ref.refs_10_, bf16[4,1536,1536]{2,1,0:T(8,128)(2,1)} %get-tuple-element.95.refs_4_.matrix_ref), custom_call_target="tpu_custom_call" | custom-call | flops 4600000000 | bytes 1024 | tf_op jit(solution)/shard_map/expert_route/pallas_call | solution.py:339
  346.5 5.2 all-to-all-start.3
  351.7 45.2 %attention_back.1 = (f32[384,1536]{1,0:T(8,128)}, f32[2,1536]{1,0:T(2,128)}, bf16[192,128,128]{2,1,0:T(8,128)(2,1)}, bf16[192,128,128]{2,1,0:T(8,128)(2,1)}) custom-call(s32[1]{0:T(128)} %bitcast.33.group_ref, s32[1]{0:T(128)} %copy.33.length_ref, s32[384]{0:T(512)} %fusion.40.position_ref, bf16[384,1536]{1,0:T(8,128)(2,1)} %tokens_ref.3, ...), custom_call_target="tpu_custom_call" | custom-call | flops 172499992576 | bytes 1024 | tf_op jit(solution)/shard_map/attention_back/pallas_call | solution.py:641
  396.8 7.8 %all-to-all-done.3 = bf16[4,384,1536]{2,1,0:T(8,128)(2,1)} async-done(((bf16[4,384,1536]{2,1,0:T(8,128)(2,1)}), bf16[4,384,1536]{2,1,0:T(8,128)(2,1)}, u32[]{:S(2)}, u32[]{:S(2)}) %all-to-all-start.3) | async-done | bytes 4718624 | tf_op jit(solution)/shard_map/all_to_all | solution.py:737
  404.6 4.4 fusion.86
  409.5 5.1 collective-permute-done.23
  414.7 1.3 add_convert_fusion.1
  416.1 1.5 collective-permute-start.24
  418.1 1.5 collective-permute-done.22
  419.6 32.9 %collective-permute-done.24 = bf16[48,128,128]{2,1,0:T(8,128)(2,1)S(1)} collective-permute-done((bf16[48,128,128]{2,1,0:T(8,128)(2,1)S(1)}, bf16[48,128,128]{2,1,0:T(8,128)(2,1)S(1)}, u32[]{:S(2)}, u32[]{:S(2)}) %collective-permute-start.24) | collective-permute-done | bytes 1572896 | tf_op jit(solution)/shard_map/ppermute | solution.py:839
  453.7 2.0 add_convert_fusion
  456.5 1.5 collective-permute-start.25
  458.0 16.3 %collective-permute-done.27 = bf16[24,128,128]{2,1,0:T(8,128)(2,1)S(1)} collective-permute-done((bf16[24,128,128]{2,1,0:T(8,128)(2,1)S(1)}, bf16[24,128,128]{2,1,0:T(8,128)(2,1)S(1)}, u32[]{:S(2)}, u32[]{:S(2)}) %collective-permute-start.27) | collective-permute-done | bytes 786464 | tf_op jit(solution)/shard_map/ppermute | solution.py:839
  477.2 1.5 collective-permute-start.29
  478.7 2.3 collective-permute-done.29
  481.0 1.5 collective-permute-start.30
  482.5 3.5 convert_reduce_fusion
  486.1 2.3 collective-permute-start.32
  488.4 1.9 collective-permute-start.33
  492.7 15.2 %reduce-scatter.2.cloned.1.call-done.refs_0_ = bf16[72,128,128]{2,1,0:T(8,128)(2,1)} async-done(((bf16[576,128,128]{2,1,0:T(8,128)(2,1)}), bf16[72,128,128]{2,1,0:T(8,128)(2,1)}) %reduce-scatter.2.cloned.1.call-update) | async-done | bytes 2359312 | tf_op jit(solution)/shard_map/reduce_scatter | solution.py:903
  507.9 2.0 collective-permute-start.34
  510.0 3.7 collective-permute-start.35
  513.8 15.7 %shampoo.2 = (f32[72,128,128]{2,1,0:T(8,128)}, f32[72,2,128,128]{3,2,1,0:T(8,128)}, f32[72,128,128]{2,1,0:T(8,128)}) custom-call(bf16[72,128,128]{2,1,0:T(8,128)(2,1)} %reduce-scatter.2.cloned.1.call-done.refs_0_, f32[72,2,128,128]{3,2,1,0:T(8,128)} %refs_1_.1, f32[72,2,128,128]{3,2,1,0:T(8,128)} %refs_2_.1, f32[72,128,128]{2,1,0:T(8,128)} %refs_3_.1), custom_call_target="tpu_custom_call" | custom-call | flops 11500000256 | bytes 1024 | tf_op jit(solution)/shard_map/shampoo/pallas_call | solution.py:707
  530.3 14.2 %collective-permute-done.35.refs_2_ = bf16[12,128,128]{2,1,0:T(8,128)(2,1)} collective-permute-done((bf16[12,128,128]{2,1,0:T(8,128)(2,1)S(1)}, bf16[12,128,128]{2,1,0:T(8,128)(2,1)}, u32[]{:S(2)}, u32[]{:S(2)}) %collective-permute-start.35) | collective-permute-done | bytes 393248 | tf_op jit(solution)/shard_map/ppermute | solution.py:724
  544.5 1.5 collective-permute-done.36.refs_3_
  546.0 4.4 shampoo.3
  (126 shorter events, 27.0 us)
Async XLA Ops:
  7.2 212.1 %all-gather.2.cloned.1.call-start = ((), (), s32[]{:S(2)}) async-start(), calls=%async_computation.5 | async-start | bytes 21233664 | tf_op jit(solution)/shard_map/all_gather | solution.py:877
  8.4 11.9 %copy-start.3 = (bf16[12,128,128]{2,1,0:T(8,128)(2,1)}, bf16[12,128,128]{2,1,0:T(8,128)(2,1)S(1)}, u32[]{:S(2)}) copy-start(bf16[12,128,128]{2,1,0:T(8,128)(2,1)S(1)} %convert_element_type.84) | copy-start | bytes 1179652
  8.4 28.0 %collective-permute-start = (bf16[12,128,128]{2,1,0:T(8,128)(2,1)S(1)}, bf16[12,128,128]{2,1,0:T(8,128)(2,1)S(1)}, u32[]{:S(2)}, u32[]{:S(2)}) collective-permute-start(bf16[12,128,128]{2,1,0:T(8,128)(2,1)S(1)} %convert_element_type.84), channel_id=1, source_target_pairs={{0,2},{1,3},{2,4},{3,5},{4,6},{5,7},{6,0},{7,1},{8,10},{9,11},{10,... | collective-permute-start | bytes 1179656 | tf_op jit(solution)/shard_map/ppermute | solution.py:724
  10.1 33.7 %collective-permute-start.1 = (bf16[12,128,128]{2,1,0:T(8,128)(2,1)S(1)}, bf16[12,128,128]{2,1,0:T(8,128)(2,1)}, u32[]{:S(2)}, u32[]{:S(2)}) collective-permute-start(bf16[12,128,128]{2,1,0:T(8,128)(2,1)S(1)} %convert_element_type.84), channel_id=1, source_target_pairs={{0,4},{1,5},{2,6},{3,7},{4,0},{5,1},{6,2},{7,3},{8,12},{9,13},{10,... | collective-permute-start | bytes 1179656 | tf_op jit(solution)/shard_map/ppermute | solution.py:724
  11.2 34.4 %collective-permute-start.2 = (bf16[12,128,128]{2,1,0:T(8,128)(2,1)S(1)}, bf16[12,128,128]{2,1,0:T(8,128)(2,1)S(1)}, u32[]{:S(2)}, u32[]{:S(2)}) collective-permute-start(bf16[12,128,128]{2,1,0:T(8,128)(2,1)S(1)} %convert_element_type.84), channel_id=1, source_target_pairs={{0,6},{1,7},{2,0},{3,1},{4,2},{5,3},{6,4},{7,5},{8,14},{9,15},{10,... | collective-permute-start | bytes 1179656 | tf_op jit(solution)/shard_map/ppermute | solution.py:724
  13.1 32.4 %collective-permute-start.3 = (bf16[12,128,128]{2,1,0:T(8,128)(2,1)S(1)}, bf16[12,128,128]{2,1,0:T(8,128)(2,1)}, u32[]{:S(2)}, u32[]{:S(2)}) collective-permute-start(bf16[12,128,128]{2,1,0:T(8,128)(2,1)S(1)} %convert_element_type.84), channel_id=1, source_target_pairs={{0,8},{8,0},{16,24},{24,16},{1,9},{9,1},{17,25},{25,17},{2,10},{10... | collective-permute-start | bytes 1179656 | tf_op jit(solution)/shard_map/ppermute | solution.py:839
  14.6 30.9 %collective-permute-start.4 = (bf16[12,128,128]{2,1,0:T(8,128)(2,1)S(1)}, bf16[12,128,128]{2,1,0:T(8,128)(2,1)S(1)}, u32[]{:S(2)}, u32[]{:S(2)}) collective-permute-start(bf16[12,128,128]{2,1,0:T(8,128)(2,1)S(1)} %convert_element_type.84), channel_id=1, source_target_pairs={{0,16},{8,24},{16,0},{24,8},{1,17},{9,25},{17,1},{25,9},{2,18},{10... | collective-permute-start | bytes 1179656 | tf_op jit(solution)/shard_map/ppermute | solution.py:839
  20.3 25.9 %copy-start.12 = (bf16[384,8]{0,1:T(8,128)(2,1)S(1)}, bf16[384,8]{0,1:T(8,128)(2,1)}, u32[]{:S(2)}) copy-start(bf16[384,8]{0,1:T(8,128)(2,1)} %param.18) | copy-start | bytes 18436
  20.3 26.0 %copy-start.13 = (s32[384,8]{0,1:T(8,128)S(1)}, s32[384,8]{0,1:T(8,128)}, u32[]{:S(2)}) copy-start(s32[384,8]{0,1:T(8,128)} %param.17) | copy-start | bytes 36868
  20.3 27.2 %copy-start.5 = (bf16[384,1536]{1,0:T(8,128)(2,1)S(1)}, bf16[384,1536]{1,0:T(8,128)(2,1)}, u32[]{:S(2)}) copy-start(bf16[384,1536]{1,0:T(8,128)(2,1)} %param.15) | copy-start | bytes 3538948
  36.4 16.1 %copy-start.10 = (bf16[12,128,128]{2,1,0:T(8,128)(2,1)}, bf16[12,128,128]{2,1,0:T(8,128)(2,1)S(1)}, u32[]{:S(2)}) copy-start(bf16[12,128,128]{2,1,0:T(8,128)(2,1)S(1)} %collective-permute-done) | copy-start | bytes 1179652
  45.5 2.1 copy-start.8
  45.5 2.1 copy-start.6
  47.7 3.1 copy-start
  47.7 15.5 %collective-permute-start.9 = (bf16[12,128,128]{2,1,0:T(8,128)(2,1)}, bf16[12,128,128]{2,1,0:T(8,128)(2,1)}, u32[]{:S(2)}, u32[]{:S(2)}) collective-permute-start(bf16[12,128,128]{2,1,0:T(8,128)(2,1)} %collective-permute-done.1), channel_id=1, source_target_pairs={{0,8},{8,0},{16,24},{24,16},{1,9},{9,1},{17,25},{25,17},{2,10},{10... | collective-permute-start | bytes 1179656 | tf_op jit(solution)/shard_map/ppermute | solution.py:839
  49.3 26.0 %collective-permute-start.5 = (bf16[12,128,128]{2,1,0:T(8,128)(2,1)}, bf16[12,128,128]{2,1,0:T(8,128)(2,1)}, u32[]{:S(2)}, u32[]{:S(2)}) collective-permute-start(bf16[12,128,128]{2,1,0:T(8,128)(2,1)} %collective-permute-done.3), channel_id=1, source_target_pairs={{0,16},{8,24},{16,0},{24,8},{1,17},{9,25},{17,1},{25,9},{2,18},{10... | collective-permute-start | bytes 1179656 | tf_op jit(solution)/shard_map/ppermute | solution.py:839
  52.5 77.8 %all-to-all-start = ((bf16[4,192,1664]{2,1,0:T(8,128)(2,1)}), bf16[4,192,1664]{2,1,0:T(8,128)(2,1)S(1)}, u32[]{:S(2)}, u32[]{:S(2)}) async-start(bf16[4,192,1664]{2,1,0:T(8,128)(2,1)} %broadcast_in_dim.157), calls=%async_computation | async-start | bytes 5111808 | tf_op jit(solution)/shard_map/all_to_all | solution.py:742
  56.3 6.1 %copy-start.9 = (bf16[12,128,128]{2,1,0:T(8,128)(2,1)S(1)}, bf16[12,128,128]{2,1,0:T(8,128)(2,1)}, u32[]{:S(2)}) copy-start(bf16[12,128,128]{2,1,0:T(8,128)(2,1)} %copy-done.8) | copy-start | bytes 1179652
  56.3 20.5 %copy-start.4 = (bf16[12,128,128]{2,1,0:T(8,128)(2,1)S(1)}, bf16[12,128,128]{2,1,0:T(8,128)(2,1)}, u32[]{:S(2)}) copy-start(bf16[12,128,128]{2,1,0:T(8,128)(2,1)} %copy-done.3) | copy-start | bytes 1179652
  56.3 20.5 %copy-start.7 = (bf16[12,128,128]{2,1,0:T(8,128)(2,1)S(1)}, bf16[12,128,128]{2,1,0:T(8,128)(2,1)}, u32[]{:S(2)}) copy-start(bf16[12,128,128]{2,1,0:T(8,128)(2,1)} %copy-done.6) | copy-start | bytes 1179652
  56.3 59.4 %collective-permute-start.10 = (bf16[12,128,128]{2,1,0:T(8,128)(2,1)}, bf16[12,128,128]{2,1,0:T(8,128)(2,1)S(1)}, u32[]{:S(2)}, u32[]{:S(2)}) collective-permute-start(bf16[12,128,128]{2,1,0:T(8,128)(2,1)} %collective-permute-done.1), channel_id=1, source_target_pairs={{0,16},{8,24},{16,0},{24,8},{1,17},{9,25},{17,1},{25,9},{2,18},{10... | collective-permute-start | bytes 1179656 | tf_op jit(solution)/shard_map/ppermute | solution.py:839
  58.3 37.7 %collective-permute-start.6 = (bf16[12,128,128]{2,1,0:T(8,128)(2,1)}, bf16[12,128,128]{2,1,0:T(8,128)(2,1)S(1)}, u32[]{:S(2)}, u32[]{:S(2)}) collective-permute-start(bf16[12,128,128]{2,1,0:T(8,128)(2,1)} %copy-done.10), channel_id=1, source_target_pairs={{0,8},{8,0},{16,24},{24,16},{1,9},{9,1},{17,25},{25,17},{2,10},{10... | collective-permute-start | bytes 1179656 | tf_op jit(solution)/shard_map/ppermute | solution.py:839
  59.7 46.0 %collective-permute-start.7 = (bf16[12,128,128]{2,1,0:T(8,128)(2,1)}, bf16[12,128,128]{2,1,0:T(8,128)(2,1)S(1)}, u32[]{:S(2)}, u32[]{:S(2)}) collective-permute-start(bf16[12,128,128]{2,1,0:T(8,128)(2,1)} %copy-done.10), channel_id=1, source_target_pairs={{0,16},{8,24},{16,0},{24,8},{1,17},{9,25},{17,1},{25,9},{2,18},{10... | collective-permute-start | bytes 1179656 | tf_op jit(solution)/shard_map/ppermute | solution.py:839
  63.2 44.8 %collective-permute-start.12 = (bf16[12,128,128]{2,1,0:T(8,128)(2,1)S(1)}, bf16[12,128,128]{2,1,0:T(8,128)(2,1)S(1)}, u32[]{:S(2)}, u32[]{:S(2)}) collective-permute-start(bf16[12,128,128]{2,1,0:T(8,128)(2,1)S(1)} %copy-done.9), channel_id=1, source_target_pairs={{0,8},{8,0},{16,24},{24,16},{1,9},{9,1},{17,25},{25,17},{2,10},{10... | collective-permute-start | bytes 1179656 | tf_op jit(solution)/shard_map/ppermute | solution.py:839
  75.3 38.9 %collective-permute-start.13 = (bf16[12,128,128]{2,1,0:T(8,128)(2,1)S(1)}, bf16[12,128,128]{2,1,0:T(8,128)(2,1)S(1)}, u32[]{:S(2)}, u32[]{:S(2)}) collective-permute-start(bf16[12,128,128]{2,1,0:T(8,128)(2,1)S(1)} %copy-done.9), channel_id=1, source_target_pairs={{0,16},{8,24},{16,0},{24,8},{1,17},{9,25},{17,1},{25,9},{2,18},{10... | collective-permute-start | bytes 1179656 | tf_op jit(solution)/shard_map/ppermute | solution.py:839
  95.9 32.6 %collective-permute-start.15 = (bf16[48,128,128]{2,1,0:T(8,128)(2,1)}, bf16[48,128,128]{2,1,0:T(8,128)(2,1)}, u32[]{:S(2)}, u32[]{:S(2)}) collective-permute-start(bf16[48,128,128]{2,1,0:T(8,128)(2,1)} %pad_maximum_fusion.1.refs_0_), channel_id=1, source_target_pairs={{0,1},{1,0},{2,3},{3,2},{4,5},{5,4},{6,7},{7,6},{8,9},{9,8},{10,11... | collective-permute-start | bytes 4718600 | tf_op jit(solution)/shard_map/ppermute | solution.py:724
  105.7 15.6 %collective-permute-start.11 = (bf16[12,128,128]{2,1,0:T(8,128)(2,1)}, bf16[12,128,128]{2,1,0:T(8,128)(2,1)S(1)}, u32[]{:S(2)}, u32[]{:S(2)}) collective-permute-start(bf16[12,128,128]{2,1,0:T(8,128)(2,1)} %collective-permute-done.9), channel_id=1, source_target_pairs={{0,16},{8,24},{16,0},{24,8},{1,17},{9,25},{17,1},{25,9},{2,18},{10... | collective-permute-start | bytes 1179656 | tf_op jit(solution)/shard_map/ppermute | solution.py:839
  108.0 14.1 %collective-permute-start.8 = (bf16[12,128,128]{2,1,0:T(8,128)(2,1)S(1)}, bf16[12,128,128]{2,1,0:T(8,128)(2,1)S(1)}, u32[]{:S(2)}, u32[]{:S(2)}) collective-permute-start(bf16[12,128,128]{2,1,0:T(8,128)(2,1)S(1)} %collective-permute-done.7), channel_id=1, source_target_pairs={{0,8},{8,0},{16,24},{24,16},{1,9},{9,1},{17,25},{25,17},{2,10},{10... | collective-permute-start | bytes 1179656 | tf_op jit(solution)/shard_map/ppermute | solution.py:839
  114.1 10.7 %collective-permute-start.14 = (bf16[12,128,128]{2,1,0:T(8,128)(2,1)S(1)}, bf16[12,128,128]{2,1,0:T(8,128)(2,1)S(1)}, u32[]{:S(2)}, u32[]{:S(2)}) collective-permute-start(bf16[12,128,128]{2,1,0:T(8,128)(2,1)S(1)} %collective-permute-done.13), channel_id=1, source_target_pairs={{0,8},{8,0},{16,24},{24,16},{1,9},{9,1},{17,25},{25,17},{2,10},{10... | collective-permute-start | bytes 1179656 | tf_op jit(solution)/shard_map/ppermute | solution.py:839
  115.7 9.9 %copy-start.16 = (s32[384]{0:T(512)S(1)}, s32[384]{0:T(512)}, u32[]{:S(2)}) copy-start(s32[384]{0:T(512)} %param.23) | copy-start | bytes 4612
  122.1 6.5 %collective-permute-start.17 = (bf16[48,128,128]{2,1,0:T(8,128)(2,1)}, bf16[48,128,128]{2,1,0:T(8,128)(2,1)}, u32[]{:S(2)}, u32[]{:S(2)}) collective-permute-start(bf16[48,128,128]{2,1,0:T(8,128)(2,1)} %constant_dynamic-update-slice_fusion.4.refs_2_), channel_id=1, source_target_pairs={{0,1},{1,0},{2,3},{3,2},{4,5},{5,4},{6,7},{7,6},{8,9},{9,8},{10,11... | collective-permute-start | bytes 4718600 | tf_op jit(solution)/shard_map/ppermute | solution.py:724
  122.9 5.7 %collective-permute-start.16 = (bf16[48,128,128]{2,1,0:T(8,128)(2,1)}, bf16[48,128,128]{2,1,0:T(8,128)(2,1)}, u32[]{:S(2)}, u32[]{:S(2)}) collective-permute-start(bf16[48,128,128]{2,1,0:T(8,128)(2,1)} %constant_dynamic-update-slice_fusion.refs_1_), channel_id=1, source_target_pairs={{0,1},{1,0},{2,3},{3,2},{4,5},{5,4},{6,7},{7,6},{8,9},{9,8},{10,11... | collective-permute-start | bytes 4718600 | tf_op jit(solution)/shard_map/ppermute | solution.py:724
  125.7 4.7 collective-permute-start.18
  130.3 2.3 copy-start.1
  132.7 86.6 %all-to-all-start.1 = ((bf16[4,192,1664]{2,1,0:T(8,128)(2,1)}), bf16[4,192,1664]{2,1,0:T(8,128)(2,1)}, u32[]{:S(2)}, u32[]{:S(2)}) async-start(bf16[4,192,1664]{2,1,0:T(8,128)(2,1)} %broadcast_in_dim.158), calls=%async_computation.1 | async-start | bytes 5111808 | tf_op jit(solution)/shard_map/all_to_all | solution.py:742
  137.4 28.3 %copy-start.17 = (s32[1,576]{1,0:T(1,128)S(1)}, s32[1,576]{1,0:T(1,128)}, u32[]{:S(2)}) copy-start(s32[1,576]{1,0:T(1,128)} %param.27) | copy-start | bytes 6916
  162.0 31.9 %collective-permute-start.19 = (bf16[384,1536]{1,0:T(8,128)(2,1)}, bf16[384,1536]{1,0:T(8,128)(2,1)}, u32[]{:S(2)}, u32[]{:S(2)}) collective-permute-start(bf16[384,1536]{1,0:T(8,128)(2,1)} %get-tuple-element.89.refs_0_), channel_id=1, source_target_pairs={{0,8},{8,0},{16,24},{24,16},{1,9},{9,1},{17,25},{25,17},{2,10},{10... | collective-permute-start | bytes 3538952 | tf_op jit(solution)/shard_map/ppermute | solution.py:839
  164.2 29.7 %collective-permute-start.20 = (bf16[384,1536]{1,0:T(8,128)(2,1)}, bf16[384,1536]{1,0:T(8,128)(2,1)}, u32[]{:S(2)}, u32[]{:S(2)}) collective-permute-start(bf16[384,1536]{1,0:T(8,128)(2,1)} %get-tuple-element.89.refs_0_), channel_id=1, source_target_pairs={{0,16},{8,24},{16,0},{24,8},{1,17},{9,25},{17,1},{25,9},{2,18},{10... | collective-permute-start | bytes 3538952 | tf_op jit(solution)/shard_map/ppermute | solution.py:839
  165.6 53.6 %collective-permute-start.21 = (bf16[384,1536]{1,0:T(8,128)(2,1)}, bf16[384,1536]{1,0:T(8,128)(2,1)}, u32[]{:S(2)}, u32[]{:S(2)}) collective-permute-start(bf16[384,1536]{1,0:T(8,128)(2,1)} %get-tuple-element.89.refs_0_), channel_id=1, source_target_pairs={{0,24},{8,16},{16,8},{24,0},{1,25},{9,17},{17,9},{25,1},{2,26},{10... | collective-permute-start | bytes 3538952 | tf_op jit(solution)/shard_map/ppermute | solution.py:839
  278.2 68.3 %all-to-all-start.2 = ((bf16[4,384,1536]{2,1,0:T(8,128)(2,1)}), bf16[4,384,1536]{2,1,0:T(8,128)(2,1)}, u32[]{:S(2)}, u32[]{:S(2)}) async-start(bf16[4,384,1536]{2,1,0:T(8,128)(2,1)} %get-tuple-element.101), calls=%async_computation.2 | async-start | bytes 9437184 | tf_op jit(solution)/shard_map/all_to_all | solution.py:737
  283.1 224.8 %reduce-scatter.2.cloned.1.call-start = ((), (), s32[]{:S(2)}) async-start(), calls=%async_computation.6 | async-start | bytes 21233664 | tf_op jit(solution)/shard_map/reduce_scatter | solution.py:903
  346.5 58.1 %all-to-all-start.3 = ((bf16[4,384,1536]{2,1,0:T(8,128)(2,1)}), bf16[4,384,1536]{2,1,0:T(8,128)(2,1)}, u32[]{:S(2)}, u32[]{:S(2)}) async-start(bf16[4,384,1536]{2,1,0:T(8,128)(2,1)} %expert_outputs.1), calls=%async_computation.3 | async-start | bytes 9437184 | tf_op jit(solution)/shard_map/all_to_all | solution.py:737
  404.6 10.1 %slice-start = ((s8[6291456]{0:T(1024)(128)(4,1)}), s8[4194304]{0:T(1024)(128)(4,1)S(1)}, s32[]{:S(2)}) async-start(s8[6291456]{0:T(1024)(128)(4,1)} %bitcast.73), calls=%async_computation.7 | async-start | bytes 8388608
  404.6 10.1 %slice-start.1 = ((s8[6291456]{0:T(1024)(128)(4,1)}), s8[2097152]{0:T(1024)(128)(4,1)S(1)}, s32[]{:S(2)}) async-start(s8[6291456]{0:T(1024)(128)(4,1)} %bitcast.73), calls=%async_computation.8 | async-start | bytes 4194304
  409.0 5.7 %collective-permute-start.23 = (bf16[96,128,128]{2,1,0:T(8,128)(2,1)S(1)}, bf16[96,128,128]{2,1,0:T(8,128)(2,1)S(1)}, u32[]{:S(2)}, u32[]{:S(2)}) collective-permute-start(bf16[96,128,128]{2,1,0:T(8,128)(2,1)S(1)} %get-tuple-element.157), channel_id=1, source_target_pairs={{0,1},{1,0},{2,3},{3,2},{4,5},{5,4},{6,7},{7,6},{8,9},{9,8},{10,11... | collective-permute-start | bytes 9437192 | tf_op jit(solution)/shard_map/ppermute | solution.py:724
  409.1 10.6 %collective-permute-start.22 = (bf16[96,128,128]{2,1,0:T(8,128)(2,1)S(1)}, bf16[96,128,128]{2,1,0:T(8,128)(2,1)S(1)}, u32[]{:S(2)}, u32[]{:S(2)}) collective-permute-start(bf16[96,128,128]{2,1,0:T(8,128)(2,1)S(1)} %get-tuple-element.156), channel_id=1, source_target_pairs={{0,1},{1,0},{2,3},{3,2},{4,5},{5,4},{6,7},{7,6},{8,9},{9,8},{10,11... | collective-permute-start | bytes 9437192 | tf_op jit(solution)/shard_map/ppermute | solution.py:724
  416.1 36.5 %collective-permute-start.24 = (bf16[48,128,128]{2,1,0:T(8,128)(2,1)S(1)}, bf16[48,128,128]{2,1,0:T(8,128)(2,1)S(1)}, u32[]{:S(2)}, u32[]{:S(2)}) collective-permute-start(bf16[48,128,128]{2,1,0:T(8,128)(2,1)S(1)} %get-tuple-element.155), channel_id=1, source_target_pairs={{0,8},{8,0},{16,24},{24,16},{1,9},{9,1},{17,25},{25,17},{2,10},{10... | collective-permute-start | bytes 4718600 | tf_op jit(solution)/shard_map/ppermute | solution.py:839
  417.6 36.2 %collective-permute-start.26 = (bf16[48,128,128]{2,1,0:T(8,128)(2,1)S(1)}, bf16[48,128,128]{2,1,0:T(8,128)(2,1)S(1)}, u32[]{:S(2)}, u32[]{:S(2)}) collective-permute-start(bf16[48,128,128]{2,1,0:T(8,128)(2,1)S(1)} %get-tuple-element.154), channel_id=1, source_target_pairs={{0,16},{8,24},{16,0},{24,8},{1,17},{9,25},{17,1},{25,9},{2,18},{10... | collective-permute-start | bytes 4718600 | tf_op jit(solution)/shard_map/ppermute | solution.py:839
  455.8 18.6 %collective-permute-start.27 = (bf16[24,128,128]{2,1,0:T(8,128)(2,1)S(1)}, bf16[24,128,128]{2,1,0:T(8,128)(2,1)S(1)}, u32[]{:S(2)}, u32[]{:S(2)}) collective-permute-start(bf16[24,128,128]{2,1,0:T(8,128)(2,1)S(1)} %slice.157), channel_id=1, source_target_pairs={{0,8},{8,0},{16,24},{24,16},{1,9},{9,1},{17,25},{25,17},{2,10},{10... | collective-permute-start | bytes 2359304 | tf_op jit(solution)/shard_map/ppermute | solution.py:839
  456.5 18.3 %collective-permute-start.25 = (bf16[24,128,128]{2,1,0:T(8,128)(2,1)S(1)}, bf16[24,128,128]{2,1,0:T(8,128)(2,1)S(1)}, u32[]{:S(2)}, u32[]{:S(2)}) collective-permute-start(bf16[24,128,128]{2,1,0:T(8,128)(2,1)S(1)} %slice.151), channel_id=1, source_target_pairs={{0,16},{8,24},{16,0},{24,8},{1,17},{9,25},{17,1},{25,9},{2,18},{10... | collective-permute-start | bytes 2359304 | tf_op jit(solution)/shard_map/ppermute | solution.py:839
  474.7 1.4 copy-start.15
  476.0 1.2 collective-permute-start.28
  477.2 3.8 collective-permute-start.29
  481.0 5.0 collective-permute-start.30
  482.5 7.8 %copy-start.2 = (f32[384,1536]{1,0:T(8,128)S(1)}, f32[384,1536]{1,0:T(8,128)}, u32[]{:S(2)}) copy-start(f32[384,1536]{1,0:T(8,128)} %get-tuple-element.86.middle_ref) | copy-start | bytes 7077892
  486.0 5.6 %collective-permute-start.31 = (f32[2,1536]{1,0:T(2,128)S(1)}, f32[2,1536]{1,0:T(2,128)S(1)}, u32[]{:S(2)}, u32[]{:S(2)}) collective-permute-start(f32[2,1536]{1,0:T(2,128)S(1)} %add.343), channel_id=1, source_target_pairs={{0,2},{1,3},{2,4},{3,5},{4,6},{5,7},{6,0},{7,1},{8,10},{9,11},{10,... | collective-permute-start | bytes 36872 | tf_op jit(solution)/shard_map/ppermute | solution.py:724
  486.1 5.5 collective-permute-start.32
  488.4 4.3 collective-permute-start.33
  492.7 36.9 %copy-start.11 = (f32[2,1536]{1,0:T(2,128)}, f32[2,1536]{1,0:T(2,128)S(1)}, u32[]{:S(2)}) copy-start(f32[2,1536]{1,0:T(2,128)S(1)} %add_bitcast_fusion) | copy-start | bytes 36868
  507.9 22.3 %collective-permute-start.34 = (bf16[12,128,128]{2,1,0:T(8,128)(2,1)}, bf16[12,128,128]{2,1,0:T(8,128)(2,1)}, u32[]{:S(2)}, u32[]{:S(2)}) collective-permute-start(bf16[12,128,128]{2,1,0:T(8,128)(2,1)} %get-tuple-element.121), channel_id=1, source_target_pairs={{0,2},{1,3},{2,4},{3,5},{4,6},{5,7},{6,0},{7,1},{8,10},{9,11},{10,... | collective-permute-start | bytes 1179656 | tf_op jit(solution)/shard_map/ppermute | solution.py:724
  510.0 34.5 %collective-permute-start.35 = (bf16[12,128,128]{2,1,0:T(8,128)(2,1)S(1)}, bf16[12,128,128]{2,1,0:T(8,128)(2,1)}, u32[]{:S(2)}, u32[]{:S(2)}) collective-permute-start(bf16[12,128,128]{2,1,0:T(8,128)(2,1)S(1)} %get-tuple-element.122), channel_id=1, source_target_pairs={{0,4},{1,5},{2,6},{3,7},{4,0},{5,1},{6,2},{7,3},{8,12},{9,13},{10,... | collective-permute-start | bytes 1179656 | tf_op jit(solution)/shard_map/ppermute | solution.py:724
  513.7 32.3 %collective-permute-start.36 = (bf16[12,128,128]{2,1,0:T(8,128)(2,1)S(1)}, bf16[12,128,128]{2,1,0:T(8,128)(2,1)}, u32[]{:S(2)}, u32[]{:S(2)}) collective-permute-start(bf16[12,128,128]{2,1,0:T(8,128)(2,1)S(1)} %get-tuple-element.123), channel_id=1, source_target_pairs={{0,6},{1,7},{2,0},{3,1},{4,2},{5,3},{6,4},{7,5},{8,14},{9,15},{10,... | collective-permute-start | bytes 1179656 | tf_op jit(solution)/shard_map/ppermute | solution.py:724
  513.8 15.8 %copy-start.14 = (f32[2,1536]{1,0:T(2,128)S(1)}, f32[2,1536]{1,0:T(2,128)}, u32[]{:S(2)}) copy-start(f32[2,1536]{1,0:T(2,128)} %gains_ref.3) | copy-start | bytes 36868
Sparse Core Ops, SparseCore 0:
  45.7 165.5 all-gather.1
  321.7 186.1 reduce-scatter.1

commit v4 on v3

--- a/solution.py
+++ b/solution.py
@@ -14,7 +14,6 @@
 BLOCK = 128
 EXP_DEV = 4
 LANES = 128
-VMEM_BYTES = 63 * 1024 * 1024
 BF16 = jnp.bfloat16
 F32 = jnp.float32
 
@@ -50,8 +49,8 @@
     return lax.dot_general(left, right, (((0,), (0,)), ((), ())), preferred_element_type=F32)
 
 
-def params(**more):
-    return pltpu.CompilerParams(vmem_limit_bytes=VMEM_BYTES, **more)
+def params(megabytes=63, **more):
+    return pltpu.CompilerParams(vmem_limit_bytes=megabytes * 1024 * 1024, **more)
 
 
 def cost(microseconds):
@@ -715,7 +714,7 @@
         ),
         in_specs=[one] * terms + [two, two, one],
         out_specs=(one, two, one),
-        compiler_params=params(dimension_semantics=("arbitrary",)),
+        compiler_params=params(44, dimension_semantics=("arbitrary",)),
         cost_estimate=cost(10),
     )(*gradient, statistics, inverse_roots, master)
 
@@ -781,7 +780,7 @@
     mask = (owner // size) ^ lax.axis_index("expert")
     me = lax.axis_index("shard")
     core = (owner % 2) ^ (me % 2)
-    distance = ((owner % size) // 2 - me // 2) % (size // 2)
+    distance = ((owner % size) // 2) ^ (me // 2)
     part = distance // (size // 4)
     first, second = jnp.where(part == 0, mask % 2, mask // 2), jnp.where(part == 0, mask // 2, mask % 2)
     place = ((core * 2 + 1 - first) * 2 + part) * 2 + second
@@ -810,8 +809,19 @@
     return terms
 
 
+def toward(array, mask):
+    return move(array, [(i, i ^ (2 * mask)) for i in range(lax.axis_size("shard"))])
+
+
+def fold_line(terms):
+    if len(terms) == 1:
+        return terms
+    own, one, two, three = terms
+    return [own, one, add_low(two, toward(three, 1))]
+
+
 def scatter_line(terms):
-    return terms[:1] + [along(term, d) for d, term in enumerate(terms) if d > 0]
+    return terms[:1] + [toward(term, mask) for mask, term in enumerate(terms) if mask > 0]
 
 
 def sum_across(values):
@@ -901,6 +911,7 @@
     output = (middle + jnp.sum(moe_parts.astype(F32), axis=0)).astype(BF16)
     attn_terms = scatter_attention(near_blocks, far_blocks, slots)
     expert_term = lax.psum_scatter(expert_term, "shard", scatter_dimension=0, tiled=True)
+    attn_terms = fold_line(attn_terms)
     attn_terms, gain_parts = lax.optimization_barrier((attn_terms, gain_parts))
     gain_grads = sum_line(sum_across(gain_parts))
     expert_term, attn_terms, gain_grads = lax.optimization_barrier((expert_term, attn_terms, gain_grads))

time: 563 us -> 557 us (0.989)
    reduce_scatter x1, waiting for transfers between devices: 15.2 us -> 6.01 us  [per_device(): lax.psum_scatter(expert_term, 'shard', scatter_dimension=0, tiled=True)]
    unnamed x48 -> x58, local copies, waits for them, and re-layouts: 9.16 us -> 13.1 us
where the time goes in v4:
time: 557 us; the launch traced here: 549 us
  waiting for transfers between devices  220 us (39%)
  Pallas kernels  209 us (38%)
  starting transfers between devices  55.4 us (10%)
  other arithmetic  25.4 us (5%)
  local copies, waits for them, and re-layouts  23.9 us (4%)
  between operations  15.6 us (3%)
    ppermute x21, waiting for transfers between devices, swap(): lax.ppermute(array, 'expert', [(i, i ^ mask) for i in range(lax.axis_size...  151 us
    pallas_call x1, Pallas kernels, expert_front(): pl.pallas_call(kernel, name='expert_front', grid=(EXP_DEV,), out_shape=[j...  58.9 us
    ppermute x16, waiting for transfers between devices, move(): return lax.ppermute(array, 'shard', pairs)  55 us
    pallas_call x1, Pallas kernels, attention_back(): pl.pallas_call(kernel, name='attention_back', out_shape=(jax.ShapeDtypeSt...  45.2 us
    pallas_call x1, Pallas kernels, expert_weight_grads(): pl.pallas_call(kernel, name='expert_weight_grads', grid=(EXP_DEV,), out_s...  38.3 us
    pallas_call x1, Pallas kernels, attention_front(): pl.pallas_call(kernel, name='attention_front', out_shape=(jax.ShapeDtypeS...  24.6 us
    ppermute x21, starting transfers between devices, swap(): lax.ppermute(array, 'expert', [(i, i ^ mask) for i in range(lax.axis_size...  23.3 us
    pallas_call x2, Pallas kernels, shampoo(): pl.pallas_call(kernel, name='shampoo', grid=(slots // many,), out_shape=(...  17.2 us
  transfers between devices with their start and end apart: 43, of which 25 were waited for; matrix products, arithmetic and copies ran while one was open for 8% of the time, Pallas kernels for 27%

profile of v4, /device:TPU:8, one launch (start us, length us, event | category | flops | bytes accessed | tf_op | source)
XLA Modules:
  0.0 548.9 jit_solution(14375146029828271123)
XLA Ops:
  7.2 1.2 convert_element_type.93
  8.4 1.6 collective-permute-start
  11.2 1.9 collective-permute-start.2
  13.1 1.5 collective-permute-start.3
  14.6 1.5 collective-permute-start.4
  16.1 4.2 convert_element_type.94
  20.3 16.1 %collective-permute-done = bf16[12,128,128]{2,1,0:T(8,128)(2,1)S(1)} collective-permute-done((bf16[12,128,128]{2,1,0:T(8,128)(2,1)S(1)}, bf16[12,128,128]{2,1,0:T(8,128)(2,1)S(1)}, u32[]{:S(2)}, u32[]{:S(2)}) %collective-permute-start) | collective-permute-done | bytes 393248 | tf_op jit(solution)/shard_map/ppermute | solution.py:723
  36.4 7.3 %collective-permute-done.1 = bf16[12,128,128]{2,1,0:T(8,128)(2,1)} collective-permute-done((bf16[12,128,128]{2,1,0:T(8,128)(2,1)S(1)}, bf16[12,128,128]{2,1,0:T(8,128)(2,1)}, u32[]{:S(2)}, u32[]{:S(2)}) %collective-permute-start.1) | collective-permute-done | bytes 393248 | tf_op jit(solution)/shard_map/ppermute | solution.py:723
  43.7 1.8 collective-permute-done.2
  47.7 1.6 collective-permute-start.9
  49.3 1.5 collective-permute-start.5
  50.9 1.6 broadcast_in_dim.157
  52.5 3.7 all-to-all-start
  56.3 2.0 collective-permute-start.10
  58.3 1.5 collective-permute-start.6
  60.3 2.1 constant_dynamic-update-slice_fusion.3
  63.4 1.8 constant_dynamic-update-slice_fusion.6
  65.1 10.2 %collective-permute-done.5 = bf16[12,128,128]{2,1,0:T(8,128)(2,1)} collective-permute-done((bf16[12,128,128]{2,1,0:T(8,128)(2,1)}, bf16[12,128,128]{2,1,0:T(8,128)(2,1)}, u32[]{:S(2)}, u32[]{:S(2)}) %collective-permute-start.5) | collective-permute-done | bytes 393248 | tf_op jit(solution)/shard_map/ppermute | solution.py:849
  75.3 1.5 collective-permute-start.13
  76.8 2.5 pad_maximum_fusion.1.refs_0_
  79.3 16.7 %collective-permute-done.6 = bf16[12,128,128]{2,1,0:T(8,128)(2,1)S(1)} collective-permute-done((bf16[12,128,128]{2,1,0:T(8,128)(2,1)}, bf16[12,128,128]{2,1,0:T(8,128)(2,1)S(1)}, u32[]{:S(2)}, u32[]{:S(2)}) %collective-permute-start.6) | collective-permute-done | bytes 393248 | tf_op jit(solution)/shard_map/ppermute | solution.py:849
  96.7 9.0 %collective-permute-done.7 = bf16[12,128,128]{2,1,0:T(8,128)(2,1)S(1)} collective-permute-done((bf16[12,128,128]{2,1,0:T(8,128)(2,1)}, bf16[12,128,128]{2,1,0:T(8,128)(2,1)S(1)}, u32[]{:S(2)}, u32[]{:S(2)}) %collective-permute-start.7) | collective-permute-done | bytes 393248 | tf_op jit(solution)/shard_map/ppermute | solution.py:849
  105.7 1.5 collective-permute-start.11
  108.6 5.6 %collective-permute-done.13 = bf16[12,128,128]{2,1,0:T(8,128)(2,1)S(1)} collective-permute-done((bf16[12,128,128]{2,1,0:T(8,128)(2,1)S(1)}, bf16[12,128,128]{2,1,0:T(8,128)(2,1)S(1)}, u32[]{:S(2)}, u32[]{:S(2)}) %collective-permute-start.13) | collective-permute-done | bytes 393248 | tf_op jit(solution)/shard_map/ppermute | solution.py:849
  116.5 4.8 collective-permute-done.11
  123.4 1.5 collective-permute-done.14
  128.5 1.8 collective-permute-done.18.refs_7_
  130.3 1.8 broadcast_in_dim.158
  132.7 4.7 all-to-all-start.1
  137.4 24.6 %attention_front.1 = (bf16[384,1536]{1,0:T(8,128)(2,1)}, f32[384,1536]{1,0:T(8,128)}, bf16[384,1536]{1,0:T(8,128)(2,1)}, bf16[24,384,64]{2,1,0:T(8,128)(2,1)}, b...) custom-call(s32[1]{0:T(128)} %copy.33.length_ref, ...), custom_call_target="tpu_custom_call" | custom-call | flops 115000000512 | bytes 1024 | tf_op jit(solution)/shard_map/attention_front/pallas_call | solution.py:502
  162.0 2.2 collective-permute-start.19
  164.1 1.5 collective-permute-start.20
  167.3 2.5 pad_maximum_fusion.packed_ref
  169.8 24.1 %collective-permute-done.19.refs_1_ = bf16[384,1536]{1,0:T(8,128)(2,1)} collective-permute-done((bf16[384,1536]{1,0:T(8,128)(2,1)}, bf16[384,1536]{1,0:T(8,128)(2,1)}, u32[]{:S(2)}, u32[]{:S(2)}) %collective-permute-start.19) | collective-permute-done | bytes 1179680 | tf_op jit(solution)/shard_map/ppermute | solution.py:849
  193.9 25.4 %collective-permute-done.21.refs_3_ = bf16[384,1536]{1,0:T(8,128)(2,1)} collective-permute-done((bf16[384,1536]{1,0:T(8,128)(2,1)}, bf16[384,1536]{1,0:T(8,128)(2,1)}, u32[]{:S(2)}, u32[]{:S(2)}) %collective-permute-start.21) | collective-permute-done | bytes 1179680 | tf_op jit(solution)/shard_map/ppermute | solution.py:849
  219.3 58.9 %expert_front.1 = (bf16[4,384,512]{2,1,0:T(8,128)(2,1)}, bf16[4,384,512]{2,1,0:T(8,128)(2,1)}, bf16[4,384,512]{2,1,0:T(8,128)(2,1)}, bf16[4,384,512]{2,1,0:T(8,1...) custom-call(s32[1]{0:T(128)} %bitcast.33.group_ref, ...), custom_call_target="tpu_custom_call" | custom-call | flops 115000000512 | bytes 1024 | tf_op jit(solution)/shard_map/expert_front/pallas_call | solution.py:195
  278.1 4.9 all-to-all-start.2
  283.1 38.3 %expert_weight_grads.1 = bf16[576,128,128]{2,1,0:T(8,128)(2,1)} custom-call(s32[1]{0:T(128)} %bitcast.33.group_ref, s32[576]{0:T(1024)} %select_reduce_fusion.inverse_ref.position_ref, bf16[384,1536]{1,0:T(8,128)(2,1)} %get-tuple-element.86.refs_0_, bf16[384,1536]{1,0:T(8,128)(2,1)} %collective-permute-done.19.refs_1_, ...), custom_call_target="tpu_custom_call" | custom-call | flops 115000000512 | bytes 1024 | tf_op jit(solution)/shard_map/expert_weight_grads/pallas_call | solution.py:309
  321.5 14.9 %expert_outputs.1 = bf16[4,384,1536]{2,1,0:T(8,128)(2,1)} custom-call(s32[1]{0:T(128)} %bitcast.33.group_ref, bf16[4,384,512]{2,1,0:T(8,128)(2,1)} %get-tuple-element.88.refs_0_.refs_6_, bf16[4,384,512]{2,1,0:T(8,128)(2,1)} %get-tuple-element.89.refs_1_.refs_7_, bf16[4,384,512]{2,1,0:T(8,128)(2,1)} %get-tuple-element.90.refs_2_.refs_8_, ...), custom_call_target="tpu_custom_call" | custom-call | flops 344999985152 | bytes 1024 | tf_op jit(solution)/shard_map/expert_outputs/pallas_call | solution.py:364
  336.4 9.9 %expert_route.1.refs_0_ = bf16[384,1536]{1,0:T(8,128)(2,1)} custom-call(bf16[4,384,1024]{2,1,0:T(8,128)(2,1)} %get-tuple-element.97.both_ref.refs_10_, bf16[4,1536,1536]{2,1,0:T(8,128)(2,1)} %get-tuple-element.92.refs_4_.matrix_ref), custom_call_target="tpu_custom_call" | custom-call | flops 4600000000 | bytes 1024 | tf_op jit(solution)/shard_map/expert_route/pallas_call | solution.py:338
  346.3 5.2 all-to-all-start.3
  351.5 45.2 %attention_back.1 = (f32[384,1536]{1,0:T(8,128)}, f32[2,1536]{1,0:T(2,128)}, bf16[192,128,128]{2,1,0:T(8,128)(2,1)}, bf16[192,128,128]{2,1,0:T(8,128)(2,1)}) custom-call(s32[1]{0:T(128)} %bitcast.33.group_ref, s32[1]{0:T(128)} %copy.33.length_ref, s32[384]{0:T(512)} %fusion.39.position_ref, bf16[384,1536]{1,0:T(8,128)(2,1)} %tokens_ref.3, ...), custom_call_target="tpu_custom_call" | custom-call | flops 172499992576 | bytes 1024 | tf_op jit(solution)/shard_map/attention_back/pallas_call | solution.py:640
  396.7 7.7 %all-to-all-done.3 = bf16[4,384,1536]{2,1,0:T(8,128)(2,1)} async-done(((bf16[4,384,1536]{2,1,0:T(8,128)(2,1)}), bf16[4,384,1536]{2,1,0:T(8,128)(2,1)}, u32[]{:S(2)}, u32[]{:S(2)}) %all-to-all-start.3) | async-done | bytes 4718624 | tf_op jit(solution)/shard_map/all_to_all | solution.py:736
  404.4 4.4 fusion.85
  409.4 5.1 collective-permute-done.23
  414.6 1.3 add_convert_fusion.1
  415.9 1.5 collective-permute-start.24
  418.0 1.5 collective-permute-done.22
  419.5 32.9 %collective-permute-done.24 = bf16[48,128,128]{2,1,0:T(8,128)(2,1)S(1)} collective-permute-done((bf16[48,128,128]{2,1,0:T(8,128)(2,1)S(1)}, bf16[48,128,128]{2,1,0:T(8,128)(2,1)S(1)}, u32[]{:S(2)}, u32[]{:S(2)}) %collective-permute-start.24) | collective-permute-done | bytes 1572896 | tf_op jit(solution)/shard_map/ppermute | solution.py:849
  453.6 2.0 add_convert_fusion
  456.3 1.5 collective-permute-start.25
  457.9 16.3 %collective-permute-done.27 = bf16[24,128,128]{2,1,0:T(8,128)(2,1)S(1)} collective-permute-done((bf16[24,128,128]{2,1,0:T(8,128)(2,1)S(1)}, bf16[24,128,128]{2,1,0:T(8,128)(2,1)S(1)}, u32[]{:S(2)}, u32[]{:S(2)}) %collective-permute-start.27) | collective-permute-done | bytes 786464 | tf_op jit(solution)/shard_map/ppermute | solution.py:849
  475.0 19.2 %collective-permute-done.28 = bf16[12,128,128]{2,1,0:T(8,128)(2,1)S(1)} collective-permute-done((bf16[12,128,128]{2,1,0:T(8,128)(2,1)S(1)}, bf16[12,128,128]{2,1,0:T(8,128)(2,1)S(1)}, u32[]{:S(2)}, u32[]{:S(2)}) %collective-permute-start.28) | collective-permute-done | bytes 393248 | tf_op jit(solution)/shard_map/ppermute | solution.py:723
  496.3 3.1 collective-permute-done.30
  500.2 3.5 convert_reduce_fusion
  504.3 2.0 collective-permute-start.33
  506.3 1.5 collective-permute-start.34
  507.9 1.3 add_convert_fusion.6
  510.2 6.0 %reduce-scatter.2.cloned.1.call-done.refs_0_ = bf16[72,128,128]{2,1,0:T(8,128)(2,1)} async-done(((bf16[576,128,128]{2,1,0:T(8,128)(2,1)}), bf16[72,128,128]{2,1,0:T(8,128)(2,1)}) %reduce-scatter.2.cloned.1.call-update) | async-done | bytes 2359312 | tf_op jit(solution)/shard_map/reduce_scatter | solution.py:913
  516.3 3.4 collective-permute-start.35
  519.8 2.3 copy-done
  522.2 1.7 copy-done.2
  523.8 14.8 %shampoo.2 = (f32[72,128,128]{2,1,0:T(8,128)}, f32[72,2,128,128]{3,2,1,0:T(8,128)}, f32[72,128,128]{2,1,0:T(8,128)}) custom-call(bf16[72,128,128]{2,1,0:T(8,128)(2,1)S(1)} %copy-done.2, f32[72,2,128,128]{3,2,1,0:T(8,128)} %refs_1_.1, f32[72,2,128,128]{3,2,1,0:T(8,128)} %refs_2_.1, f32[72,128,128]{2,1,0:T(8,128)S(1)} %copy-done), custom_call_target="tpu_custom_call" | custom-call | flops 11500000256 | bytes 1024 | tf_op jit(solution)/shard_map/shampoo/pallas_call | solution.py:706
  539.3 2.5 shampoo.3
  (137 shorter events, 25.7 us)
Async XLA Ops:
  7.2 212.1 %all-gather.2.cloned.1.call-start = ((), (), s32[]{:S(2)}) async-start(), calls=%async_computation.5 | async-start | bytes 21233664 | tf_op jit(solution)/shard_map/all_gather | solution.py:887
  8.4 11.9 %copy-start.8 = (bf16[12,128,128]{2,1,0:T(8,128)(2,1)}, bf16[12,128,128]{2,1,0:T(8,128)(2,1)S(1)}, u32[]{:S(2)}) copy-start(bf16[12,128,128]{2,1,0:T(8,128)(2,1)S(1)} %convert_element_type.93) | copy-start | bytes 1179652
  8.4 28.0 %collective-permute-start = (bf16[12,128,128]{2,1,0:T(8,128)(2,1)S(1)}, bf16[12,128,128]{2,1,0:T(8,128)(2,1)S(1)}, u32[]{:S(2)}, u32[]{:S(2)}) collective-permute-start(bf16[12,128,128]{2,1,0:T(8,128)(2,1)S(1)} %convert_element_type.93), channel_id=1, source_target_pairs={{0,2},{1,3},{2,4},{3,5},{4,6},{5,7},{6,0},{7,1},{8,10},{9,11},{10,... | collective-permute-start | bytes 1179656 | tf_op jit(solution)/shard_map/ppermute | solution.py:723
  10.1 33.7 %collective-permute-start.1 = (bf16[12,128,128]{2,1,0:T(8,128)(2,1)S(1)}, bf16[12,128,128]{2,1,0:T(8,128)(2,1)}, u32[]{:S(2)}, u32[]{:S(2)}) collective-permute-start(bf16[12,128,128]{2,1,0:T(8,128)(2,1)S(1)} %convert_element_type.93), channel_id=1, source_target_pairs={{0,4},{1,5},{2,6},{3,7},{4,0},{5,1},{6,2},{7,3},{8,12},{9,13},{10,... | collective-permute-start | bytes 1179656 | tf_op jit(solution)/shard_map/ppermute | solution.py:723
  11.2 34.4 %collective-permute-start.2 = (bf16[12,128,128]{2,1,0:T(8,128)(2,1)S(1)}, bf16[12,128,128]{2,1,0:T(8,128)(2,1)S(1)}, u32[]{:S(2)}, u32[]{:S(2)}) collective-permute-start(bf16[12,128,128]{2,1,0:T(8,128)(2,1)S(1)} %convert_element_type.93), channel_id=1, source_target_pairs={{0,6},{1,7},{2,0},{3,1},{4,2},{5,3},{6,4},{7,5},{8,14},{9,15},{10,... | collective-permute-start | bytes 1179656 | tf_op jit(solution)/shard_map/ppermute | solution.py:723
  13.1 32.4 %collective-permute-start.3 = (bf16[12,128,128]{2,1,0:T(8,128)(2,1)S(1)}, bf16[12,128,128]{2,1,0:T(8,128)(2,1)}, u32[]{:S(2)}, u32[]{:S(2)}) collective-permute-start(bf16[12,128,128]{2,1,0:T(8,128)(2,1)S(1)} %convert_element_type.93), channel_id=1, source_target_pairs={{0,8},{8,0},{16,24},{24,16},{1,9},{9,1},{17,25},{25,17},{2,10},{10... | collective-permute-start | bytes 1179656 | tf_op jit(solution)/shard_map/ppermute | solution.py:849
  14.6 30.9 %collective-permute-start.4 = (bf16[12,128,128]{2,1,0:T(8,128)(2,1)S(1)}, bf16[12,128,128]{2,1,0:T(8,128)(2,1)S(1)}, u32[]{:S(2)}, u32[]{:S(2)}) collective-permute-start(bf16[12,128,128]{2,1,0:T(8,128)(2,1)S(1)} %convert_element_type.93), channel_id=1, source_target_pairs={{0,16},{8,24},{16,0},{24,8},{1,17},{9,25},{17,1},{25,9},{2,18},{10... | collective-permute-start | bytes 1179656 | tf_op jit(solution)/shard_map/ppermute | solution.py:849
  20.3 25.9 %copy-start.17 = (bf16[384,8]{0,1:T(8,128)(2,1)S(1)}, bf16[384,8]{0,1:T(8,128)(2,1)}, u32[]{:S(2)}) copy-start(bf16[384,8]{0,1:T(8,128)(2,1)} %param.18) | copy-start | bytes 18436
  20.3 26.0 %copy-start.18 = (s32[384,8]{0,1:T(8,128)S(1)}, s32[384,8]{0,1:T(8,128)}, u32[]{:S(2)}) copy-start(s32[384,8]{0,1:T(8,128)} %param.17) | copy-start | bytes 36868
  20.3 27.2 %copy-start.10 = (bf16[384,1536]{1,0:T(8,128)(2,1)S(1)}, bf16[384,1536]{1,0:T(8,128)(2,1)}, u32[]{:S(2)}) copy-start(bf16[384,1536]{1,0:T(8,128)(2,1)} %param.15) | copy-start | bytes 3538948
  36.4 16.1 %copy-start.15 = (bf16[12,128,128]{2,1,0:T(8,128)(2,1)}, bf16[12,128,128]{2,1,0:T(8,128)(2,1)S(1)}, u32[]{:S(2)}) copy-start(bf16[12,128,128]{2,1,0:T(8,128)(2,1)S(1)} %collective-permute-done) | copy-start | bytes 1179652
  47.7 3.1 copy-start.5
  47.7 15.5 %collective-permute-start.9 = (bf16[12,128,128]{2,1,0:T(8,128)(2,1)}, bf16[12,128,128]{2,1,0:T(8,128)(2,1)}, u32[]{:S(2)}, u32[]{:S(2)}) collective-permute-start(bf16[12,128,128]{2,1,0:T(8,128)(2,1)} %collective-permute-done.1), channel_id=1, source_target_pairs={{0,8},{8,0},{16,24},{24,16},{1,9},{9,1},{17,25},{25,17},{2,10},{10... | collective-permute-start | bytes 1179656 | tf_op jit(solution)/shard_map/ppermute | solution.py:849
  49.3 26.0 %collective-permute-start.5 = (bf16[12,128,128]{2,1,0:T(8,128)(2,1)}, bf16[12,128,128]{2,1,0:T(8,128)(2,1)}, u32[]{:S(2)}, u32[]{:S(2)}) collective-permute-start(bf16[12,128,128]{2,1,0:T(8,128)(2,1)} %collective-permute-done.3), channel_id=1, source_target_pairs={{0,16},{8,24},{16,0},{24,8},{1,17},{9,25},{17,1},{25,9},{2,18},{10... | collective-permute-start | bytes 1179656 | tf_op jit(solution)/shard_map/ppermute | solution.py:849
  52.5 77.8 %all-to-all-start = ((bf16[4,192,1664]{2,1,0:T(8,128)(2,1)}), bf16[4,192,1664]{2,1,0:T(8,128)(2,1)S(1)}, u32[]{:S(2)}, u32[]{:S(2)}) async-start(bf16[4,192,1664]{2,1,0:T(8,128)(2,1)} %broadcast_in_dim.157), calls=%async_computation | async-start | bytes 5111808 | tf_op jit(solution)/shard_map/all_to_all | solution.py:741
  56.3 6.1 %copy-start.14 = (bf16[12,128,128]{2,1,0:T(8,128)(2,1)S(1)}, bf16[12,128,128]{2,1,0:T(8,128)(2,1)}, u32[]{:S(2)}) copy-start(bf16[12,128,128]{2,1,0:T(8,128)(2,1)} %copy-done.13) | copy-start | bytes 1179652
  56.3 20.5 %copy-start.9 = (bf16[12,128,128]{2,1,0:T(8,128)(2,1)S(1)}, bf16[12,128,128]{2,1,0:T(8,128)(2,1)}, u32[]{:S(2)}) copy-start(bf16[12,128,128]{2,1,0:T(8,128)(2,1)} %copy-done.8) | copy-start | bytes 1179652
  56.3 20.5 %copy-start.12 = (bf16[12,128,128]{2,1,0:T(8,128)(2,1)S(1)}, bf16[12,128,128]{2,1,0:T(8,128)(2,1)}, u32[]{:S(2)}) copy-start(bf16[12,128,128]{2,1,0:T(8,128)(2,1)} %copy-done.11) | copy-start | bytes 1179652
  56.3 59.4 %collective-permute-start.10 = (bf16[12,128,128]{2,1,0:T(8,128)(2,1)}, bf16[12,128,128]{2,1,0:T(8,128)(2,1)S(1)}, u32[]{:S(2)}, u32[]{:S(2)}) collective-permute-start(bf16[12,128,128]{2,1,0:T(8,128)(2,1)} %collective-permute-done.1), channel_id=1, source_target_pairs={{0,16},{8,24},{16,0},{24,8},{1,17},{9,25},{17,1},{25,9},{2,18},{10... | collective-permute-start | bytes 1179656 | tf_op jit(solution)/shard_map/ppermute | solution.py:849
  58.3 37.7 %collective-permute-start.6 = (bf16[12,128,128]{2,1,0:T(8,128)(2,1)}, bf16[12,128,128]{2,1,0:T(8,128)(2,1)S(1)}, u32[]{:S(2)}, u32[]{:S(2)}) collective-permute-start(bf16[12,128,128]{2,1,0:T(8,128)(2,1)} %copy-done.15), channel_id=1, source_target_pairs={{0,8},{8,0},{16,24},{24,16},{1,9},{9,1},{17,25},{25,17},{2,10},{10... | collective-permute-start | bytes 1179656 | tf_op jit(solution)/shard_map/ppermute | solution.py:849
  59.7 46.0 %collective-permute-start.7 = (bf16[12,128,128]{2,1,0:T(8,128)(2,1)}, bf16[12,128,128]{2,1,0:T(8,128)(2,1)S(1)}, u32[]{:S(2)}, u32[]{:S(2)}) collective-permute-start(bf16[12,128,128]{2,1,0:T(8,128)(2,1)} %copy-done.15), channel_id=1, source_target_pairs={{0,16},{8,24},{16,0},{24,8},{1,17},{9,25},{17,1},{25,9},{2,18},{10... | collective-permute-start | bytes 1179656 | tf_op jit(solution)/shard_map/ppermute | solution.py:849
  63.2 44.8 %collective-permute-start.12 = (bf16[12,128,128]{2,1,0:T(8,128)(2,1)S(1)}, bf16[12,128,128]{2,1,0:T(8,128)(2,1)S(1)}, u32[]{:S(2)}, u32[]{:S(2)}) collective-permute-start(bf16[12,128,128]{2,1,0:T(8,128)(2,1)S(1)} %copy-done.14), channel_id=1, source_target_pairs={{0,8},{8,0},{16,24},{24,16},{1,9},{9,1},{17,25},{25,17},{2,10},{10... | collective-permute-start | bytes 1179656 | tf_op jit(solution)/shard_map/ppermute | solution.py:849
  75.3 38.9 %collective-permute-start.13 = (bf16[12,128,128]{2,1,0:T(8,128)(2,1)S(1)}, bf16[12,128,128]{2,1,0:T(8,128)(2,1)S(1)}, u32[]{:S(2)}, u32[]{:S(2)}) collective-permute-start(bf16[12,128,128]{2,1,0:T(8,128)(2,1)S(1)} %copy-done.14), channel_id=1, source_target_pairs={{0,16},{8,24},{16,0},{24,8},{1,17},{9,25},{17,1},{25,9},{2,18},{10... | collective-permute-start | bytes 1179656 | tf_op jit(solution)/shard_map/ppermute | solution.py:849
  95.9 32.6 %collective-permute-start.15 = (bf16[48,128,128]{2,1,0:T(8,128)(2,1)}, bf16[48,128,128]{2,1,0:T(8,128)(2,1)}, u32[]{:S(2)}, u32[]{:S(2)}) collective-permute-start(bf16[48,128,128]{2,1,0:T(8,128)(2,1)} %pad_maximum_fusion.1.refs_0_), channel_id=1, source_target_pairs={{0,1},{1,0},{2,3},{3,2},{4,5},{5,4},{6,7},{7,6},{8,9},{9,8},{10,11... | collective-permute-start | bytes 4718600 | tf_op jit(solution)/shard_map/ppermute | solution.py:723
  105.7 15.6 %collective-permute-start.11 = (bf16[12,128,128]{2,1,0:T(8,128)(2,1)}, bf16[12,128,128]{2,1,0:T(8,128)(2,1)S(1)}, u32[]{:S(2)}, u32[]{:S(2)}) collective-permute-start(bf16[12,128,128]{2,1,0:T(8,128)(2,1)} %collective-permute-done.9), channel_id=1, source_target_pairs={{0,16},{8,24},{16,0},{24,8},{1,17},{9,25},{17,1},{25,9},{2,18},{10... | collective-permute-start | bytes 1179656 | tf_op jit(solution)/shard_map/ppermute | solution.py:849
  108.0 14.1 %collective-permute-start.8 = (bf16[12,128,128]{2,1,0:T(8,128)(2,1)S(1)}, bf16[12,128,128]{2,1,0:T(8,128)(2,1)S(1)}, u32[]{:S(2)}, u32[]{:S(2)}) collective-permute-start(bf16[12,128,128]{2,1,0:T(8,128)(2,1)S(1)} %collective-permute-done.7), channel_id=1, source_target_pairs={{0,8},{8,0},{16,24},{24,16},{1,9},{9,1},{17,25},{25,17},{2,10},{10... | collective-permute-start | bytes 1179656 | tf_op jit(solution)/shard_map/ppermute | solution.py:849
  114.1 10.7 %collective-permute-start.14 = (bf16[12,128,128]{2,1,0:T(8,128)(2,1)S(1)}, bf16[12,128,128]{2,1,0:T(8,128)(2,1)S(1)}, u32[]{:S(2)}, u32[]{:S(2)}) collective-permute-start(bf16[12,128,128]{2,1,0:T(8,128)(2,1)S(1)} %collective-permute-done.13), channel_id=1, source_target_pairs={{0,8},{8,0},{16,24},{24,16},{1,9},{9,1},{17,25},{25,17},{2,10},{10... | collective-permute-start | bytes 1179656 | tf_op jit(solution)/shard_map/ppermute | solution.py:849
  115.8 9.9 %copy-start.21 = (s32[384]{0:T(512)S(1)}, s32[384]{0:T(512)}, u32[]{:S(2)}) copy-start(s32[384]{0:T(512)} %param.23) | copy-start | bytes 4612
  122.1 6.5 %collective-permute-start.17 = (bf16[48,128,128]{2,1,0:T(8,128)(2,1)}, bf16[48,128,128]{2,1,0:T(8,128)(2,1)}, u32[]{:S(2)}, u32[]{:S(2)}) collective-permute-start(bf16[48,128,128]{2,1,0:T(8,128)(2,1)} %constant_dynamic-update-slice_fusion.4.refs_2_), channel_id=1, source_target_pairs={{0,1},{1,0},{2,3},{3,2},{4,5},{5,4},{6,7},{7,6},{8,9},{9,8},{10,11... | collective-permute-start | bytes 4718600 | tf_op jit(solution)/shard_map/ppermute | solution.py:723
  122.9 5.7 %collective-permute-start.16 = (bf16[48,128,128]{2,1,0:T(8,128)(2,1)}, bf16[48,128,128]{2,1,0:T(8,128)(2,1)}, u32[]{:S(2)}, u32[]{:S(2)}) collective-permute-start(bf16[48,128,128]{2,1,0:T(8,128)(2,1)} %constant_dynamic-update-slice_fusion.refs_1_), channel_id=1, source_target_pairs={{0,1},{1,0},{2,3},{3,2},{4,5},{5,4},{6,7},{7,6},{8,9},{9,8},{10,11... | collective-permute-start | bytes 4718600 | tf_op jit(solution)/shard_map/ppermute | solution.py:723
  125.6 4.7 collective-permute-start.18
  132.7 86.6 %all-to-all-start.1 = ((bf16[4,192,1664]{2,1,0:T(8,128)(2,1)}), bf16[4,192,1664]{2,1,0:T(8,128)(2,1)}, u32[]{:S(2)}, u32[]{:S(2)}) async-start(bf16[4,192,1664]{2,1,0:T(8,128)(2,1)} %broadcast_in_dim.158), calls=%async_computation.1 | async-start | bytes 5111808 | tf_op jit(solution)/shard_map/all_to_all | solution.py:741
  137.4 28.3 %copy-start.22 = (s32[1,576]{1,0:T(1,128)S(1)}, s32[1,576]{1,0:T(1,128)}, u32[]{:S(2)}) copy-start(s32[1,576]{1,0:T(1,128)} %param.27) | copy-start | bytes 6916
  162.0 31.9 %collective-permute-start.19 = (bf16[384,1536]{1,0:T(8,128)(2,1)}, bf16[384,1536]{1,0:T(8,128)(2,1)}, u32[]{:S(2)}, u32[]{:S(2)}) collective-permute-start(bf16[384,1536]{1,0:T(8,128)(2,1)} %get-tuple-element.86.refs_0_), channel_id=1, source_target_pairs={{0,8},{8,0},{16,24},{24,16},{1,9},{9,1},{17,25},{25,17},{2,10},{10... | collective-permute-start | bytes 3538952 | tf_op jit(solution)/shard_map/ppermute | solution.py:849
  164.1 29.7 %collective-permute-start.20 = (bf16[384,1536]{1,0:T(8,128)(2,1)}, bf16[384,1536]{1,0:T(8,128)(2,1)}, u32[]{:S(2)}, u32[]{:S(2)}) collective-permute-start(bf16[384,1536]{1,0:T(8,128)(2,1)} %get-tuple-element.86.refs_0_), channel_id=1, source_target_pairs={{0,16},{8,24},{16,0},{24,8},{1,17},{9,25},{17,1},{25,9},{2,18},{10... | collective-permute-start | bytes 3538952 | tf_op jit(solution)/shard_map/ppermute | solution.py:849
  165.6 53.6 %collective-permute-start.21 = (bf16[384,1536]{1,0:T(8,128)(2,1)}, bf16[384,1536]{1,0:T(8,128)(2,1)}, u32[]{:S(2)}, u32[]{:S(2)}) collective-permute-start(bf16[384,1536]{1,0:T(8,128)(2,1)} %get-tuple-element.86.refs_0_), channel_id=1, source_target_pairs={{0,24},{8,16},{16,8},{24,0},{1,25},{9,17},{17,9},{25,1},{2,26},{10... | collective-permute-start | bytes 3538952 | tf_op jit(solution)/shard_map/ppermute | solution.py:849
  278.1 68.2 %all-to-all-start.2 = ((bf16[4,384,1536]{2,1,0:T(8,128)(2,1)}), bf16[4,384,1536]{2,1,0:T(8,128)(2,1)}, u32[]{:S(2)}, u32[]{:S(2)}) async-start(bf16[4,384,1536]{2,1,0:T(8,128)(2,1)} %get-tuple-element.98), calls=%async_computation.2 | async-start | bytes 9437184 | tf_op jit(solution)/shard_map/all_to_all | solution.py:736
  283.1 233.2 %reduce-scatter.2.cloned.1.call-start = ((), (), s32[]{:S(2)}) async-start(), calls=%async_computation.6 | async-start | bytes 21233664 | tf_op jit(solution)/shard_map/reduce_scatter | solution.py:913
  346.3 58.1 %all-to-all-start.3 = ((bf16[4,384,1536]{2,1,0:T(8,128)(2,1)}), bf16[4,384,1536]{2,1,0:T(8,128)(2,1)}, u32[]{:S(2)}, u32[]{:S(2)}) async-start(bf16[4,384,1536]{2,1,0:T(8,128)(2,1)} %expert_outputs.1), calls=%async_computation.3 | async-start | bytes 9437184 | tf_op jit(solution)/shard_map/all_to_all | solution.py:736
  404.4 10.1 %slice-start = ((s8[6291456]{0:T(1024)(128)(4,1)}), s8[4194304]{0:T(1024)(128)(4,1)S(1)}, s32[]{:S(2)}) async-start(s8[6291456]{0:T(1024)(128)(4,1)} %bitcast.73), calls=%async_computation.7 | async-start | bytes 8388608
  404.4 10.1 %slice-start.1 = ((s8[6291456]{0:T(1024)(128)(4,1)}), s8[2097152]{0:T(1024)(128)(4,1)S(1)}, s32[]{:S(2)}) async-start(s8[6291456]{0:T(1024)(128)(4,1)} %bitcast.73), calls=%async_computation.8 | async-start | bytes 4194304
  408.8 5.7 %collective-permute-start.23 = (bf16[96,128,128]{2,1,0:T(8,128)(2,1)S(1)}, bf16[96,128,128]{2,1,0:T(8,128)(2,1)S(1)}, u32[]{:S(2)}, u32[]{:S(2)}) collective-permute-start(bf16[96,128,128]{2,1,0:T(8,128)(2,1)S(1)} %get-tuple-element.151), channel_id=1, source_target_pairs={{0,1},{1,0},{2,3},{3,2},{4,5},{5,4},{6,7},{7,6},{8,9},{9,8},{10,11... | collective-permute-start | bytes 9437192 | tf_op jit(solution)/shard_map/ppermute | solution.py:723
  408.9 10.6 %collective-permute-start.22 = (bf16[96,128,128]{2,1,0:T(8,128)(2,1)S(1)}, bf16[96,128,128]{2,1,0:T(8,128)(2,1)S(1)}, u32[]{:S(2)}, u32[]{:S(2)}) collective-permute-start(bf16[96,128,128]{2,1,0:T(8,128)(2,1)S(1)} %get-tuple-element.150), channel_id=1, source_target_pairs={{0,1},{1,0},{2,3},{3,2},{4,5},{5,4},{6,7},{7,6},{8,9},{9,8},{10,11... | collective-permute-start | bytes 9437192 | tf_op jit(solution)/shard_map/ppermute | solution.py:723
  415.9 36.5 %collective-permute-start.24 = (bf16[48,128,128]{2,1,0:T(8,128)(2,1)S(1)}, bf16[48,128,128]{2,1,0:T(8,128)(2,1)S(1)}, u32[]{:S(2)}, u32[]{:S(2)}) collective-permute-start(bf16[48,128,128]{2,1,0:T(8,128)(2,1)S(1)} %get-tuple-element.149), channel_id=1, source_target_pairs={{0,8},{8,0},{16,24},{24,16},{1,9},{9,1},{17,25},{25,17},{2,10},{10... | collective-permute-start | bytes 4718600 | tf_op jit(solution)/shard_map/ppermute | solution.py:849
  417.4 36.2 %collective-permute-start.26 = (bf16[48,128,128]{2,1,0:T(8,128)(2,1)S(1)}, bf16[48,128,128]{2,1,0:T(8,128)(2,1)S(1)}, u32[]{:S(2)}, u32[]{:S(2)}) collective-permute-start(bf16[48,128,128]{2,1,0:T(8,128)(2,1)S(1)} %get-tuple-element.148), channel_id=1, source_target_pairs={{0,16},{8,24},{16,0},{24,8},{1,17},{9,25},{17,1},{25,9},{2,18},{10... | collective-permute-start | bytes 4718600 | tf_op jit(solution)/shard_map/ppermute | solution.py:849
  455.6 18.6 %collective-permute-start.27 = (bf16[24,128,128]{2,1,0:T(8,128)(2,1)S(1)}, bf16[24,128,128]{2,1,0:T(8,128)(2,1)S(1)}, u32[]{:S(2)}, u32[]{:S(2)}) collective-permute-start(bf16[24,128,128]{2,1,0:T(8,128)(2,1)S(1)} %slice.157), channel_id=1, source_target_pairs={{0,8},{8,0},{16,24},{24,16},{1,9},{9,1},{17,25},{25,17},{2,10},{10... | collective-permute-start | bytes 2359304 | tf_op jit(solution)/shard_map/ppermute | solution.py:849
  456.3 18.3 %collective-permute-start.25 = (bf16[24,128,128]{2,1,0:T(8,128)(2,1)S(1)}, bf16[24,128,128]{2,1,0:T(8,128)(2,1)S(1)}, u32[]{:S(2)}, u32[]{:S(2)}) collective-permute-start(bf16[24,128,128]{2,1,0:T(8,128)(2,1)S(1)} %slice.151), channel_id=1, source_target_pairs={{0,16},{8,24},{16,0},{24,8},{1,17},{9,25},{17,1},{25,9},{2,18},{10... | collective-permute-start | bytes 2359304 | tf_op jit(solution)/shard_map/ppermute | solution.py:849
  474.5 19.8 %collective-permute-start.28 = (bf16[12,128,128]{2,1,0:T(8,128)(2,1)S(1)}, bf16[12,128,128]{2,1,0:T(8,128)(2,1)S(1)}, u32[]{:S(2)}, u32[]{:S(2)}) collective-permute-start(bf16[12,128,128]{2,1,0:T(8,128)(2,1)S(1)} %slice.159), channel_id=1, source_target_pairs={{0,2},{1,3},{2,0},{3,1},{4,6},{5,7},{6,4},{7,5},{8,10},{9,11},{10,... | collective-permute-start | bytes 1179656 | tf_op jit(solution)/shard_map/ppermute | solution.py:723
  474.9 19.4 %copy-start.20 = (f32[2,1536]{1,0:T(2,128)S(1)}, f32[2,1536]{1,0:T(2,128)}, u32[]{:S(2)}) copy-start(f32[2,1536]{1,0:T(2,128)} %get-tuple-element.114) | copy-start | bytes 36868
  494.4 1.2 collective-permute-start.29
  495.7 3.8 collective-permute-start.30
  499.4 4.3 collective-permute-start.31
  500.2 7.7 %copy-start.7 = (f32[384,1536]{1,0:T(8,128)S(1)}, f32[384,1536]{1,0:T(8,128)}, u32[]{:S(2)}) copy-start(f32[384,1536]{1,0:T(8,128)} %get-tuple-element.83.middle_ref) | copy-start | bytes 7077892
  503.7 5.5 collective-permute-start.32
  504.3 5.0 collective-permute-start.33
  506.3 3.8 collective-permute-start.34
  510.2 28.4 %copy-start.16 = (f32[2,1536]{1,0:T(2,128)}, f32[2,1536]{1,0:T(2,128)S(1)}, u32[]{:S(2)}) copy-start(f32[2,1536]{1,0:T(2,128)S(1)} %add_bitcast_fusion) | copy-start | bytes 36868
  516.3 23.0 %collective-permute-start.35 = (bf16[12,128,128]{2,1,0:T(8,128)(2,1)S(1)}, bf16[12,128,128]{2,1,0:T(8,128)(2,1)S(1)}, u32[]{:S(2)}, u32[]{:S(2)}) collective-permute-start(bf16[12,128,128]{2,1,0:T(8,128)(2,1)S(1)} %get-tuple-element.117), channel_id=1, source_target_pairs={{0,2},{1,3},{2,0},{3,1},{4,6},{5,7},{6,4},{7,5},{8,10},{9,11},{10,... | collective-permute-start | bytes 1179656 | tf_op jit(solution)/shard_map/ppermute | solution.py:723
  519.7 19.6 %collective-permute-start.36 = (bf16[12,128,128]{2,1,0:T(8,128)(2,1)S(1)}, bf16[12,128,128]{2,1,0:T(8,128)(2,1)S(1)}, u32[]{:S(2)}, u32[]{:S(2)}) collective-permute-start(bf16[12,128,128]{2,1,0:T(8,128)(2,1)S(1)} %add_convert_fusion.9), channel_id=1, source_target_pairs={{0,4},{1,5},{2,6},{3,7},{4,0},{5,1},{6,2},{7,3},{8,12},{9,13},{10,... | collective-permute-start | bytes 1179656 | tf_op jit(solution)/shard_map/ppermute | solution.py:723
  519.8 2.3 copy-start
  523.8 14.8 %copy-start.19 = (f32[2,1536]{1,0:T(2,128)S(1)}, f32[2,1536]{1,0:T(2,128)}, u32[]{:S(2)}) copy-start(f32[2,1536]{1,0:T(2,128)} %gains_ref.3) | copy-start | bytes 36868
  523.8 15.5 %copy-start.1 = (f32[12,128,128]{2,1,0:T(8,128)S(1)}, f32[12,128,128]{2,1,0:T(8,128)}, u32[]{:S(2)}) copy-start(f32[12,128,128]{2,1,0:T(8,128)} %refs_5_.1) | copy-start | bytes 2359300
  523.8 15.5 %copy-start.3 = (f32[12,2,128,128]{3,2,1,0:T(8,128)S(1)}, f32[12,2,128,128]{3,2,1,0:T(8,128)}, u32[]{:S(2)}) copy-start(f32[12,2,128,128]{3,2,1,0:T(8,128)} %refs_3_.3) | copy-start | bytes 4718596
  523.8 15.5 %copy-start.4 = (f32[12,2,128,128]{3,2,1,0:T(8,128)S(1)}, f32[12,2,128,128]{3,2,1,0:T(8,128)}, u32[]{:S(2)}) copy-start(f32[12,2,128,128]{3,2,1,0:T(8,128)} %refs_4_.1) | copy-start | bytes 4718596
  (4 other events, 8.3 us)
Sparse Core Ops, SparseCore 0:
  45.7 165.5 all-gather.1
  321.6 194.6 reduce-scatter.1

commit v5 on v4

--- a/solution.py
+++ b/solution.py
@@ -755,7 +755,8 @@
         pieces = [lax.all_gather(own, ("expert", "shard"), axis=0, tiled=True)]
         return pieces, deal, later
     me_e, me_s = lax.axis_index("expert"), lax.axis_index("shard")
-    lines = [along(own, d) for d in range(1, size // 2)]
+    near, across = toward(own, 1), toward(own, 2)
+    lines = [near, across, toward(across, 1)]
     beside = [swap(own, 1), swap(own, 2)]
     lines, beside, later = lax.optimization_barrier((lines, beside, later))
     fours = [jnp.concatenate([own, *beside, swap(beside[0], 2)], axis=0)]
@@ -763,7 +764,7 @@
     pieces, names, far_names = [], [], []
     for d, four in enumerate(fours):
         pieces.append(four)
-        source = (me_s - 2 * d) % size
+        source = me_s ^ (2 * d)
         for m in range(groups):
             names.append(by_device[me_e ^ m, source])
             far_names.append(by_device[me_e ^ m, source ^ 1])

time: 557 us -> 552 us (level)
  waiting for transfers between devices: 220 us -> 211 us
    ppermute x16, waiting for transfers between devices: 55 us -> 48.2 us  [move(): return lax.ppermute(array, 'shard', pairs)]
  transfers between devices with their start and end apart: 43 -> 43, of which waited for: 25 -> 23; matrix products, arithmetic and copies ran while one was open for 8% -> 8% of each run, Pallas kernels for 27% -> 27%
where the time goes in v5:
time: 552 us; the launch traced here: 545 us
  waiting for transfers between devices  211 us (38%)
  Pallas kernels  209 us (38%)
  starting transfers between devices  59.3 us (11%)
  other arithmetic  25.4 us (5%)
  local copies, waits for them, and re-layouts  24.1 us (4%)
  between operations  15.6 us (3%)
    ppermute x21, waiting for transfers between devices, swap(): lax.ppermute(array, 'expert', [(i, i ^ mask) for i in range(lax.axis_size...  150 us
    pallas_call x1, Pallas kernels, expert_front(): pl.pallas_call(kernel, name='expert_front', grid=(EXP_DEV,), out_shape=[j...  58.9 us
    ppermute x16, waiting for transfers between devices, move(): return lax.ppermute(array, 'shard', pairs)  48.2 us
    pallas_call x1, Pallas kernels, attention_back(): pl.pallas_call(kernel, name='attention_back', out_shape=(jax.ShapeDtypeSt...  45.1 us
    pallas_call x1, Pallas kernels, expert_weight_grads(): pl.pallas_call(kernel, name='expert_weight_grads', grid=(EXP_DEV,), out_s...  38.3 us
    pallas_call x1, Pallas kernels, attention_front(): pl.pallas_call(kernel, name='attention_front', out_shape=(jax.ShapeDtypeS...  24.6 us
    ppermute x21, starting transfers between devices, swap(): lax.ppermute(array, 'expert', [(i, i ^ mask) for i in range(lax.axis_size...  23.8 us
    pallas_call x2, Pallas kernels, shampoo(): pl.pallas_call(kernel, name='shampoo', grid=(slots // many,), out_shape=(...  17.2 us
  transfers between devices with their start and end apart: 43, of which 23 were waited for; matrix products, arithmetic and copies ran while one was open for 8% of the time, Pallas kernels for 27%

profile of v5, /device:TPU:8, one launch (start us, length us, event | category | flops | bytes accessed | tf_op | source)
XLA Modules:
  0.0 544.7 jit_solution(3723924469481948745)
XLA Ops:
  7.2 1.2 convert_element_type.93
  8.4 2.7 collective-permute-start.1
  11.5 1.5 collective-permute-start.3
  13.0 1.5 collective-permute-start.4
  14.6 13.2 %collective-permute-done.1 = bf16[12,128,128]{2,1,0:T(8,128)(2,1)} collective-permute-done((bf16[12,128,128]{2,1,0:T(8,128)(2,1)S(1)}, bf16[12,128,128]{2,1,0:T(8,128)(2,1)}, u32[]{:S(2)}, u32[]{:S(2)}) %collective-permute-start.1) | collective-permute-done | bytes 393248 | tf_op jit(solution)/shard_map/ppermute | solution.py:723
  27.8 1.5 collective-permute-start.2
  29.3 4.2 convert_element_type.94
  33.6 5.5 %collective-permute-done.2 = bf16[12,128,128]{2,1,0:T(8,128)(2,1)S(1)} collective-permute-done((bf16[12,128,128]{2,1,0:T(8,128)(2,1)}, bf16[12,128,128]{2,1,0:T(8,128)(2,1)S(1)}, u32[]{:S(2)}, u32[]{:S(2)}) %collective-permute-start.2) | collective-permute-done | bytes 393248 | tf_op jit(solution)/shard_map/ppermute | solution.py:723
  41.2 1.6 collective-permute-start.9
  42.8 1.5 collective-permute-start.5
  44.4 1.6 broadcast_in_dim.157
  46.0 3.7 all-to-all-start
  49.8 2.0 collective-permute-start.10
  51.8 1.5 collective-permute-start.6
  53.8 2.1 constant_dynamic-update-slice_fusion.3
  56.9 1.8 constant_dynamic-update-slice_fusion.6
  58.7 9.8 %collective-permute-done.5 = bf16[12,128,128]{2,1,0:T(8,128)(2,1)} collective-permute-done((bf16[12,128,128]{2,1,0:T(8,128)(2,1)}, bf16[12,128,128]{2,1,0:T(8,128)(2,1)}, u32[]{:S(2)}, u32[]{:S(2)}) %collective-permute-start.5) | collective-permute-done | bytes 393248 | tf_op jit(solution)/shard_map/ppermute | solution.py:850
  68.4 1.9 collective-permute-start.13
  70.3 2.5 pad_maximum_fusion.1.refs_0_
  72.8 16.6 %collective-permute-done.6 = bf16[12,128,128]{2,1,0:T(8,128)(2,1)S(1)} collective-permute-done((bf16[12,128,128]{2,1,0:T(8,128)(2,1)}, bf16[12,128,128]{2,1,0:T(8,128)(2,1)S(1)}, u32[]{:S(2)}, u32[]{:S(2)}) %collective-permute-start.6) | collective-permute-done | bytes 393248 | tf_op jit(solution)/shard_map/ppermute | solution.py:850
  90.2 8.7 %collective-permute-done.7 = bf16[12,128,128]{2,1,0:T(8,128)(2,1)S(1)} collective-permute-done((bf16[12,128,128]{2,1,0:T(8,128)(2,1)}, bf16[12,128,128]{2,1,0:T(8,128)(2,1)S(1)}, u32[]{:S(2)}, u32[]{:S(2)}) %collective-permute-start.7) | collective-permute-done | bytes 393248 | tf_op jit(solution)/shard_map/ppermute | solution.py:850
  98.9 1.9 collective-permute-start.11
  101.7 5.6 %collective-permute-done.13 = bf16[12,128,128]{2,1,0:T(8,128)(2,1)S(1)} collective-permute-done((bf16[12,128,128]{2,1,0:T(8,128)(2,1)S(1)}, bf16[12,128,128]{2,1,0:T(8,128)(2,1)S(1)}, u32[]{:S(2)}, u32[]{:S(2)}) %collective-permute-start.13) | collective-permute-done | bytes 393248 | tf_op jit(solution)/shard_map/ppermute | solution.py:850
  110.0 4.0 collective-permute-done.11
  116.0 1.7 collective-permute-done.14
  121.4 2.0 collective-permute-done.18.refs_7_
  123.4 1.8 broadcast_in_dim.158
  125.7 4.7 all-to-all-start.1
  130.5 24.6 %attention_front.1 = (bf16[384,1536]{1,0:T(8,128)(2,1)}, f32[384,1536]{1,0:T(8,128)}, bf16[384,1536]{1,0:T(8,128)(2,1)}, bf16[24,384,64]{2,1,0:T(8,128)(2,1)}, b...) custom-call(s32[1]{0:T(128)} %copy.33.length_ref, ...), custom_call_target="tpu_custom_call" | custom-call | flops 115000000512 | bytes 1024 | tf_op jit(solution)/shard_map/attention_front/pallas_call | solution.py:502
  155.1 2.0 collective-permute-start.19
  157.1 1.5 collective-permute-start.20
  160.3 2.5 pad_maximum_fusion.packed_ref
  162.8 24.2 %collective-permute-done.19.refs_1_ = bf16[384,1536]{1,0:T(8,128)(2,1)} collective-permute-done((bf16[384,1536]{1,0:T(8,128)(2,1)}, bf16[384,1536]{1,0:T(8,128)(2,1)}, u32[]{:S(2)}, u32[]{:S(2)}) %collective-permute-start.19) | collective-permute-done | bytes 1179680 | tf_op jit(solution)/shard_map/ppermute | solution.py:850
  187.0 25.4 %collective-permute-done.21.refs_3_ = bf16[384,1536]{1,0:T(8,128)(2,1)} collective-permute-done((bf16[384,1536]{1,0:T(8,128)(2,1)}, bf16[384,1536]{1,0:T(8,128)(2,1)}, u32[]{:S(2)}, u32[]{:S(2)}) %collective-permute-start.21) | collective-permute-done | bytes 1179680 | tf_op jit(solution)/shard_map/ppermute | solution.py:850
  212.3 58.9 %expert_front.1 = (bf16[4,384,512]{2,1,0:T(8,128)(2,1)}, bf16[4,384,512]{2,1,0:T(8,128)(2,1)}, bf16[4,384,512]{2,1,0:T(8,128)(2,1)}, bf16[4,384,512]{2,1,0:T(8,1...) custom-call(s32[1]{0:T(128)} %bitcast.33.group_ref, ...), custom_call_target="tpu_custom_call" | custom-call | flops 115000000512 | bytes 1024 | tf_op jit(solution)/shard_map/expert_front/pallas_call | solution.py:195
  271.3 4.9 all-to-all-start.2
  276.3 38.3 %expert_weight_grads.1 = bf16[576,128,128]{2,1,0:T(8,128)(2,1)} custom-call(s32[1]{0:T(128)} %bitcast.33.group_ref, s32[576]{0:T(1024)} %select_reduce_fusion.inverse_ref.position_ref, bf16[384,1536]{1,0:T(8,128)(2,1)} %get-tuple-element.86.refs_0_, bf16[384,1536]{1,0:T(8,128)(2,1)} %collective-permute-done.19.refs_1_, ...), custom_call_target="tpu_custom_call" | custom-call | flops 115000000512 | bytes 1024 | tf_op jit(solution)/shard_map/expert_weight_grads/pallas_call | solution.py:309
  314.7 14.9 %expert_outputs.1 = bf16[4,384,1536]{2,1,0:T(8,128)(2,1)} custom-call(s32[1]{0:T(128)} %bitcast.33.group_ref, bf16[4,384,512]{2,1,0:T(8,128)(2,1)} %get-tuple-element.88.refs_0_.refs_6_, bf16[4,384,512]{2,1,0:T(8,128)(2,1)} %get-tuple-element.89.refs_1_.refs_7_, bf16[4,384,512]{2,1,0:T(8,128)(2,1)} %get-tuple-element.90.refs_2_.refs_8_, ...), custom_call_target="tpu_custom_call" | custom-call | flops 344999985152 | bytes 1024 | tf_op jit(solution)/shard_map/expert_outputs/pallas_call | solution.py:364
  329.6 10.1 %expert_route.1.refs_0_ = bf16[384,1536]{1,0:T(8,128)(2,1)} custom-call(bf16[4,384,1024]{2,1,0:T(8,128)(2,1)} %get-tuple-element.97.both_ref.refs_10_, bf16[4,1536,1536]{2,1,0:T(8,128)(2,1)} %get-tuple-element.92.refs_4_.matrix_ref), custom_call_target="tpu_custom_call" | custom-call | flops 4600000000 | bytes 1024 | tf_op jit(solution)/shard_map/expert_route/pallas_call | solution.py:338
  339.6 5.2 all-to-all-start.3
  344.8 45.1 %attention_back.1 = (f32[384,1536]{1,0:T(8,128)}, f32[2,1536]{1,0:T(2,128)}, bf16[192,128,128]{2,1,0:T(8,128)(2,1)}, bf16[192,128,128]{2,1,0:T(8,128)(2,1)}) custom-call(s32[1]{0:T(128)} %bitcast.33.group_ref, s32[1]{0:T(128)} %copy.33.length_ref, s32[384]{0:T(512)} %fusion.39.position_ref, bf16[384,1536]{1,0:T(8,128)(2,1)} %tokens_ref.3, ...), custom_call_target="tpu_custom_call" | custom-call | flops 172499992576 | bytes 1024 | tf_op jit(solution)/shard_map/attention_back/pallas_call | solution.py:640
  390.0 7.5 %all-to-all-done.3 = bf16[4,384,1536]{2,1,0:T(8,128)(2,1)} async-done(((bf16[4,384,1536]{2,1,0:T(8,128)(2,1)}), bf16[4,384,1536]{2,1,0:T(8,128)(2,1)}, u32[]{:S(2)}, u32[]{:S(2)}) %all-to-all-start.3) | async-done | bytes 4718624 | tf_op jit(solution)/shard_map/all_to_all | solution.py:736
  397.5 4.5 fusion.85
  402.6 5.1 collective-permute-done.23
  407.8 1.3 add_convert_fusion.1
  409.1 1.5 collective-permute-start.24
  411.1 1.4 collective-permute-done.22
  412.5 33.2 %collective-permute-done.24 = bf16[48,128,128]{2,1,0:T(8,128)(2,1)S(1)} collective-permute-done((bf16[48,128,128]{2,1,0:T(8,128)(2,1)S(1)}, bf16[48,128,128]{2,1,0:T(8,128)(2,1)S(1)}, u32[]{:S(2)}, u32[]{:S(2)}) %collective-permute-start.24) | collective-permute-done | bytes 1572896 | tf_op jit(solution)/shard_map/ppermute | solution.py:850
  446.8 2.0 add_convert_fusion
  449.6 1.5 collective-permute-start.25
  451.1 16.3 %collective-permute-done.27 = bf16[24,128,128]{2,1,0:T(8,128)(2,1)S(1)} collective-permute-done((bf16[24,128,128]{2,1,0:T(8,128)(2,1)S(1)}, bf16[24,128,128]{2,1,0:T(8,128)(2,1)S(1)}, u32[]{:S(2)}, u32[]{:S(2)}) %collective-permute-start.27) | collective-permute-done | bytes 786464 | tf_op jit(solution)/shard_map/ppermute | solution.py:850
  468.2 19.2 %collective-permute-done.28 = bf16[12,128,128]{2,1,0:T(8,128)(2,1)S(1)} collective-permute-done((bf16[12,128,128]{2,1,0:T(8,128)(2,1)S(1)}, bf16[12,128,128]{2,1,0:T(8,128)(2,1)S(1)}, u32[]{:S(2)}, u32[]{:S(2)}) %collective-permute-start.28) | collective-permute-done | bytes 393248 | tf_op jit(solution)/shard_map/ppermute | solution.py:723
  489.5 3.1 collective-permute-done.30
  493.4 3.5 convert_reduce_fusion
  496.9 3.2 collective-permute-start.32
  500.1 2.4 collective-permute-start.33
  502.5 1.9 collective-permute-start.34
  504.4 1.3 add_convert_fusion.6
  506.3 5.6 %reduce-scatter.2.cloned.1.call-done.refs_0_ = bf16[72,128,128]{2,1,0:T(8,128)(2,1)} async-done(((bf16[576,128,128]{2,1,0:T(8,128)(2,1)}), bf16[72,128,128]{2,1,0:T(8,128)(2,1)}) %reduce-scatter.2.cloned.1.call-update) | async-done | bytes 2359312 | tf_op jit(solution)/shard_map/reduce_scatter | solution.py:914
  512.0 3.4 collective-permute-start.35
  515.6 2.3 copy-done
  517.9 1.7 copy-done.2
  519.6 14.8 %shampoo.2 = (f32[72,128,128]{2,1,0:T(8,128)}, f32[72,2,128,128]{3,2,1,0:T(8,128)}, f32[72,128,128]{2,1,0:T(8,128)}) custom-call(bf16[72,128,128]{2,1,0:T(8,128)(2,1)S(1)} %copy-done.2, f32[72,2,128,128]{3,2,1,0:T(8,128)} %refs_1_.1, f32[72,2,128,128]{3,2,1,0:T(8,128)} %refs_2_.1, f32[72,128,128]{2,1,0:T(8,128)S(1)} %copy-done), custom_call_target="tpu_custom_call" | custom-call | flops 11500000256 | bytes 1024 | tf_op jit(solution)/shard_map/shampoo/pallas_call | solution.py:706
  535.0 2.5 shampoo.3
  (137 shorter events, 23.9 us)
Async XLA Ops:
  7.2 205.2 %all-gather.2.cloned.1.call-start = ((), (), s32[]{:S(2)}) async-start(), calls=%async_computation.5 | async-start | bytes 21233664 | tf_op jit(solution)/shard_map/all_gather | solution.py:888
  8.4 25.1 %copy-start.8 = (bf16[12,128,128]{2,1,0:T(8,128)(2,1)}, bf16[12,128,128]{2,1,0:T(8,128)(2,1)S(1)}, u32[]{:S(2)}) copy-start(bf16[12,128,128]{2,1,0:T(8,128)(2,1)S(1)} %convert_element_type.93) | copy-start | bytes 1179652
  8.4 19.3 %collective-permute-start.1 = (bf16[12,128,128]{2,1,0:T(8,128)(2,1)S(1)}, bf16[12,128,128]{2,1,0:T(8,128)(2,1)}, u32[]{:S(2)}, u32[]{:S(2)}) collective-permute-start(bf16[12,128,128]{2,1,0:T(8,128)(2,1)S(1)} %convert_element_type.93), channel_id=1, source_target_pairs={{0,4},{1,5},{2,6},{3,7},{4,0},{5,1},{6,2},{7,3},{8,12},{9,13},{10,... | collective-permute-start | bytes 1179656 | tf_op jit(solution)/shard_map/ppermute | solution.py:723
  11.1 22.4 %collective-permute-start = (bf16[12,128,128]{2,1,0:T(8,128)(2,1)S(1)}, bf16[12,128,128]{2,1,0:T(8,128)(2,1)S(1)}, u32[]{:S(2)}, u32[]{:S(2)}) collective-permute-start(bf16[12,128,128]{2,1,0:T(8,128)(2,1)S(1)} %convert_element_type.93), channel_id=1, source_target_pairs={{0,2},{1,3},{2,0},{3,1},{4,6},{5,7},{6,4},{7,5},{8,10},{9,11},{10,... | collective-permute-start | bytes 1179656 | tf_op jit(solution)/shard_map/ppermute | solution.py:723
  11.5 22.0 %collective-permute-start.3 = (bf16[12,128,128]{2,1,0:T(8,128)(2,1)S(1)}, bf16[12,128,128]{2,1,0:T(8,128)(2,1)}, u32[]{:S(2)}, u32[]{:S(2)}) collective-permute-start(bf16[12,128,128]{2,1,0:T(8,128)(2,1)S(1)} %convert_element_type.93), channel_id=1, source_target_pairs={{0,8},{8,0},{16,24},{24,16},{1,9},{9,1},{17,25},{25,17},{2,10},{10... | collective-permute-start | bytes 1179656 | tf_op jit(solution)/shard_map/ppermute | solution.py:850
  13.0 20.5 %collective-permute-start.4 = (bf16[12,128,128]{2,1,0:T(8,128)(2,1)S(1)}, bf16[12,128,128]{2,1,0:T(8,128)(2,1)S(1)}, u32[]{:S(2)}, u32[]{:S(2)}) collective-permute-start(bf16[12,128,128]{2,1,0:T(8,128)(2,1)S(1)} %convert_element_type.93), channel_id=1, source_target_pairs={{0,16},{8,24},{16,0},{24,8},{1,17},{9,25},{17,1},{25,9},{2,18},{10... | collective-permute-start | bytes 1179656 | tf_op jit(solution)/shard_map/ppermute | solution.py:850
  27.8 11.2 %collective-permute-start.2 = (bf16[12,128,128]{2,1,0:T(8,128)(2,1)}, bf16[12,128,128]{2,1,0:T(8,128)(2,1)S(1)}, u32[]{:S(2)}, u32[]{:S(2)}) collective-permute-start(bf16[12,128,128]{2,1,0:T(8,128)(2,1)} %collective-permute-done.1), channel_id=1, source_target_pairs={{0,2},{1,3},{2,0},{3,1},{4,6},{5,7},{6,4},{7,5},{8,10},{9,11},{10,... | collective-permute-start | bytes 1179656 | tf_op jit(solution)/shard_map/ppermute | solution.py:723
  33.5 6.3 %copy-start.17 = (bf16[384,8]{0,1:T(8,128)(2,1)S(1)}, bf16[384,8]{0,1:T(8,128)(2,1)}, u32[]{:S(2)}) copy-start(bf16[384,8]{0,1:T(8,128)(2,1)} %param.18) | copy-start | bytes 18436
  33.5 6.3 %copy-start.18 = (s32[384,8]{0,1:T(8,128)S(1)}, s32[384,8]{0,1:T(8,128)}, u32[]{:S(2)}) copy-start(s32[384,8]{0,1:T(8,128)} %param.17) | copy-start | bytes 36868
  33.5 7.5 %copy-start.10 = (bf16[384,1536]{1,0:T(8,128)(2,1)S(1)}, bf16[384,1536]{1,0:T(8,128)(2,1)}, u32[]{:S(2)}) copy-start(bf16[384,1536]{1,0:T(8,128)(2,1)} %param.15) | copy-start | bytes 3538948
  33.5 12.5 %copy-start.15 = (bf16[12,128,128]{2,1,0:T(8,128)(2,1)}, bf16[12,128,128]{2,1,0:T(8,128)(2,1)S(1)}, u32[]{:S(2)}) copy-start(bf16[12,128,128]{2,1,0:T(8,128)(2,1)S(1)} %collective-permute-done) | copy-start | bytes 1179652
  33.6 7.6 %copy-start.11 = (bf16[12,128,128]{2,1,0:T(8,128)(2,1)}, bf16[12,128,128]{2,1,0:T(8,128)(2,1)S(1)}, u32[]{:S(2)}) copy-start(bf16[12,128,128]{2,1,0:T(8,128)(2,1)S(1)} %collective-permute-done.4) | copy-start | bytes 1179652
  41.2 3.1 copy-start.5
  41.2 15.5 %collective-permute-start.9 = (bf16[12,128,128]{2,1,0:T(8,128)(2,1)}, bf16[12,128,128]{2,1,0:T(8,128)(2,1)}, u32[]{:S(2)}, u32[]{:S(2)}) collective-permute-start(bf16[12,128,128]{2,1,0:T(8,128)(2,1)} %collective-permute-done.1), channel_id=1, source_target_pairs={{0,8},{8,0},{16,24},{24,16},{1,9},{9,1},{17,25},{25,17},{2,10},{10... | collective-permute-start | bytes 1179656 | tf_op jit(solution)/shard_map/ppermute | solution.py:850
  42.8 25.7 %collective-permute-start.5 = (bf16[12,128,128]{2,1,0:T(8,128)(2,1)}, bf16[12,128,128]{2,1,0:T(8,128)(2,1)}, u32[]{:S(2)}, u32[]{:S(2)}) collective-permute-start(bf16[12,128,128]{2,1,0:T(8,128)(2,1)} %collective-permute-done.3), channel_id=1, source_target_pairs={{0,16},{8,24},{16,0},{24,8},{1,17},{9,25},{17,1},{25,9},{2,18},{10... | collective-permute-start | bytes 1179656 | tf_op jit(solution)/shard_map/ppermute | solution.py:850
  46.0 77.4 %all-to-all-start = ((bf16[4,192,1664]{2,1,0:T(8,128)(2,1)}), bf16[4,192,1664]{2,1,0:T(8,128)(2,1)S(1)}, u32[]{:S(2)}, u32[]{:S(2)}) async-start(bf16[4,192,1664]{2,1,0:T(8,128)(2,1)} %broadcast_in_dim.157), calls=%async_computation | async-start | bytes 5111808 | tf_op jit(solution)/shard_map/all_to_all | solution.py:741
  49.8 6.2 %copy-start.14 = (bf16[12,128,128]{2,1,0:T(8,128)(2,1)S(1)}, bf16[12,128,128]{2,1,0:T(8,128)(2,1)}, u32[]{:S(2)}) copy-start(bf16[12,128,128]{2,1,0:T(8,128)(2,1)} %copy-done.13) | copy-start | bytes 1179652
  49.8 20.6 %copy-start.9 = (bf16[12,128,128]{2,1,0:T(8,128)(2,1)S(1)}, bf16[12,128,128]{2,1,0:T(8,128)(2,1)}, u32[]{:S(2)}) copy-start(bf16[12,128,128]{2,1,0:T(8,128)(2,1)} %copy-done.8) | copy-start | bytes 1179652
  49.8 20.5 %copy-start.12 = (bf16[12,128,128]{2,1,0:T(8,128)(2,1)S(1)}, bf16[12,128,128]{2,1,0:T(8,128)(2,1)}, u32[]{:S(2)}) copy-start(bf16[12,128,128]{2,1,0:T(8,128)(2,1)} %copy-done.11) | copy-start | bytes 1179652
  49.8 59.4 %collective-permute-start.10 = (bf16[12,128,128]{2,1,0:T(8,128)(2,1)}, bf16[12,128,128]{2,1,0:T(8,128)(2,1)S(1)}, u32[]{:S(2)}, u32[]{:S(2)}) collective-permute-start(bf16[12,128,128]{2,1,0:T(8,128)(2,1)} %collective-permute-done.1), channel_id=1, source_target_pairs={{0,16},{8,24},{16,0},{24,8},{1,17},{9,25},{17,1},{25,9},{2,18},{10... | collective-permute-start | bytes 1179656 | tf_op jit(solution)/shard_map/ppermute | solution.py:850
  51.8 37.6 %collective-permute-start.6 = (bf16[12,128,128]{2,1,0:T(8,128)(2,1)}, bf16[12,128,128]{2,1,0:T(8,128)(2,1)S(1)}, u32[]{:S(2)}, u32[]{:S(2)}) collective-permute-start(bf16[12,128,128]{2,1,0:T(8,128)(2,1)} %copy-done.15), channel_id=1, source_target_pairs={{0,8},{8,0},{16,24},{24,16},{1,9},{9,1},{17,25},{25,17},{2,10},{10... | collective-permute-start | bytes 1179656 | tf_op jit(solution)/shard_map/ppermute | solution.py:850
  53.2 45.6 %collective-permute-start.7 = (bf16[12,128,128]{2,1,0:T(8,128)(2,1)}, bf16[12,128,128]{2,1,0:T(8,128)(2,1)S(1)}, u32[]{:S(2)}, u32[]{:S(2)}) collective-permute-start(bf16[12,128,128]{2,1,0:T(8,128)(2,1)} %copy-done.15), channel_id=1, source_target_pairs={{0,16},{8,24},{16,0},{24,8},{1,17},{9,25},{17,1},{25,9},{2,18},{10... | collective-permute-start | bytes 1179656 | tf_op jit(solution)/shard_map/ppermute | solution.py:850
  56.7 44.8 %collective-permute-start.12 = (bf16[12,128,128]{2,1,0:T(8,128)(2,1)S(1)}, bf16[12,128,128]{2,1,0:T(8,128)(2,1)S(1)}, u32[]{:S(2)}, u32[]{:S(2)}) collective-permute-start(bf16[12,128,128]{2,1,0:T(8,128)(2,1)S(1)} %copy-done.14), channel_id=1, source_target_pairs={{0,8},{8,0},{16,24},{24,16},{1,9},{9,1},{17,25},{25,17},{2,10},{10... | collective-permute-start | bytes 1179656 | tf_op jit(solution)/shard_map/ppermute | solution.py:850
  68.4 38.9 %collective-permute-start.13 = (bf16[12,128,128]{2,1,0:T(8,128)(2,1)S(1)}, bf16[12,128,128]{2,1,0:T(8,128)(2,1)S(1)}, u32[]{:S(2)}, u32[]{:S(2)}) collective-permute-start(bf16[12,128,128]{2,1,0:T(8,128)(2,1)S(1)} %copy-done.14), channel_id=1, source_target_pairs={{0,16},{8,24},{16,0},{24,8},{1,17},{9,25},{17,1},{25,9},{2,18},{10... | collective-permute-start | bytes 1179656 | tf_op jit(solution)/shard_map/ppermute | solution.py:850
  89.4 32.0 %collective-permute-start.15 = (bf16[48,128,128]{2,1,0:T(8,128)(2,1)}, bf16[48,128,128]{2,1,0:T(8,128)(2,1)}, u32[]{:S(2)}, u32[]{:S(2)}) collective-permute-start(bf16[48,128,128]{2,1,0:T(8,128)(2,1)} %pad_maximum_fusion.1.refs_0_), channel_id=1, source_target_pairs={{0,1},{1,0},{2,3},{3,2},{4,5},{5,4},{6,7},{7,6},{8,9},{9,8},{10,11... | collective-permute-start | bytes 4718600 | tf_op jit(solution)/shard_map/ppermute | solution.py:723
  98.9 15.1 %collective-permute-start.11 = (bf16[12,128,128]{2,1,0:T(8,128)(2,1)}, bf16[12,128,128]{2,1,0:T(8,128)(2,1)S(1)}, u32[]{:S(2)}, u32[]{:S(2)}) collective-permute-start(bf16[12,128,128]{2,1,0:T(8,128)(2,1)} %collective-permute-done.9), channel_id=1, source_target_pairs={{0,16},{8,24},{16,0},{24,8},{1,17},{9,25},{17,1},{25,9},{2,18},{10... | collective-permute-start | bytes 1179656 | tf_op jit(solution)/shard_map/ppermute | solution.py:850
  101.6 13.2 %collective-permute-start.8 = (bf16[12,128,128]{2,1,0:T(8,128)(2,1)S(1)}, bf16[12,128,128]{2,1,0:T(8,128)(2,1)S(1)}, u32[]{:S(2)}, u32[]{:S(2)}) collective-permute-start(bf16[12,128,128]{2,1,0:T(8,128)(2,1)S(1)} %collective-permute-done.7), channel_id=1, source_target_pairs={{0,8},{8,0},{16,24},{24,16},{1,9},{9,1},{17,25},{25,17},{2,10},{10... | collective-permute-start | bytes 1179656 | tf_op jit(solution)/shard_map/ppermute | solution.py:850
  107.3 10.5 %collective-permute-start.14 = (bf16[12,128,128]{2,1,0:T(8,128)(2,1)S(1)}, bf16[12,128,128]{2,1,0:T(8,128)(2,1)S(1)}, u32[]{:S(2)}, u32[]{:S(2)}) collective-permute-start(bf16[12,128,128]{2,1,0:T(8,128)(2,1)S(1)} %collective-permute-done.13), channel_id=1, source_target_pairs={{0,8},{8,0},{16,24},{24,16},{1,9},{9,1},{17,25},{25,17},{2,10},{10... | collective-permute-start | bytes 1179656 | tf_op jit(solution)/shard_map/ppermute | solution.py:850
  109.2 9.3 %copy-start.21 = (s32[384]{0:T(512)S(1)}, s32[384]{0:T(512)}, u32[]{:S(2)}) copy-start(s32[384]{0:T(512)} %param.23) | copy-start | bytes 4612
  114.8 6.7 %collective-permute-start.17 = (bf16[48,128,128]{2,1,0:T(8,128)(2,1)}, bf16[48,128,128]{2,1,0:T(8,128)(2,1)}, u32[]{:S(2)}, u32[]{:S(2)}) collective-permute-start(bf16[48,128,128]{2,1,0:T(8,128)(2,1)} %constant_dynamic-update-slice_fusion.4.refs_2_), channel_id=1, source_target_pairs={{0,1},{1,0},{2,3},{3,2},{4,5},{5,4},{6,7},{7,6},{8,9},{9,8},{10,11... | collective-permute-start | bytes 4718600 | tf_op jit(solution)/shard_map/ppermute | solution.py:723
  115.5 5.9 %collective-permute-start.16 = (bf16[48,128,128]{2,1,0:T(8,128)(2,1)}, bf16[48,128,128]{2,1,0:T(8,128)(2,1)}, u32[]{:S(2)}, u32[]{:S(2)}) collective-permute-start(bf16[48,128,128]{2,1,0:T(8,128)(2,1)} %constant_dynamic-update-slice_fusion.refs_1_), channel_id=1, source_target_pairs={{0,1},{1,0},{2,3},{3,2},{4,5},{5,4},{6,7},{7,6},{8,9},{9,8},{10,11... | collective-permute-start | bytes 4718600 | tf_op jit(solution)/shard_map/ppermute | solution.py:723
  118.5 4.9 collective-permute-start.18
  125.7 86.6 %all-to-all-start.1 = ((bf16[4,192,1664]{2,1,0:T(8,128)(2,1)}), bf16[4,192,1664]{2,1,0:T(8,128)(2,1)}, u32[]{:S(2)}, u32[]{:S(2)}) async-start(bf16[4,192,1664]{2,1,0:T(8,128)(2,1)} %broadcast_in_dim.158), calls=%async_computation.1 | async-start | bytes 5111808 | tf_op jit(solution)/shard_map/all_to_all | solution.py:741
  130.5 28.2 %copy-start.22 = (s32[1,576]{1,0:T(1,128)S(1)}, s32[1,576]{1,0:T(1,128)}, u32[]{:S(2)}) copy-start(s32[1,576]{1,0:T(1,128)} %param.27) | copy-start | bytes 6916
  155.1 31.9 %collective-permute-start.19 = (bf16[384,1536]{1,0:T(8,128)(2,1)}, bf16[384,1536]{1,0:T(8,128)(2,1)}, u32[]{:S(2)}, u32[]{:S(2)}) collective-permute-start(bf16[384,1536]{1,0:T(8,128)(2,1)} %get-tuple-element.86.refs_0_), channel_id=1, source_target_pairs={{0,8},{8,0},{16,24},{24,16},{1,9},{9,1},{17,25},{25,17},{2,10},{10... | collective-permute-start | bytes 3538952 | tf_op jit(solution)/shard_map/ppermute | solution.py:850
  157.1 29.9 %collective-permute-start.20 = (bf16[384,1536]{1,0:T(8,128)(2,1)}, bf16[384,1536]{1,0:T(8,128)(2,1)}, u32[]{:S(2)}, u32[]{:S(2)}) collective-permute-start(bf16[384,1536]{1,0:T(8,128)(2,1)} %get-tuple-element.86.refs_0_), channel_id=1, source_target_pairs={{0,16},{8,24},{16,0},{24,8},{1,17},{9,25},{17,1},{25,9},{2,18},{10... | collective-permute-start | bytes 3538952 | tf_op jit(solution)/shard_map/ppermute | solution.py:850
  158.6 53.8 %collective-permute-start.21 = (bf16[384,1536]{1,0:T(8,128)(2,1)}, bf16[384,1536]{1,0:T(8,128)(2,1)}, u32[]{:S(2)}, u32[]{:S(2)}) collective-permute-start(bf16[384,1536]{1,0:T(8,128)(2,1)} %get-tuple-element.86.refs_0_), channel_id=1, source_target_pairs={{0,24},{8,16},{16,8},{24,0},{1,25},{9,17},{17,9},{25,1},{2,26},{10... | collective-permute-start | bytes 3538952 | tf_op jit(solution)/shard_map/ppermute | solution.py:850
  271.3 68.3 %all-to-all-start.2 = ((bf16[4,384,1536]{2,1,0:T(8,128)(2,1)}), bf16[4,384,1536]{2,1,0:T(8,128)(2,1)}, u32[]{:S(2)}, u32[]{:S(2)}) async-start(bf16[4,384,1536]{2,1,0:T(8,128)(2,1)} %get-tuple-element.98), calls=%async_computation.2 | async-start | bytes 9437184 | tf_op jit(solution)/shard_map/all_to_all | solution.py:736
  276.3 235.7 %reduce-scatter.2.cloned.1.call-start = ((), (), s32[]{:S(2)}) async-start(), calls=%async_computation.6 | async-start | bytes 21233664 | tf_op jit(solution)/shard_map/reduce_scatter | solution.py:914
  339.6 57.9 %all-to-all-start.3 = ((bf16[4,384,1536]{2,1,0:T(8,128)(2,1)}), bf16[4,384,1536]{2,1,0:T(8,128)(2,1)}, u32[]{:S(2)}, u32[]{:S(2)}) async-start(bf16[4,384,1536]{2,1,0:T(8,128)(2,1)} %expert_outputs.1), calls=%async_computation.3 | async-start | bytes 9437184 | tf_op jit(solution)/shard_map/all_to_all | solution.py:736
  397.5 10.2 %slice-start = ((s8[6291456]{0:T(1024)(128)(4,1)}), s8[4194304]{0:T(1024)(128)(4,1)S(1)}, s32[]{:S(2)}) async-start(s8[6291456]{0:T(1024)(128)(4,1)} %bitcast.73), calls=%async_computation.7 | async-start | bytes 8388608
  397.5 10.2 %slice-start.1 = ((s8[6291456]{0:T(1024)(128)(4,1)}), s8[2097152]{0:T(1024)(128)(4,1)S(1)}, s32[]{:S(2)}) async-start(s8[6291456]{0:T(1024)(128)(4,1)} %bitcast.73), calls=%async_computation.8 | async-start | bytes 4194304
  402.0 5.7 %collective-permute-start.23 = (bf16[96,128,128]{2,1,0:T(8,128)(2,1)S(1)}, bf16[96,128,128]{2,1,0:T(8,128)(2,1)S(1)}, u32[]{:S(2)}, u32[]{:S(2)}) collective-permute-start(bf16[96,128,128]{2,1,0:T(8,128)(2,1)S(1)} %get-tuple-element.151), channel_id=1, source_target_pairs={{0,1},{1,0},{2,3},{3,2},{4,5},{5,4},{6,7},{7,6},{8,9},{9,8},{10,11... | collective-permute-start | bytes 9437192 | tf_op jit(solution)/shard_map/ppermute | solution.py:723
  402.1 10.4 %collective-permute-start.22 = (bf16[96,128,128]{2,1,0:T(8,128)(2,1)S(1)}, bf16[96,128,128]{2,1,0:T(8,128)(2,1)S(1)}, u32[]{:S(2)}, u32[]{:S(2)}) collective-permute-start(bf16[96,128,128]{2,1,0:T(8,128)(2,1)S(1)} %get-tuple-element.150), channel_id=1, source_target_pairs={{0,1},{1,0},{2,3},{3,2},{4,5},{5,4},{6,7},{7,6},{8,9},{9,8},{10,11... | collective-permute-start | bytes 9437192 | tf_op jit(solution)/shard_map/ppermute | solution.py:723
  409.1 36.5 %collective-permute-start.24 = (bf16[48,128,128]{2,1,0:T(8,128)(2,1)S(1)}, bf16[48,128,128]{2,1,0:T(8,128)(2,1)S(1)}, u32[]{:S(2)}, u32[]{:S(2)}) collective-permute-start(bf16[48,128,128]{2,1,0:T(8,128)(2,1)S(1)} %get-tuple-element.149), channel_id=1, source_target_pairs={{0,8},{8,0},{16,24},{24,16},{1,9},{9,1},{17,25},{25,17},{2,10},{10... | collective-permute-start | bytes 4718600 | tf_op jit(solution)/shard_map/ppermute | solution.py:850
  410.6 36.2 %collective-permute-start.26 = (bf16[48,128,128]{2,1,0:T(8,128)(2,1)S(1)}, bf16[48,128,128]{2,1,0:T(8,128)(2,1)S(1)}, u32[]{:S(2)}, u32[]{:S(2)}) collective-permute-start(bf16[48,128,128]{2,1,0:T(8,128)(2,1)S(1)} %get-tuple-element.148), channel_id=1, source_target_pairs={{0,16},{8,24},{16,0},{24,8},{1,17},{9,25},{17,1},{25,9},{2,18},{10... | collective-permute-start | bytes 4718600 | tf_op jit(solution)/shard_map/ppermute | solution.py:850
  448.8 18.6 %collective-permute-start.27 = (bf16[24,128,128]{2,1,0:T(8,128)(2,1)S(1)}, bf16[24,128,128]{2,1,0:T(8,128)(2,1)S(1)}, u32[]{:S(2)}, u32[]{:S(2)}) collective-permute-start(bf16[24,128,128]{2,1,0:T(8,128)(2,1)S(1)} %slice.157), channel_id=1, source_target_pairs={{0,8},{8,0},{16,24},{24,16},{1,9},{9,1},{17,25},{25,17},{2,10},{10... | collective-permute-start | bytes 2359304 | tf_op jit(solution)/shard_map/ppermute | solution.py:850
  449.6 18.4 %collective-permute-start.25 = (bf16[24,128,128]{2,1,0:T(8,128)(2,1)S(1)}, bf16[24,128,128]{2,1,0:T(8,128)(2,1)S(1)}, u32[]{:S(2)}, u32[]{:S(2)}) collective-permute-start(bf16[24,128,128]{2,1,0:T(8,128)(2,1)S(1)} %slice.151), channel_id=1, source_target_pairs={{0,16},{8,24},{16,0},{24,8},{1,17},{9,25},{17,1},{25,9},{2,18},{10... | collective-permute-start | bytes 2359304 | tf_op jit(solution)/shard_map/ppermute | solution.py:850
  467.7 19.8 %collective-permute-start.28 = (bf16[12,128,128]{2,1,0:T(8,128)(2,1)S(1)}, bf16[12,128,128]{2,1,0:T(8,128)(2,1)S(1)}, u32[]{:S(2)}, u32[]{:S(2)}) collective-permute-start(bf16[12,128,128]{2,1,0:T(8,128)(2,1)S(1)} %slice.159), channel_id=1, source_target_pairs={{0,2},{1,3},{2,0},{3,1},{4,6},{5,7},{6,4},{7,5},{8,10},{9,11},{10,... | collective-permute-start | bytes 1179656 | tf_op jit(solution)/shard_map/ppermute | solution.py:723
  468.2 19.4 %copy-start.20 = (f32[2,1536]{1,0:T(2,128)S(1)}, f32[2,1536]{1,0:T(2,128)}, u32[]{:S(2)}) copy-start(f32[2,1536]{1,0:T(2,128)} %get-tuple-element.114) | copy-start | bytes 36868
  487.6 1.2 collective-permute-start.29
  488.9 3.8 collective-permute-start.30
  492.6 4.3 collective-permute-start.31
  493.4 11.0 %copy-start.7 = (f32[384,1536]{1,0:T(8,128)S(1)}, f32[384,1536]{1,0:T(8,128)}, u32[]{:S(2)}) copy-start(f32[384,1536]{1,0:T(8,128)} %get-tuple-element.83.middle_ref) | copy-start | bytes 7077892
  496.9 8.8 %collective-permute-start.32 = (f32[2,1536]{1,0:T(2,128)S(1)}, f32[2,1536]{1,0:T(2,128)S(1)}, u32[]{:S(2)}, u32[]{:S(2)}) collective-permute-start(f32[2,1536]{1,0:T(2,128)S(1)} %add.323), channel_id=1, source_target_pairs={{0,2},{1,3},{2,4},{3,5},{4,6},{5,7},{6,0},{7,1},{8,10},{9,11},{10,... | collective-permute-start | bytes 36872 | tf_op jit(solution)/shard_map/ppermute | solution.py:723
  500.1 5.7 %collective-permute-start.33 = (f32[2,1536]{1,0:T(2,128)S(1)}, f32[2,1536]{1,0:T(2,128)S(1)}, u32[]{:S(2)}, u32[]{:S(2)}) collective-permute-start(f32[2,1536]{1,0:T(2,128)S(1)} %add.323), channel_id=1, source_target_pairs={{0,4},{1,5},{2,6},{3,7},{4,0},{5,1},{6,2},{7,3},{8,12},{9,13},{10,... | collective-permute-start | bytes 36872 | tf_op jit(solution)/shard_map/ppermute | solution.py:723
  502.5 3.8 collective-permute-start.34
  506.3 28.0 %copy-start.16 = (f32[2,1536]{1,0:T(2,128)}, f32[2,1536]{1,0:T(2,128)S(1)}, u32[]{:S(2)}) copy-start(f32[2,1536]{1,0:T(2,128)S(1)} %add_bitcast_fusion) | copy-start | bytes 36868
  512.0 23.0 %collective-permute-start.35 = (bf16[12,128,128]{2,1,0:T(8,128)(2,1)S(1)}, bf16[12,128,128]{2,1,0:T(8,128)(2,1)S(1)}, u32[]{:S(2)}, u32[]{:S(2)}) collective-permute-start(bf16[12,128,128]{2,1,0:T(8,128)(2,1)S(1)} %get-tuple-element.117), channel_id=1, source_target_pairs={{0,2},{1,3},{2,0},{3,1},{4,6},{5,7},{6,4},{7,5},{8,10},{9,11},{10,... | collective-permute-start | bytes 1179656 | tf_op jit(solution)/shard_map/ppermute | solution.py:723
  515.4 19.6 %collective-permute-start.36 = (bf16[12,128,128]{2,1,0:T(8,128)(2,1)S(1)}, bf16[12,128,128]{2,1,0:T(8,128)(2,1)S(1)}, u32[]{:S(2)}, u32[]{:S(2)}) collective-permute-start(bf16[12,128,128]{2,1,0:T(8,128)(2,1)S(1)} %add_convert_fusion.9), channel_id=1, source_target_pairs={{0,4},{1,5},{2,6},{3,7},{4,0},{5,1},{6,2},{7,3},{8,12},{9,13},{10,... | collective-permute-start | bytes 1179656 | tf_op jit(solution)/shard_map/ppermute | solution.py:723
  519.6 14.8 %copy-start.19 = (f32[2,1536]{1,0:T(2,128)S(1)}, f32[2,1536]{1,0:T(2,128)}, u32[]{:S(2)}) copy-start(f32[2,1536]{1,0:T(2,128)} %gains_ref.3) | copy-start | bytes 36868
  519.6 15.5 %copy-start.1 = (f32[12,128,128]{2,1,0:T(8,128)S(1)}, f32[12,128,128]{2,1,0:T(8,128)}, u32[]{:S(2)}) copy-start(f32[12,128,128]{2,1,0:T(8,128)} %refs_5_.1) | copy-start | bytes 2359300
  519.6 15.5 %copy-start.3 = (f32[12,2,128,128]{3,2,1,0:T(8,128)S(1)}, f32[12,2,128,128]{3,2,1,0:T(8,128)}, u32[]{:S(2)}) copy-start(f32[12,2,128,128]{3,2,1,0:T(8,128)} %refs_3_.3) | copy-start | bytes 4718596
  519.6 15.5 %copy-start.4 = (f32[12,2,128,128]{3,2,1,0:T(8,128)S(1)}, f32[12,2,128,128]{3,2,1,0:T(8,128)}, u32[]{:S(2)}) copy-start(f32[12,2,128,128]{3,2,1,0:T(8,128)} %refs_4_.1) | copy-start | bytes 4718596
  (4 other events, 8.5 us)
Sparse Core Ops, SparseCore 0:
  39.2 167.3 all-gather.1
  314.8 197.1 reduce-scatter.1
